TPU v7x, 32 devices: a whole 2x2x4 slice. The times are simulated.
32 devices in a mesh: ctx: 4 (over z), head: 4 (over y, x), section: 2 (over core).
Axes of the slice: x: 2, y: 2, z: 4, core: 2. Of those that a mesh axis runs over, the one named last changes fastest.
Arguments:
- queries: bfloat16 [2, 512, 16384], P('section', 'ctx', 'head')
- keys: bfloat16 [2, 512, 1024], P('section', 'ctx', 'head')
- values: bfloat16 [2, 512, 1024], P('section', 'ctx', 'head'), may hold values from -6 to 6
- order: int32 [512], replicated, may hold values from 0 to 511, as said below
- doc_lengths: int32 [16], replicated, may hold values from 1 to 256, 512 in all
Outputs:
- handed: bfloat16 [2, 512, 16384], P('section', ('ctx', 'head'))
Inputs may be any that keep to these rules, and one draw needn't show every extreme that they name: The stored tokens of ctx index c are two aligned runs of 64 pack positions, run j and run 2 * 4 - 1 - j, each in rising order, j a permutation of the indices drawn from the seed.
All inputs are finite; a program needn't handle non-finite values.
Results may differ from a plain program's by a relative error of at most 0.0075.
Values may be sent and summed in bfloat16 or wider, within the bound.
No kernel may reach another device: no remote copies, remote signals or barrier semaphores. Data moves between devices by JAX's collectives and lax.ppermute only.
A program may use at most 64 MiB of HBM per device.

v0:
```python
import math

import jax
import jax.numpy as jnp
from jax import lax
from jax.sharding import PartitionSpec as P

HD = 128


def passed_along(value, axis, steps):
    count = lax.axis_size(axis)
    pairs = [(source, (source + steps) % count) for source in range(count)]
    return lax.ppermute(value, axis, pairs)


def doc_of(positions, starts):
    return jnp.sum((positions[:, None] >= starts[None, :]).astype(jnp.int32), axis=1) - 1


def local(queries, keys, values, order, doc_lengths):
    rows_q = queries.shape[1]
    kv_dev = keys.shape[2] // HD
    hq_dev = queries.shape[2] // HD
    group = hq_dev // kv_dev
    scale = 1.0 / HD**0.5
    starts = jnp.cumsum(doc_lengths) - doc_lengths
    shard = lax.axis_index("ctx")
    my_pos = lax.dynamic_slice_in_dim(order, shard * rows_q, rows_q, 0)
    my_doc = doc_of(my_pos, starts)
    q_local = queries[0].reshape(rows_q, kv_dev, group, HD)
    init = (
        jnp.full((rows_q, kv_dev, group), -1e30, jnp.float32),
        jnp.zeros((rows_q, kv_dev, group), jnp.float32),
        jnp.zeros((rows_q, kv_dev, group, HD), jnp.float32),
    )
    k_piece = lax.all_gather(keys, "ctx", axis=1, tiled=True)[0]
    v_piece = lax.all_gather(values, "ctx", axis=1, tiled=True)[0]
    rows = k_piece.shape[0]
    width = math.gcd(rows, 512)

    def one_block(index, state):
        offset = (index * width).astype(jnp.int32)
        k_block = lax.dynamic_slice_in_dim(k_piece, offset, width, 0).reshape(width, kv_dev, HD)
        v_block = lax.dynamic_slice_in_dim(v_piece, offset, width, 0).reshape(width, kv_dev, HD)
        key_pos = lax.dynamic_slice_in_dim(order, offset, width, 0)
        key_doc = doc_of(key_pos, starts)
        mask = (my_doc[:, None] == key_doc[None, :]) & (key_pos[None, :] <= my_pos[:, None])
        top_old, sum_old, acc_old = state
        score = (
            jnp.einsum("tkgd,skd->tkgs", q_local, k_block, preferred_element_type=jnp.float32)
            * scale
        )
        live = mask[:, None, None, :]
        score = jnp.where(live, score, -1e30)
        top_new = jnp.maximum(top_old, jnp.max(score, axis=3))
        weight = jnp.where(live, jnp.exp(score - top_new[..., None]), 0.0)
        factor = jnp.exp(top_old - top_new)
        sum_new = sum_old * factor + jnp.sum(weight, axis=3)
        weight_b = weight.astype(jnp.bfloat16)
        acc_new = acc_old * factor[..., None] + jnp.einsum(
            "tkgs,skd->tkgd", weight_b, v_block, preferred_element_type=jnp.float32
        )
        return (top_new, sum_new, acc_new)

    top_all, sum_all, acc_all = lax.fori_loop(0, rows // width, one_block, init)
    attn = (acc_all / sum_all[..., None]).astype(jnp.bfloat16).reshape(1, rows_q, hq_dev * HD)
    regrouped = lax.all_to_all(attn, "head", split_axis=1, concat_axis=2, tiled=True)
    return passed_along(regrouped, "section", 1)


def solution(mesh):
    in_specs = (
        P("section", "ctx", "head"),
        P("section", "ctx", "head"),
        P("section", "ctx", "head"),
        P(),
        P(),
    )
    out_specs = P("section", ("ctx", "head"), None)
    return jax.shard_map(local, mesh=mesh, in_specs=in_specs, out_specs=out_specs, check_vma=False)
```

profile of v0, /device:TPU:0, one launch (start us, length us, event | category | flops | bytes accessed | tf_op | source)
XLA Modules:
  0.0 79.2 jit_solution(1599756334528950546)
XLA Ops:
  0.0 0.7 copy.34
  0.8 0.1 reduce
  0.9 0.7 sub.34
  1.5 0.8 dynamic_slice.9
  2.3 0.8 convert_reduce_fusion
  3.1 0.1 convert_reduce_fusion.1
  3.2 1.4 %copy.49 = bf16[16,8,32,128]{3,2,1,0:T(8,128)(2,1)S(1)} copy(bf16[16,8,32,128]{3,1,2,0:T(8,128)(2,1)} %bitcast.50) | data formatting | bytes 2097152
  4.6 1.0 %copy.35 = bf16[1,128,256]{1,2,0:T(8,128)(2,1)S(1)} copy(bf16[1,128,256]{2,1,0:T(8,128)(2,1)} %param.6) | data formatting | bytes 131072 | tf_op args[1]
  5.6 14.5 %all_gather.6 = bf16[1,512,256]{1,2,0:T(8,128)(2,1)S(1)} all-gather(bf16[1,128,256]{1,2,0:T(8,128)(2,1)S(1)} %copy.35), channel_id=1, replica_groups=mesh['ctx'=4,'head'=4,'section'=2] {'ctx'}, dimensions={1}, use_global_device_ids=true | all-gather | bytes 327680 | tf_op jit(solution)/shard_map/all_gather | solution.py:37
  20.0 0.9 %compare_and_fusion = pred[128,512]{0,1:T(8,128)(4,1)S(1)} fusion(s32[128]{0:T(128)S(1)} %dynamic_slice.9, s32[128]{0:T(128)S(1)} %broadcast_add_fusion.1, s32[512]{0:T(512)} %param.8, s32[512]{0:T(512)S(1)} %broadcast_add_fusion), kind=kLoop, calls=%fused_computation.12 | loop fusion | flops 196608 | bytes 70656 | tf_op jit(solution)/shard_map/while/body/eval_jaxpr/and | solution.py:48
  20.9 0.0 copy-start.1
  20.9 1.9 %fusion = (f32[128,2,16]{0,2,1:T(8,128)S(1)}, f32[2,512,128,16]{2,1,3,0:T(8,128)S(1)}) fusion(pred[128,512]{0,1:T(8,128)(4,1)S(1)} %compare_and_fusion, bf16[512,2,128,1]{0,2,3,1:T(8,128)(2,1)S(1)} %bitcast.49, bf16[128,2,16,128]{3,2,1,0:T(8,128)(2,1)S(1)} %bitcast.46), kind=kOutput, calls=%fused_computation.2 | convolution fusion | flops 543158272 | bytes 9781248 | tf_op jit(solution)/shard_map/while/body/eval_jaxpr/tkgd,skd->tkgs/dot_general | solution.py:51
  22.9 0.0 copy-start
  22.9 3.2 %copy-done = f32[2,512,128,16]{2,1,3,0:T(8,128)} copy-done((f32[2,512,128,16]{2,1,3,0:T(8,128)}, f32[2,512,128,16]{2,1,3,0:T(8,128)S(1)}, u32[]{:S(2)}) %copy-start) | copy-done | bytes 8388632
  26.1 2.1 %fusion.1 = f32[128,2,16]{0,2,1:T(8,128)S(1)} fusion(f32[2,512,128,16]{2,1,3,0:T(8,128)S(1)} %get-tuple-element.30, f32[128,2,16]{0,2,1:T(8,128)S(1)} %broadcast_maximum_fusion, pred[128,512]{0,1:T(8,128)(4,1)S(1)} %compare_and_fusion), kind=kLoop, calls=%fused_computation.3 | loop fusion | flops 10481664 | bytes 8486912 | tf_op jit(solution)/shard_map/while/body/eval_jaxpr/reduce_sum | solution.py:59
  28.2 0.0 copy-done.1
  28.3 14.5 %all_gather.7 = bf16[1,512,256]{2,1,0:T(8,128)(2,1)S(1)} all-gather(bf16[1,128,256]{2,1,0:T(8,128)(2,1)S(1)} %copy-done.1), channel_id=1, replica_groups=mesh['ctx'=4,'head'=4,'section'=2] {'ctx'}, dimensions={1}, use_global_device_ids=true | all-gather | bytes 327680 | tf_op jit(solution)/shard_map/all_gather | solution.py:38
  42.8 0.1 copy.38
  42.9 5.6 %fusion.7 = bf16[128,2,16,128]{0,3,2,1:T(8,128)(2,1)S(1)} fusion(bf16[512,2,128,1]{0,2,3,1:T(8,128)(2,1)S(1)} %bitcast.52, f32[2,512,128,16]{2,1,3,0:T(8,128)} %copy-done, f32[128,2,16]{0,2,1:T(8,128)S(1)} %broadcast_maximum_fusion, pred[128,512]{0,1:T(8,128)(4,1)S(1)} %compare_and_fusion, f32[128,2,16]{0,2,1:T(8,128)S(1)} %get-tuple-element.28, ...), kind=kOutput, calls=%fused_computation.9 | convolution fusion | flops 548929536 | bytes 9814016 | tf_op jit(solution)/shard_map/while/body/eval_jaxpr/tkgs,skd->tkgd/dot_general | solution.py:61
  48.6 2.9 %copy.40 = bf16[1,128,4096]{2,0,1:T(2,128)(2,1)S(1)} copy(bf16[1,128,4096]{1,2,0:T(8,128)(2,1)S(1)} %bitcast.48) | data formatting | bytes 2097152 | tf_op jit(solution)/shard_map/reshape | solution.py:67
  51.5 0.5 broadcast.90
  52.0 7.0 %reduce.1 = bf16[128,4096]{1,0:T(8,128)(2,1)S(1)} reduce(bf16[128,1,4096]{2,1,0:T(2,128)(2,1)S(1)} %bitcast.45, bf16[]{:T(256)} %broadcast.90), dimensions={1}, to_apply=%bitcast.40.reduce_sub_computation | reduce | bytes 2097154
  59.0 0.8 %reshape.114 = bf16[4,2,65536]{2,1,0:T(2,128)(2,1)S(1)} reshape(bf16[128,4096]{1,0:T(8,128)(2,1)S(1)} %reduce.1) | data formatting | bytes 2097152
  59.8 13.5 %all_to_all.18 = bf16[4,2,65536]{2,1,0:T(2,128)(2,1)S(1)} all-to-all(bf16[4,2,65536]{2,1,0:T(2,128)(2,1)S(1)} %reshape.114), channel_id=1, replica_groups=mesh['ctx'=4,'head'=4,'section'=2] {'head'}, dimensions={0} | all-to-all | bytes 2097152 | tf_op jit(solution)/shard_map/all_to_all | solution.py:68
  73.3 0.9 %reshape.115 = bf16[128,1,4096]{2,1,0:T(2,128)(2,1)S(1)} reshape(bf16[4,2,65536]{2,1,0:T(2,128)(2,1)S(1)} %all_to_all.18) | data formatting | bytes 2097152
  74.3 1.1 %copy.47 = bf16[1,128,4096]{2,1,0:T(8,128)(2,1)S(1)} copy(bf16[1,128,4096]{2,0,1:T(2,128)(2,1)S(1)} %bitcast.44) | data formatting | bytes 2097152
  75.4 0.1 copy.48
  75.5 0.1 collective-permute-start
  75.6 2.6 %collective-permute-done = bf16[1,32,16384]{2,1,0:T(8,128)(2,1)S(1)} collective-permute-done((bf16[1,32,16384]{2,1,0:T(8,128)(2,1)S(1)}, bf16[1,32,16384]{2,1,0:T(8,128)(2,1)S(1)}, u32[]{:S(2)}, u32[]{:S(2)}) %collective-permute-start) | collective-permute-done | bytes 1048608 | tf_op jit(solution)/shard_map/ppermute | solution.py:14
  78.2 1.0 %copy.55 = bf16[1,32,16384]{2,1,0:T(8,128)(2,1)} copy(bf16[1,32,16384]{2,1,0:T(8,128)(2,1)S(1)} %collective-permute-done) | data formatting | bytes 2097152
  (5 shorter events, 0.1 us)
Async XLA Ops:
  20.9 7.3 %copy-start.1 = (bf16[1,128,256]{2,1,0:T(8,128)(2,1)S(1)}, bf16[1,128,256]{2,1,0:T(8,128)(2,1)}, u32[]{:S(2)}) copy-start(bf16[1,128,256]{2,1,0:T(8,128)(2,1)} %param.7) | copy-start | bytes 196612
  22.9 3.2 %copy-start = (f32[2,512,128,16]{2,1,3,0:T(8,128)}, f32[2,512,128,16]{2,1,3,0:T(8,128)S(1)}, u32[]{:S(2)}) copy-start(f32[2,512,128,16]{2,1,3,0:T(8,128)S(1)} %get-tuple-element.30) | copy-start | bytes 25165828
  75.5 2.7 %collective-permute-start = (bf16[1,32,16384]{2,1,0:T(8,128)(2,1)S(1)}, bf16[1,32,16384]{2,1,0:T(8,128)(2,1)S(1)}, u32[]{:S(2)}, u32[]{:S(2)}) collective-permute-start(bf16[1,32,16384]{2,1,0:T(8,128)(2,1)S(1)} %bitcast.51), channel_id=1, source_target_pairs={{0,1},{1,0},{2,3},{3,2},{4,5},{5,4},{6,7},{7,6},{8,9},{9,8},{10,11... | collective-permute-start | bytes 3145736 | tf_op jit(solution)/shard_map/ppermute | solution.py:14
where the time goes:
time: 79.6 us; the launch traced here: 79.2 us
  blocking collectives  42.5 us (53%)
  local copies, waits for them, and re-layouts  14.6 us (18%)
  other arithmetic  11.7 us (15%)
  matrix products  7.55 us (9%)
  waiting for transfers between devices  2.65 us (3%)
    all_gather x1, blocking collectives, local(): v_piece = lax.all_gather(values, 'ctx', axis=1, tiled=True)[0]  14.5 us
    all_gather x1, blocking collectives, local(): k_piece = lax.all_gather(keys, 'ctx', axis=1, tiled=True)[0]  14.5 us
    all_to_all x1, blocking collectives, local(): lax.all_to_all(attn, 'head', split_axis=1, concat_axis=2, tiled=True)  13.5 us
    unnamed x11, local copies, waits for them, and re-layouts  9.97 us
    unnamed x1, other arithmetic  7.02 us
    dot_general x1, matrix products, one_block(): jnp.einsum('tkgs,skd->tkgd', weight_b, v_block, preferred_element_type=jn...  5.63 us
    reshape x1, local copies, waits for them, and re-layouts, local(): (acc_all / sum_all[..., None]).astype(jnp.bfloat16)  2.91 us
    ppermute x1, waiting for transfers between devices, passed_along(): return lax.ppermute(value, axis, pairs)  2.65 us
  transfers between devices with their start and end apart: 1, of which 1 were waited for; matrix products, arithmetic and copies ran while one was open for 0% of the time, Pallas kernels for 0%

commit v1 on v0

v1 whole, which is shorter than its diff:
```python
import functools

import jax
import jax.numpy as jnp
from jax import lax
from jax.experimental import pallas as pl
from jax.experimental.pallas import tpu as pltpu
from jax.sharding import PartitionSpec as P

HD = 128
LOG2E = 1.4426950408889634
VMEM = pltpu.VMEM
VMEM_LIMIT = 48 * 1024 * 1024
BLOCK = 8


def bias_kernel(lengths, order, *refs):
    bias = refs[-1]
    shards, rows = order.shape
    c = lax.axis_index("ctx")
    pos = order[pl.ds(c, 1), :]
    lo = jnp.zeros_like(pos)
    start = jnp.int32(0)
    for n in range(lengths.shape[0]):
        lo = jnp.where(pos >= start, start, lo)
        start = start + lengths[n]
    square = (rows, rows)
    pos_rows = jnp.transpose(jnp.broadcast_to(pos.astype(jnp.float32), square))
    lo_rows = jnp.transpose(jnp.broadcast_to(lo.astype(jnp.float32), square))

    for step in range(shards):
        key_pos = order[pl.ds(jnp.bitwise_xor(c, step), 1), :].astype(jnp.float32)
        seen = (key_pos >= lo_rows) & (key_pos <= pos_rows)
        bias[:, step * rows : (step + 1) * rows] = jnp.where(seen, 0.0, -jnp.inf)


def attend_kernel(scale, slots, pieces, q, bias, *refs):
    outs = refs[-len(slots) :]
    part, width = outs[0].shape
    heads = width // HD
    me = lax.axis_index("head")
    for index, group in enumerate(sorted({group for _, group in slots})):
        kvs = refs[index * pieces : (index + 1) * pieces]
        kvs = [kv[group] if len(kv.shape) == 3 else kv[...] for kv in kvs]
        keys = jnp.concatenate([kv[:, :HD] for kv in kvs], axis=0)
        vals = jnp.concatenate([kv[:, HD:] for kv in kvs], axis=0)
        vals = jnp.concatenate([vals, jnp.ones_like(vals)], axis=1)
        for d, out in [(d, out) for (d, g), out in zip(slots, outs) if g == group]:
            rows = pl.ds(pl.multiple_of(jnp.bitwise_xor(me, d) * part, part), part)
            seen = bias[rows, :][None]
            for first in range(0, heads, BLOCK):
                block = [slice(j * HD, (j + 1) * HD) for j in range(first, min(first + BLOCK, heads))]
                shift = group * width
                stacked = jnp.concatenate(
                    [q[0, rows, shift + col.start : shift + col.stop] for col in block], axis=0
                )
                score = lax.dot_general(
                    stacked, keys, (((1,), (1,)), ((), ())), preferred_element_type=jnp.float32
                )
                score = score.reshape(len(block), part, -1) + seen
                top = jnp.max(score, axis=2, keepdims=True)
                weight = jnp.exp2((score - top) * scale).astype(jnp.bfloat16)
                both = jnp.dot(
                    weight.reshape(len(block) * part, -1), vals, preferred_element_type=jnp.float32
                )
                attn = (both[:, :HD] / both[:, HD:]).astype(jnp.bfloat16)
                for j, col in enumerate(block):
                    out[:, col] = attn[j * part : (j + 1) * part]


def place_kernel(slots, groups, *refs):
    pieces, out, sem = refs[: len(slots)], refs[-2], refs[-1]
    width = pieces[0].shape[1]
    me = lax.axis_index("head")
    copies = []
    for index, (d, g) in enumerate(slots):
        at = pl.multiple_of((jnp.bitwise_xor(me, d) * groups + g) * width, width)
        copies.append(
            pltpu.make_async_copy(pieces[index], out.at[0, :, pl.ds(at, width)], sem.at[index])
        )
    for copy in copies:
        copy.start()
    for copy in copies:
        copy.wait()


def local(queries, keys, values, order, doc_lengths):
    rows = queries.shape[1]
    groups = keys.shape[2] // HD
    width = queries.shape[2] // groups
    shards = lax.axis_size("ctx")
    heads = lax.axis_size("head")
    sections = lax.axis_size("section")
    part = rows // heads
    smem = pl.BlockSpec(memory_space=pltpu.SMEM)
    vmem = pl.BlockSpec(memory_space=VMEM)
    anywhere = pl.BlockSpec(memory_space=pl.ANY)
    params = pltpu.CompilerParams(vmem_limit_bytes=VMEM_LIMIT)
    turn = sorted(range(heads), key=lambda d: (-bin(d).count("1"), d))

    def handed(value, step):
        pairs = [
            (c * sections + s, (c ^ step) * sections + (s + 1) % sections)
            for c in range(shards)
            for s in range(sections)
        ]
        return lax.ppermute(value, ("ctx", "section"), pairs)

    def passed(value, step):
        return lax.ppermute(value, "ctx", [(c, c ^ step) for c in range(shards)])

    def after(value, *others):
        return lax.optimization_barrier((value, *others))[0]

    rows_q = handed(queries, 0)
    bias = pl.pallas_call(
        bias_kernel,
        out_shape=jax.ShapeDtypeStruct((rows, rows * shards), jnp.float32),
        in_specs=[smem, vmem],
        out_specs=vmem,
        compiler_params=params,
        name="bias",
    )(doc_lengths, order.reshape(shards, rows))

    packed = [
        jnp.concatenate([kv[0, :, g * HD : (g + 1) * HD] for kv in (keys, values)], axis=1)
        for g in range(groups)
    ]
    stacked = jnp.stack(packed)
    step = shards // 2
    blocks = {step: [handed(block, step) for block in packed]}
    own = handed(after(stacked, bias), 0)
    while step > 1:
        step //= 2
        for other in sorted(blocks):
            blocks[other ^ step] = [passed(after(block, bias), step) for block in blocks[other]]
        blocks[step] = [handed(after(stacked, bias), step)]
    kvs = [
        [own] + [blocks[step][g % len(blocks[step])] for step in range(1, shards)]
        for g in range(groups)
    ]

    def attend(slots, *others):
        needed = [block for g in sorted({g for _, g in slots}) for block in kvs[g]]
        return pl.pallas_call(
            functools.partial(attend_kernel, LOG2E / HD**0.5, slots, shards),
            out_shape=[jax.ShapeDtypeStruct((part, width), jnp.bfloat16)] * len(slots),
            in_specs=[vmem] * (2 + len(needed)) + [anywhere] * len(others),
            out_specs=[vmem] * len(slots),
            compiler_params=params,
            cost_estimate=pl.CostEstimate(
                flops=4 * part * width * rows * shards * len(slots),
                bytes_accessed=4 * part * width * len(slots),
                transcendentals=rows * shards * part * width // HD * len(slots),
            ),
            name="attend",
        )(rows_q, bias, *needed, *others)

    arrived = {}
    last = []
    for g in range(groups):
        parts = ((3,), (1, 2)) if g + 1 < groups else ((3, 1, 2),)
        for index, partners in enumerate(parts):
            for d in [(3,)][index] if g else ():
                last.append(arrived[d, g - 1])
            slots = [(d, g) for d in partners]
            pieces = attend(slots, *last)
            last = [pieces[-1]]
            for (d, _), piece in zip(slots, pieces):
                arrived[d, g] = lax.ppermute(piece, "head", [(h, h ^ d) for h in range(heads)])
    slots = [(0, g) for g in range(groups)]
    for slot, piece in zip(slots, attend(slots, *last)):
        arrived[slot] = piece

    final = groups - 1
    out = []
    for slots in [[(d, g) for g in range(final) for d in turn[:-1]] + [(0, g) for g in range(groups)], [(turn[0], final)], [(d, final) for d in turn[1:-1]]]:
        out = [
            pl.pallas_call(
                functools.partial(place_kernel, slots, groups),
                out_shape=jax.ShapeDtypeStruct((1, part, heads * groups * width), jnp.bfloat16),
                in_specs=[anywhere] * (len(slots) + len(out)),
                out_specs=anywhere,
                scratch_shapes=[pltpu.SemaphoreType.DMA((len(slots),))],
                input_output_aliases={len(slots): 0} if out else {},
                compiler_params=params,
                name="place",
            )(*[arrived[slot] for slot in slots], *out)
        ]
    return out[0]


def solution(mesh):
    in_specs = (
        P("section", "ctx", "head"),
        P("section", "ctx", "head"),
        P("section", "ctx", "head"),
        P(),
        P(),
    )
    out_specs = P("section", ("ctx", "head"), None)
    return jax.shard_map(local, mesh=mesh, in_specs=in_specs, out_specs=out_specs, check_vma=False)
```

time: 79.6 us -> 31.6 us (0.40)
  blocking collectives: 42.5 us -> 0 us
  starting transfers between devices: 0.07 us -> 18.3 us
  local copies, waits for them, and re-layouts: 14.6 us -> 1.47 us
  other arithmetic: 11.7 us -> 0.04 us
  matrix products: 7.55 us -> 0 us
  Pallas kernels: 0 us -> 6.88 us
  waiting for transfers between devices: 2.65 us -> 4.62 us
    all_gather x2 -> x0, blocking collectives: 29 us -> none  [the longest x1 14.5 us: local(): v_piece = lax.all_gather(values, 'ctx', axis=1, tiled=True)[0]]
    ppermute x1 -> x13, starting transfers between devices: 0.07 us -> 18.3 us  [the longest x5 8.72 us: handed(): return lax.ppermute(value, ('ctx', 'section'), pairs)]
    all_to_all x1 -> x0, blocking collectives: 13.5 us -> none  [local(): lax.all_to_all(attn, 'head', split_axis=1, concat_axis=2, tiled=True)]
    unnamed x11 -> x4, local copies, waits for them, and re-layouts: 9.97 us -> 0.65 us
    dot_general x2 -> x0, matrix products: 7.55 us -> none  [the longest x1 5.63 us: one_block(): jnp.einsum('tkgs,skd->tkgd', weight_b, v_block, preferred_element_type=jn...]
    unnamed x1 -> x0, other arithmetic: 7.02 us -> none
    pallas_call x0 -> x8, Pallas kernels: none -> 6.88 us  [the longest x4 3.96 us: attend(): pl.pallas_call(functools.partial(attend_kernel, LOG2E / HD ** 0.5, slots,...]
    reduce_sum x3 -> x0, other arithmetic: 2.98 us -> none  [the longest x1 2.12 us: one_block(): sum_new = sum_old * factor + jnp.sum(weight, axis=3)]
  transfers between devices with their start and end apart: 1 -> 13, of which waited for: 1 -> 6; matrix products, arithmetic and copies ran while one was open for 0% -> 3% of each run, Pallas kernels for 0% -> 20%
where the time goes in v1:
time: 31.6 us; the launch traced here: 31.4 us
  starting transfers between devices  18.3 us (58%)
  Pallas kernels  6.88 us (22%)
  waiting for transfers between devices  4.62 us (15%)
  local copies, waits for them, and re-layouts  1.47 us (5%)
    ppermute x5, starting transfers between devices, handed(): return lax.ppermute(value, ('ctx', 'section'), pairs)  8.72 us
    ppermute x6, starting transfers between devices, local(): lax.ppermute(piece, 'head', [(h, h ^ d) for h in range(heads)])  7.17 us
    pallas_call x4, Pallas kernels, attend(): pl.pallas_call(functools.partial(attend_kernel, LOG2E / HD ** 0.5, slots,...  3.96 us
    ppermute x2, starting transfers between devices, passed(): return lax.ppermute(value, 'ctx', [(c, c ^ step) for c in range(shards)])  2.43 us
    pallas_call x3, Pallas kernels, local(): pl.pallas_call(functools.partial(place_kernel, slots, groups), out_shape=...  2.26 us
    ppermute x6, waiting for transfers between devices, local(): lax.ppermute(piece, 'head', [(h, h ^ d) for h in range(heads)])  2.11 us
    ppermute x2, waiting for transfers between devices, passed(): return lax.ppermute(value, 'ctx', [(c, c ^ step) for c in range(shards)])  1.76 us
    squeeze x1, local copies, waits for them, and re-layouts, local(): kv[0, :, g * HD:(g + 1) * HD]  0.82 us
  transfers between devices with their start and end apart: 13, of which 6 were waited for; matrix products, arithmetic and copies ran while one was open for 3% of the time, Pallas kernels for 20%

profile of v1, /device:TPU:0, one launch (start us, length us, event | category | flops | bytes accessed | tf_op | source)
XLA Modules:
  0.0 31.4 jit_solution(18218113041082721251)
XLA Ops:
  0.0 0.5 %collective-permute-start = (bf16[1,128,4096]{2,1,0:T(8,128)(2,1)}, bf16[1,128,4096]{2,1,0:T(8,128)(2,1)S(1)}, u32[]{:S(2)}, u32[]{:S(2)}) collective-permute-start(bf16[1,128,4096]{2,1,0:T(8,128)(2,1)} %param.5), channel_id=1, source_target_pairs={{0,1},{1,0},{8,9},{9,8},{16,17},{17,16},{24,25},{25,24},{2,3},{3,2... | collective-permute-start | bytes 3145736 | tf_op jit(solution)/shard_map/ppermute | solution.py:107
  0.5 0.8 %slice_bitcast_fusion.2 = (bf16[128,128]{1,0:T(8,128)(2,1)S(1)}, bf16[128,128]{1,0:T(8,128)(2,1)S(1)}, bf16[128,128]{1,0:T(8,128)(2,1)S(1)}, bf16[128,128]{1,0:T(8,128)(2,1)S(1)}) fusion(bf16[1,128,256]{2,1,0:T(8,128)(2,1)} %param.7, bf16[1,128,256]{2,1,0:T(8,128)(2,1)} %param.6), kind=kLoop, calls=%fused_computation.5 | loop fusion | bytes 262144 | tf_op jit(solution)/shard_map/squeeze | solution.py:126
  1.3 3.8 %collective-permute-start.5 = (bf16[128,256]{1,0:T(8,128)(2,1)S(1)}, bf16[128,256]{1,0:T(8,128)(2,1)S(1)}, u32[]{:S(2)}, u32[]{:S(2)}) collective-permute-start(bf16[128,256]{1,0:T(8,128)(2,1)S(1)} %get-tuple-element.25), channel_id=1, source_target_pairs={{0,17},{1,16},{8,25},{9,24},{16,1},{17,0},{24,9},{25,8},{2,19},{3,... | collective-permute-start | bytes 196616 | tf_op jit(solution)/shard_map/ppermute | solution.py:107
  5.1 0.0 copy-start
  5.1 0.0 copy-start.1
  5.1 0.6 %copy-done = s32[512]{0:T(512)S(1)} copy-done((s32[512]{0:T(512)S(1)}, s32[512]{0:T(512)}, u32[]{:S(2)}) %copy-start) | copy-done | bytes 2072
  5.8 0.0 copy-done.1
  5.8 0.7 %bias.1 = f32[128,512]{1,0:T(8,128)S(1)} custom-call(s32[16]{0:T(128)S(1)} %copy-done.1, s32[4,128]{1,0:T(4,128)S(1)} %bitcast.13), custom_call_target="tpu_custom_call" | custom-call | tf_op jit(solution)/shard_map/bias/pallas_call | solution.py:116
  6.4 1.2 %collective-permute-start.2 = (bf16[2,128,256]{2,1,0:T(8,128)(2,1)S(1)}, bf16[2,128,256]{2,1,0:T(8,128)(2,1)S(1)}, u32[]{:S(2)}, u32[]{:S(2)}) collective-permute-start(bf16[2,128,256]{2,1,0:T(8,128)(2,1)S(1)} %pad_maximum_fusion), channel_id=1, source_target_pairs={{0,9},{1,8},{8,1},{9,0},{16,25},{17,24},{24,17},{25,16},{2,11},{3,... | collective-permute-start | bytes 393224 | tf_op jit(solution)/shard_map/ppermute | solution.py:107
  7.7 0.5 %collective-permute-start.1 = (bf16[2,128,256]{2,1,0:T(8,128)(2,1)S(1)}, bf16[2,128,256]{2,1,0:T(8,128)(2,1)S(1)}, u32[]{:S(2)}, u32[]{:S(2)}) collective-permute-start(bf16[2,128,256]{2,1,0:T(8,128)(2,1)S(1)} %pad_maximum_fusion), channel_id=1, source_target_pairs={{0,1},{1,0},{8,9},{9,8},{16,17},{17,16},{24,25},{25,24},{2,3},{3,2... | collective-permute-start | bytes 393224 | tf_op jit(solution)/shard_map/ppermute | solution.py:107
  8.2 0.7 %collective-permute-done.5.refs_2_ = bf16[128,256]{1,0:T(8,128)(2,1)S(1)} collective-permute-done((bf16[128,256]{1,0:T(8,128)(2,1)S(1)}, bf16[128,256]{1,0:T(8,128)(2,1)S(1)}, u32[]{:S(2)}, u32[]{:S(2)}) %collective-permute-start.5) | collective-permute-done | bytes 65568 | tf_op jit(solution)/shard_map/ppermute | solution.py:107
  8.9 0.9 %collective-permute-start.6 = (bf16[128,256]{1,0:T(8,128)(2,1)S(1)}, bf16[128,256]{1,0:T(8,128)(2,1)S(1)}, u32[]{:S(2)}, u32[]{:S(2)}) collective-permute-start(bf16[128,256]{1,0:T(8,128)(2,1)S(1)} %collective-permute-done.5.refs_2_), channel_id=1, source_target_pairs={{0,8},{8,0},{16,24},{24,16},{1,9},{9,1},{17,25},{25,17},{2,10},{10... | collective-permute-start | bytes 196616 | tf_op jit(solution)/shard_map/ppermute | solution.py:110
  9.8 2.7 %collective-permute-start.3 = (bf16[128,256]{1,0:T(8,128)(2,1)S(1)}, bf16[128,256]{1,0:T(8,128)(2,1)S(1)}, u32[]{:S(2)}, u32[]{:S(2)}) collective-permute-start(bf16[128,256]{1,0:T(8,128)(2,1)S(1)} %get-tuple-element.27), channel_id=1, source_target_pairs={{0,17},{1,16},{8,25},{9,24},{16,1},{17,0},{24,9},{25,8},{2,19},{3,... | collective-permute-start | bytes 196616 | tf_op jit(solution)/shard_map/ppermute | solution.py:107
  12.5 1.2 %collective-permute-done.6.refs_3_ = bf16[128,256]{1,0:T(8,128)(2,1)S(1)} collective-permute-done((bf16[128,256]{1,0:T(8,128)(2,1)S(1)}, bf16[128,256]{1,0:T(8,128)(2,1)S(1)}, u32[]{:S(2)}, u32[]{:S(2)}) %collective-permute-start.6) | collective-permute-done | bytes 65568 | tf_op jit(solution)/shard_map/ppermute | solution.py:110
  13.7 0.0 collective-permute-done.2.refs_1_.refs_5_
  13.7 0.0 collective-permute-done.1.refs_0_.refs_4_
  13.7 0.0 collective-permute-done.q
  13.7 0.7 %attend.4.refs_4_ = bf16[32,2048]{1,0:T(8,128)(2,1)S(1)} custom-call(bf16[1,128,4096]{2,1,0:T(8,128)(2,1)S(1)} %collective-permute-done.q, f32[128,512]{1,0:T(8,128)S(1)} %bias.1, bf16[2,128,256]{2,1,0:T(8,128)(2,1)S(1)} %collective-permute-done.1.refs_0_.refs_4_, bf16[2,128,256]{2,1,0:T(8,128)(2,1)S(1)} %collective-permute-done.2.refs_1_.refs_5_, ...), custom_call_target="tpu_custom_call" | custom-call | flops 134217728 | bytes 262144 | tf_op jit(solution)/shard_map/attend/pallas_call | solution.py:145
  14.4 2.5 %collective-permute-start.7 = (bf16[32,2048]{1,0:T(8,128)(2,1)S(1)}, bf16[32,2048]{1,0:T(8,128)(2,1)S(1)}, u32[]{:S(2)}, u32[]{:S(2)}) collective-permute-start(bf16[32,2048]{1,0:T(8,128)(2,1)S(1)} %attend.4.refs_4_), channel_id=1, source_target_pairs={{0,6},{2,4},{4,2},{6,0},{1,7},{3,5},{5,3},{7,1},{8,14},{10,12},{12... | collective-permute-start | bytes 393224 | tf_op jit(solution)/shard_map/ppermute | solution.py:170
  16.9 0.0 collective-permute-done.3.refs_2_.refs_6_
  16.9 1.6 %collective-permute-start.4 = (bf16[128,256]{1,0:T(8,128)(2,1)S(1)}, bf16[128,256]{1,0:T(8,128)(2,1)S(1)}, u32[]{:S(2)}, u32[]{:S(2)}) collective-permute-start(bf16[128,256]{1,0:T(8,128)(2,1)S(1)} %collective-permute-done.3.refs_2_.refs_6_), channel_id=1, source_target_pairs={{0,8},{8,0},{16,24},{24,16},{1,9},{9,1},{17,25},{25,17},{2,10},{10... | collective-permute-start | bytes 196616 | tf_op jit(solution)/shard_map/ppermute | solution.py:110
  18.5 1.0 %attend.5 = (bf16[32,2048]{1,0:T(8,128)(2,1)S(1)}, bf16[32,2048]{1,0:T(8,128)(2,1)S(1)}) custom-call(bf16[1,128,4096]{2,1,0:T(8,128)(2,1)S(1)} %collective-permute-done.q, f32[128,512]{1,0:T(8,128)S(1)} %bias.1, bf16[2,128,256]{2,1,0:T(8,128)(2,1)S(1)} %collective-permute-done.1.refs_0_.refs_4_, ...), custom_call_target="tpu_custom_call" | custom-call | flops 268435456 | bytes 524288 | tf_op jit(solution)/shard_map/attend/pallas_call | solution.py:145
  19.5 0.6 %collective-permute-start.11 = (bf16[32,2048]{1,0:T(8,128)(2,1)S(1)}, bf16[32,2048]{1,0:T(8,128)(2,1)S(1)}, u32[]{:S(2)}, u32[]{:S(2)}) collective-permute-start(bf16[32,2048]{1,0:T(8,128)(2,1)S(1)} %get-tuple-element.22), channel_id=1, source_target_pairs={{0,2},{2,0},{4,6},{6,4},{1,3},{3,1},{5,7},{7,5},{8,10},{10,8},{12,... | collective-permute-start | bytes 393224 | tf_op jit(solution)/shard_map/ppermute | solution.py:170
  20.1 0.5 %collective-permute-start.12 = (bf16[32,2048]{1,0:T(8,128)(2,1)S(1)}, bf16[32,2048]{1,0:T(8,128)(2,1)S(1)}, u32[]{:S(2)}, u32[]{:S(2)}) collective-permute-start(bf16[32,2048]{1,0:T(8,128)(2,1)S(1)} %get-tuple-element.18.refs_4_), channel_id=1, source_target_pairs={{0,4},{2,6},{4,0},{6,2},{1,5},{3,7},{5,1},{7,3},{8,12},{10,14},{12... | collective-permute-start | bytes 393224 | tf_op jit(solution)/shard_map/ppermute | solution.py:170
  20.6 0.6 %collective-permute-done.4.refs_3_.refs_7_ = bf16[128,256]{1,0:T(8,128)(2,1)S(1)} collective-permute-done((bf16[128,256]{1,0:T(8,128)(2,1)S(1)}, bf16[128,256]{1,0:T(8,128)(2,1)S(1)}, u32[]{:S(2)}, u32[]{:S(2)}) %collective-permute-start.4) | collective-permute-done | bytes 65568 | tf_op jit(solution)/shard_map/ppermute | solution.py:110
  21.2 0.0 collective-permute-done.7.refs_5_.refs_0_
  21.2 1.3 %attend.6 = (bf16[32,2048]{1,0:T(8,128)(2,1)S(1)}, bf16[32,2048]{1,0:T(8,128)(2,1)S(1)}, bf16[32,2048]{1,0:T(8,128)(2,1)S(1)}) custom-call(bf16[1,128,4096]{2,1,0:T(8,128)(2,1)S(1)} %collective-permute-done.q, f32[128,512]{1,0:T(8,128)S(1)} %bias.1, bf16[2,128,256]{2,1,0:T(8,128)(2,1)S(1)} %collective-permute-done.1.refs_0_.refs_4_, ...), custom_call_target="tpu_custom_call" | custom-call | flops 402653184 | bytes 786432 | tf_op jit(solution)/shard_map/attend/pallas_call | solution.py:145
  22.5 2.2 %collective-permute-start.10 = (bf16[32,2048]{1,0:T(8,128)(2,1)S(1)}, bf16[32,2048]{1,0:T(8,128)(2,1)S(1)}, u32[]{:S(2)}, u32[]{:S(2)}) collective-permute-start(bf16[32,2048]{1,0:T(8,128)(2,1)S(1)} %get-tuple-element.21), channel_id=1, source_target_pairs={{0,6},{2,4},{4,2},{6,0},{1,7},{3,5},{5,3},{7,1},{8,14},{10,12},{12... | collective-permute-start | bytes 393224 | tf_op jit(solution)/shard_map/ppermute | solution.py:170
  24.6 0.4 %collective-permute-start.8 = (bf16[32,2048]{1,0:T(8,128)(2,1)S(1)}, bf16[32,2048]{1,0:T(8,128)(2,1)S(1)}, u32[]{:S(2)}, u32[]{:S(2)}) collective-permute-start(bf16[32,2048]{1,0:T(8,128)(2,1)S(1)} %get-tuple-element.19), channel_id=1, source_target_pairs={{0,2},{2,0},{4,6},{6,4},{1,3},{3,1},{5,7},{7,5},{8,10},{10,8},{12,... | collective-permute-start | bytes 393224 | tf_op jit(solution)/shard_map/ppermute | solution.py:170
  25.0 1.0 %collective-permute-start.9 = (bf16[32,2048]{1,0:T(8,128)(2,1)S(1)}, bf16[32,2048]{1,0:T(8,128)(2,1)S(1)}, u32[]{:S(2)}, u32[]{:S(2)}) collective-permute-start(bf16[32,2048]{1,0:T(8,128)(2,1)S(1)} %get-tuple-element.20.refs_8_), channel_id=1, source_target_pairs={{0,4},{2,6},{4,0},{6,2},{1,5},{3,7},{5,1},{7,3},{8,12},{10,14},{12... | collective-permute-start | bytes 393224 | tf_op jit(solution)/shard_map/ppermute | solution.py:170
  26.0 1.0 %attend.7 = (bf16[32,2048]{1,0:T(8,128)(2,1)S(1)}, bf16[32,2048]{1,0:T(8,128)(2,1)S(1)}) custom-call(bf16[1,128,4096]{2,1,0:T(8,128)(2,1)S(1)} %collective-permute-done.q, f32[128,512]{1,0:T(8,128)S(1)} %bias.1, bf16[2,128,256]{2,1,0:T(8,128)(2,1)S(1)} %collective-permute-done.1.refs_0_.refs_4_, ...), custom_call_target="tpu_custom_call" | custom-call | flops 268435456 | bytes 524288 | tf_op jit(solution)/shard_map/attend/pallas_call | solution.py:145
  27.0 0.0 collective-permute-done.11.refs_1_
  27.1 0.0 collective-permute-done.12.refs_2_
  27.1 0.9 %place.3.refs_1_ = bf16[1,32,16384]{2,1,0:T(8,128)(2,1)} custom-call(bf16[32,2048]{1,0:T(8,128)(2,1)S(1)} %collective-permute-done.7.refs_5_.refs_0_, bf16[32,2048]{1,0:T(8,128)(2,1)S(1)} %collective-permute-done.11.refs_1_, bf16[32,2048]{1,0:T(8,128)(2,1)S(1)} %collective-permute-done.12.refs_2_, bf16[32,2048]{1,0:T(8,128)(2,1)S(1)} %get-tuple-element.23.refs_3_, ...), custom_call_target="tpu_custom_call" | custom-call | tf_op jit(solution)/shard_map/place/pallas_call | solution.py:179
  28.0 1.3 %collective-permute-done.10.refs_0_ = bf16[32,2048]{1,0:T(8,128)(2,1)S(1)} collective-permute-done((bf16[32,2048]{1,0:T(8,128)(2,1)S(1)}, bf16[32,2048]{1,0:T(8,128)(2,1)S(1)}, u32[]{:S(2)}, u32[]{:S(2)}) %collective-permute-start.10) | collective-permute-done | bytes 131104 | tf_op jit(solution)/shard_map/ppermute | solution.py:170
  29.2 0.7 %place.4.refs_2_ = bf16[1,32,16384]{2,1,0:T(8,128)(2,1)} custom-call(bf16[32,2048]{1,0:T(8,128)(2,1)S(1)} %collective-permute-done.10.refs_0_, bf16[1,32,16384]{2,1,0:T(8,128)(2,1)} %place.3.refs_1_), custom_call_target="tpu_custom_call", output_to_operand_aliasing={{}: (1, {})} | custom-call | tf_op jit(solution)/shard_map/place/pallas_call | solution.py:179
  29.9 0.8 %collective-permute-done.8.refs_0_ = bf16[32,2048]{1,0:T(8,128)(2,1)S(1)} collective-permute-done((bf16[32,2048]{1,0:T(8,128)(2,1)S(1)}, bf16[32,2048]{1,0:T(8,128)(2,1)S(1)}, u32[]{:S(2)}, u32[]{:S(2)}) %collective-permute-start.8) | collective-permute-done | bytes 131104 | tf_op jit(solution)/shard_map/ppermute | solution.py:170
  30.7 0.1 collective-permute-done.9.refs_1_
  30.7 0.7 %place.5 = bf16[1,32,16384]{2,1,0:T(8,128)(2,1)} custom-call(bf16[32,2048]{1,0:T(8,128)(2,1)S(1)} %collective-permute-done.8.refs_0_, bf16[32,2048]{1,0:T(8,128)(2,1)S(1)} %collective-permute-done.9.refs_1_, bf16[1,32,16384]{2,1,0:T(8,128)(2,1)} %place.4.refs_2_), custom_call_target="tpu_custom_call", output_to_operand_aliasing={{}: (2, {})} | custom-call | tf_op jit(solution)/shard_map/place/pallas_call | solution.py:179
  (3 shorter events, 0.0 us)
Async XLA Ops:
  0.0 13.7 %collective-permute-start = (bf16[1,128,4096]{2,1,0:T(8,128)(2,1)}, bf16[1,128,4096]{2,1,0:T(8,128)(2,1)S(1)}, u32[]{:S(2)}, u32[]{:S(2)}) collective-permute-start(bf16[1,128,4096]{2,1,0:T(8,128)(2,1)} %param.5), channel_id=1, source_target_pairs={{0,1},{1,0},{8,9},{9,8},{16,17},{17,16},{24,25},{25,24},{2,3},{3,2... | collective-permute-start | bytes 3145736 | tf_op jit(solution)/shard_map/ppermute | solution.py:107
  1.3 7.6 %collective-permute-start.5 = (bf16[128,256]{1,0:T(8,128)(2,1)S(1)}, bf16[128,256]{1,0:T(8,128)(2,1)S(1)}, u32[]{:S(2)}, u32[]{:S(2)}) collective-permute-start(bf16[128,256]{1,0:T(8,128)(2,1)S(1)} %get-tuple-element.25), channel_id=1, source_target_pairs={{0,17},{1,16},{8,25},{9,24},{16,1},{17,0},{24,9},{25,8},{2,19},{3,... | collective-permute-start | bytes 196616 | tf_op jit(solution)/shard_map/ppermute | solution.py:107
  5.1 0.7 %copy-start = (s32[512]{0:T(512)S(1)}, s32[512]{0:T(512)}, u32[]{:S(2)}) copy-start(s32[512]{0:T(512)} %param.8) | copy-start | bytes 6148
  5.1 0.7 %copy-start.1 = (s32[16]{0:T(128)S(1)}, s32[16]{0:T(128)}, u32[]{:S(2)}) copy-start(s32[16]{0:T(128)} %lengths.1) | copy-start | bytes 196
  6.4 7.3 %collective-permute-start.2 = (bf16[2,128,256]{2,1,0:T(8,128)(2,1)S(1)}, bf16[2,128,256]{2,1,0:T(8,128)(2,1)S(1)}, u32[]{:S(2)}, u32[]{:S(2)}) collective-permute-start(bf16[2,128,256]{2,1,0:T(8,128)(2,1)S(1)} %pad_maximum_fusion), channel_id=1, source_target_pairs={{0,9},{1,8},{8,1},{9,0},{16,25},{17,24},{24,17},{25,16},{2,11},{3,... | collective-permute-start | bytes 393224 | tf_op jit(solution)/shard_map/ppermute | solution.py:107
  7.7 6.0 %collective-permute-start.1 = (bf16[2,128,256]{2,1,0:T(8,128)(2,1)S(1)}, bf16[2,128,256]{2,1,0:T(8,128)(2,1)S(1)}, u32[]{:S(2)}, u32[]{:S(2)}) collective-permute-start(bf16[2,128,256]{2,1,0:T(8,128)(2,1)S(1)} %pad_maximum_fusion), channel_id=1, source_target_pairs={{0,1},{1,0},{8,9},{9,8},{16,17},{17,16},{24,25},{25,24},{2,3},{3,2... | collective-permute-start | bytes 393224 | tf_op jit(solution)/shard_map/ppermute | solution.py:107
  8.9 4.8 %collective-permute-start.6 = (bf16[128,256]{1,0:T(8,128)(2,1)S(1)}, bf16[128,256]{1,0:T(8,128)(2,1)S(1)}, u32[]{:S(2)}, u32[]{:S(2)}) collective-permute-start(bf16[128,256]{1,0:T(8,128)(2,1)S(1)} %collective-permute-done.5.refs_2_), channel_id=1, source_target_pairs={{0,8},{8,0},{16,24},{24,16},{1,9},{9,1},{17,25},{25,17},{2,10},{10... | collective-permute-start | bytes 196616 | tf_op jit(solution)/shard_map/ppermute | solution.py:110
  9.8 7.2 %collective-permute-start.3 = (bf16[128,256]{1,0:T(8,128)(2,1)S(1)}, bf16[128,256]{1,0:T(8,128)(2,1)S(1)}, u32[]{:S(2)}, u32[]{:S(2)}) collective-permute-start(bf16[128,256]{1,0:T(8,128)(2,1)S(1)} %get-tuple-element.27), channel_id=1, source_target_pairs={{0,17},{1,16},{8,25},{9,24},{16,1},{17,0},{24,9},{25,8},{2,19},{3,... | collective-permute-start | bytes 196616 | tf_op jit(solution)/shard_map/ppermute | solution.py:107
  14.4 6.8 %collective-permute-start.7 = (bf16[32,2048]{1,0:T(8,128)(2,1)S(1)}, bf16[32,2048]{1,0:T(8,128)(2,1)S(1)}, u32[]{:S(2)}, u32[]{:S(2)}) collective-permute-start(bf16[32,2048]{1,0:T(8,128)(2,1)S(1)} %attend.4.refs_4_), channel_id=1, source_target_pairs={{0,6},{2,4},{4,2},{6,0},{1,7},{3,5},{5,3},{7,1},{8,14},{10,12},{12... | collective-permute-start | bytes 393224 | tf_op jit(solution)/shard_map/ppermute | solution.py:170
  16.9 4.3 %collective-permute-start.4 = (bf16[128,256]{1,0:T(8,128)(2,1)S(1)}, bf16[128,256]{1,0:T(8,128)(2,1)S(1)}, u32[]{:S(2)}, u32[]{:S(2)}) collective-permute-start(bf16[128,256]{1,0:T(8,128)(2,1)S(1)} %collective-permute-done.3.refs_2_.refs_6_), channel_id=1, source_target_pairs={{0,8},{8,0},{16,24},{24,16},{1,9},{9,1},{17,25},{25,17},{2,10},{10... | collective-permute-start | bytes 196616 | tf_op jit(solution)/shard_map/ppermute | solution.py:110
  19.5 7.5 %collective-permute-start.11 = (bf16[32,2048]{1,0:T(8,128)(2,1)S(1)}, bf16[32,2048]{1,0:T(8,128)(2,1)S(1)}, u32[]{:S(2)}, u32[]{:S(2)}) collective-permute-start(bf16[32,2048]{1,0:T(8,128)(2,1)S(1)} %get-tuple-element.22), channel_id=1, source_target_pairs={{0,2},{2,0},{4,6},{6,4},{1,3},{3,1},{5,7},{7,5},{8,10},{10,8},{12,... | collective-permute-start | bytes 393224 | tf_op jit(solution)/shard_map/ppermute | solution.py:170
  20.1 6.9 %collective-permute-start.12 = (bf16[32,2048]{1,0:T(8,128)(2,1)S(1)}, bf16[32,2048]{1,0:T(8,128)(2,1)S(1)}, u32[]{:S(2)}, u32[]{:S(2)}) collective-permute-start(bf16[32,2048]{1,0:T(8,128)(2,1)S(1)} %get-tuple-element.18.refs_4_), channel_id=1, source_target_pairs={{0,4},{2,6},{4,0},{6,2},{1,5},{3,7},{5,1},{7,3},{8,12},{10,14},{12... | collective-permute-start | bytes 393224 | tf_op jit(solution)/shard_map/ppermute | solution.py:170
  22.5 6.7 %collective-permute-start.10 = (bf16[32,2048]{1,0:T(8,128)(2,1)S(1)}, bf16[32,2048]{1,0:T(8,128)(2,1)S(1)}, u32[]{:S(2)}, u32[]{:S(2)}) collective-permute-start(bf16[32,2048]{1,0:T(8,128)(2,1)S(1)} %get-tuple-element.21), channel_id=1, source_target_pairs={{0,6},{2,4},{4,2},{6,0},{1,7},{3,5},{5,3},{7,1},{8,14},{10,12},{12... | collective-permute-start | bytes 393224 | tf_op jit(solution)/shard_map/ppermute | solution.py:170
  24.6 6.0 %collective-permute-start.8 = (bf16[32,2048]{1,0:T(8,128)(2,1)S(1)}, bf16[32,2048]{1,0:T(8,128)(2,1)S(1)}, u32[]{:S(2)}, u32[]{:S(2)}) collective-permute-start(bf16[32,2048]{1,0:T(8,128)(2,1)S(1)} %get-tuple-element.19), channel_id=1, source_target_pairs={{0,2},{2,0},{4,6},{6,4},{1,3},{3,1},{5,7},{7,5},{8,10},{10,8},{12,... | collective-permute-start | bytes 393224 | tf_op jit(solution)/shard_map/ppermute | solution.py:170
  25.0 5.7 %collective-permute-start.9 = (bf16[32,2048]{1,0:T(8,128)(2,1)S(1)}, bf16[32,2048]{1,0:T(8,128)(2,1)S(1)}, u32[]{:S(2)}, u32[]{:S(2)}) collective-permute-start(bf16[32,2048]{1,0:T(8,128)(2,1)S(1)} %get-tuple-element.20.refs_8_), channel_id=1, source_target_pairs={{0,4},{2,6},{4,0},{6,2},{1,5},{3,7},{5,1},{7,3},{8,12},{10,14},{12... | collective-permute-start | bytes 393224 | tf_op jit(solution)/shard_map/ppermute | solution.py:170

commit v2 on v1

--- a/solution.py
+++ b/solution.py
@@ -149,7 +149,7 @@
             out_specs=[vmem] * len(slots),
             compiler_params=params,
             cost_estimate=pl.CostEstimate(
-                flops=4 * part * width * rows * shards * len(slots),
+                flops=16 * part * width * rows * shards * len(slots),
                 bytes_accessed=4 * part * width * len(slots),
                 transcendentals=rows * shards * part * width // HD * len(slots),
             ),
@@ -161,12 +161,12 @@
     for g in range(groups):
         parts = ((3,), (1, 2)) if g + 1 < groups else ((3, 1, 2),)
         for index, partners in enumerate(parts):
-            for d in [(3,)][index] if g else ():
-                last.append(arrived[d, g - 1])
             slots = [(d, g) for d in partners]
             pieces = attend(slots, *last)
             last = [pieces[-1]]
             for (d, _), piece in zip(slots, pieces):
+                if g and d == 2:
+                    piece = after(piece, arrived[1, g - 1])
                 arrived[d, g] = lax.ppermute(piece, "head", [(h, h ^ d) for h in range(heads)])
     slots = [(0, g) for g in range(groups)]
     for slot, piece in zip(slots, attend(slots, *last)):

time: 31.6 us -> 33 us (1.044)
  waiting for transfers between devices: 4.62 us -> 10.5 us
  starting transfers between devices: 18.3 us -> 13.8 us
    ppermute x5, waiting for transfers between devices: 0.75 us -> 5.75 us  [handed(): return lax.ppermute(value, ('ctx', 'section'), pairs)]
    ppermute x5, starting transfers between devices: 8.72 us -> 5.99 us  [handed(): return lax.ppermute(value, ('ctx', 'section'), pairs)]
    ppermute x6, waiting for transfers between devices: 2.11 us -> 4.52 us  [local(): lax.ppermute(piece, 'head', [(h, h ^ d) for h in range(heads)])]
    ppermute x2, starting transfers between devices: 2.43 us -> 0.91 us  [passed(): return lax.ppermute(value, 'ctx', [(c, c ^ step) for c in range(shards)])]
    ppermute x2, waiting for transfers between devices: 1.76 us -> 0.25 us  [passed(): return lax.ppermute(value, 'ctx', [(c, c ^ step) for c in range(shards)])]
  transfers between devices with their start and end apart: 13 -> 13, of which waited for: 6 -> 6; matrix products, arithmetic and copies ran while one was open for 3% -> 3% of each run, Pallas kernels for 20% -> 19%
where the time goes in v2:
time: 33 us; the launch traced here: 32.8 us
  starting transfers between devices  13.8 us (42%)
  waiting for transfers between devices  10.5 us (32%)
  Pallas kernels  6.88 us (21%)
  local copies, waits for them, and re-layouts  1.47 us (4%)
    ppermute x6, starting transfers between devices, local(): lax.ppermute(piece, 'head', [(h, h ^ d) for h in range(heads)])  6.88 us
    ppermute x5, starting transfers between devices, handed(): return lax.ppermute(value, ('ctx', 'section'), pairs)  5.99 us
    ppermute x5, waiting for transfers between devices, handed(): return lax.ppermute(value, ('ctx', 'section'), pairs)  5.75 us
    ppermute x6, waiting for transfers between devices, local(): lax.ppermute(piece, 'head', [(h, h ^ d) for h in range(heads)])  4.52 us
    pallas_call x4, Pallas kernels, attend(): pl.pallas_call(functools.partial(attend_kernel, LOG2E / HD ** 0.5, slots,...  3.96 us
    pallas_call x3, Pallas kernels, local(): pl.pallas_call(functools.partial(place_kernel, slots, groups), out_shape=...  2.26 us
    ppermute x2, starting transfers between devices, passed(): return lax.ppermute(value, 'ctx', [(c, c ^ step) for c in range(shards)])  0.91 us
    squeeze x1, local copies, waits for them, and re-layouts, local(): kv[0, :, g * HD:(g + 1) * HD]  0.82 us
  transfers between devices with their start and end apart: 13, of which 6 were waited for; matrix products, arithmetic and copies ran while one was open for 3% of the time, Pallas kernels for 19%

profile of v2, /device:TPU:0, one launch (start us, length us, event | category | flops | bytes accessed | tf_op | source)
XLA Modules:
  0.0 32.8 jit_solution(16398495133402495821)
XLA Ops:
  0.0 0.5 %collective-permute-start = (bf16[1,128,4096]{2,1,0:T(8,128)(2,1)}, bf16[1,128,4096]{2,1,0:T(8,128)(2,1)S(1)}, u32[]{:S(2)}, u32[]{:S(2)}) collective-permute-start(bf16[1,128,4096]{2,1,0:T(8,128)(2,1)} %param.5), channel_id=1, source_target_pairs={{0,1},{1,0},{8,9},{9,8},{16,17},{17,16},{24,25},{25,24},{2,3},{3,2... | collective-permute-start | bytes 3145736 | tf_op jit(solution)/shard_map/ppermute | solution.py:107
  0.5 0.8 %slice_bitcast_fusion.2 = (bf16[128,128]{1,0:T(8,128)(2,1)S(1)}, bf16[128,128]{1,0:T(8,128)(2,1)S(1)}, bf16[128,128]{1,0:T(8,128)(2,1)S(1)}, bf16[128,128]{1,0:T(8,128)(2,1)S(1)}) fusion(bf16[1,128,256]{2,1,0:T(8,128)(2,1)} %param.7, bf16[1,128,256]{2,1,0:T(8,128)(2,1)} %param.6), kind=kLoop, calls=%fused_computation.5 | loop fusion | bytes 262144 | tf_op jit(solution)/shard_map/squeeze | solution.py:126
  1.3 3.8 %collective-permute-start.5 = (bf16[128,256]{1,0:T(8,128)(2,1)S(1)}, bf16[128,256]{1,0:T(8,128)(2,1)S(1)}, u32[]{:S(2)}, u32[]{:S(2)}) collective-permute-start(bf16[128,256]{1,0:T(8,128)(2,1)S(1)} %get-tuple-element.27), channel_id=1, source_target_pairs={{0,17},{1,16},{8,25},{9,24},{16,1},{17,0},{24,9},{25,8},{2,19},{3,... | collective-permute-start | bytes 196616 | tf_op jit(solution)/shard_map/ppermute | solution.py:107
  5.1 0.0 copy-start
  5.1 0.0 copy-start.1
  5.1 0.6 %copy-done = s32[512]{0:T(512)S(1)} copy-done((s32[512]{0:T(512)S(1)}, s32[512]{0:T(512)}, u32[]{:S(2)}) %copy-start) | copy-done | bytes 2072
  5.8 0.0 copy-done.1
  5.8 0.7 %bias.1 = f32[128,512]{1,0:T(8,128)S(1)} custom-call(s32[16]{0:T(128)S(1)} %copy-done.1, s32[4,128]{1,0:T(4,128)S(1)} %bitcast.13), custom_call_target="tpu_custom_call" | custom-call | tf_op jit(solution)/shard_map/bias/pallas_call | solution.py:116
  6.4 1.2 %collective-permute-start.2 = (bf16[2,128,256]{2,1,0:T(8,128)(2,1)S(1)}, bf16[2,128,256]{2,1,0:T(8,128)(2,1)S(1)}, u32[]{:S(2)}, u32[]{:S(2)}) collective-permute-start(bf16[2,128,256]{2,1,0:T(8,128)(2,1)S(1)} %pad_maximum_fusion), channel_id=1, source_target_pairs={{0,9},{1,8},{8,1},{9,0},{16,25},{17,24},{24,17},{25,16},{2,11},{3,... | collective-permute-start | bytes 393224 | tf_op jit(solution)/shard_map/ppermute | solution.py:107
  7.7 0.5 %collective-permute-start.1 = (bf16[2,128,256]{2,1,0:T(8,128)(2,1)S(1)}, bf16[2,128,256]{2,1,0:T(8,128)(2,1)S(1)}, u32[]{:S(2)}, u32[]{:S(2)}) collective-permute-start(bf16[2,128,256]{2,1,0:T(8,128)(2,1)S(1)} %pad_maximum_fusion), channel_id=1, source_target_pairs={{0,1},{1,0},{8,9},{9,8},{16,17},{17,16},{24,25},{25,24},{2,3},{3,2... | collective-permute-start | bytes 393224 | tf_op jit(solution)/shard_map/ppermute | solution.py:107
  8.2 0.0 collective-permute-start.3
  8.2 0.7 %collective-permute-done.5.refs_2_ = bf16[128,256]{1,0:T(8,128)(2,1)S(1)} collective-permute-done((bf16[128,256]{1,0:T(8,128)(2,1)S(1)}, bf16[128,256]{1,0:T(8,128)(2,1)S(1)}, u32[]{:S(2)}, u32[]{:S(2)}) %collective-permute-start.5) | collective-permute-done | bytes 65568 | tf_op jit(solution)/shard_map/ppermute | solution.py:107
  8.9 0.9 %collective-permute-start.6 = (bf16[128,256]{1,0:T(8,128)(2,1)S(1)}, bf16[128,256]{1,0:T(8,128)(2,1)S(1)}, u32[]{:S(2)}, u32[]{:S(2)}) collective-permute-start(bf16[128,256]{1,0:T(8,128)(2,1)S(1)} %collective-permute-done.5.refs_2_), channel_id=1, source_target_pairs={{0,8},{8,0},{16,24},{24,16},{1,9},{9,1},{17,25},{25,17},{2,10},{10... | collective-permute-start | bytes 196616 | tf_op jit(solution)/shard_map/ppermute | solution.py:110
  9.8 5.0 %collective-permute-done.3.refs_2_.refs_6_ = bf16[128,256]{1,0:T(8,128)(2,1)S(1)} collective-permute-done((bf16[128,256]{1,0:T(8,128)(2,1)S(1)}, bf16[128,256]{1,0:T(8,128)(2,1)S(1)}, u32[]{:S(2)}, u32[]{:S(2)}) %collective-permute-start.3) | collective-permute-done | bytes 65568 | tf_op jit(solution)/shard_map/ppermute | solution.py:107
  14.9 0.0 collective-permute-start.4
  14.9 0.2 collective-permute-done.6.refs_3_
  15.1 0.0 collective-permute-done.2.refs_1_.refs_5_
  15.1 0.0 collective-permute-done.1.refs_0_.refs_4_
  15.1 0.0 collective-permute-done.q
  15.1 0.7 %attend.4.refs_4_ = bf16[32,2048]{1,0:T(8,128)(2,1)S(1)} custom-call(bf16[1,128,4096]{2,1,0:T(8,128)(2,1)S(1)} %collective-permute-done.q, f32[128,512]{1,0:T(8,128)S(1)} %bias.1, bf16[2,128,256]{2,1,0:T(8,128)(2,1)S(1)} %collective-permute-done.1.refs_0_.refs_4_, bf16[2,128,256]{2,1,0:T(8,128)(2,1)S(1)} %collective-permute-done.2.refs_1_.refs_5_, ...), custom_call_target="tpu_custom_call" | custom-call | flops 536870912 | bytes 262144 | tf_op jit(solution)/shard_map/attend/pallas_call | solution.py:145
  15.8 2.5 %collective-permute-start.11 = (bf16[32,2048]{1,0:T(8,128)(2,1)S(1)}, bf16[32,2048]{1,0:T(8,128)(2,1)S(1)}, u32[]{:S(2)}, u32[]{:S(2)}) collective-permute-start(bf16[32,2048]{1,0:T(8,128)(2,1)S(1)} %attend.4.refs_4_), channel_id=1, source_target_pairs={{0,6},{2,4},{4,2},{6,0},{1,7},{3,5},{5,3},{7,1},{8,14},{10,12},{12... | collective-permute-start | bytes 393224 | tf_op jit(solution)/shard_map/ppermute | solution.py:170
  18.3 1.0 %attend.5 = (bf16[32,2048]{1,0:T(8,128)(2,1)S(1)}, bf16[32,2048]{1,0:T(8,128)(2,1)S(1)}) custom-call(bf16[1,128,4096]{2,1,0:T(8,128)(2,1)S(1)} %collective-permute-done.q, f32[128,512]{1,0:T(8,128)S(1)} %bias.1, bf16[2,128,256]{2,1,0:T(8,128)(2,1)S(1)} %collective-permute-done.1.refs_0_.refs_4_, ...), custom_call_target="tpu_custom_call" | custom-call | flops 1073741824 | bytes 524288 | tf_op jit(solution)/shard_map/attend/pallas_call | solution.py:145
  19.3 0.6 %collective-permute-start.8 = (bf16[32,2048]{1,0:T(8,128)(2,1)S(1)}, bf16[32,2048]{1,0:T(8,128)(2,1)S(1)}, u32[]{:S(2)}, u32[]{:S(2)}) collective-permute-start(bf16[32,2048]{1,0:T(8,128)(2,1)S(1)} %get-tuple-element.22), channel_id=1, source_target_pairs={{0,2},{2,0},{4,6},{6,4},{1,3},{3,1},{5,7},{7,5},{8,10},{10,8},{12,... | collective-permute-start | bytes 393224 | tf_op jit(solution)/shard_map/ppermute | solution.py:170
  19.9 0.5 %collective-permute-start.12 = (bf16[32,2048]{1,0:T(8,128)(2,1)S(1)}, bf16[32,2048]{1,0:T(8,128)(2,1)S(1)}, u32[]{:S(2)}, u32[]{:S(2)}) collective-permute-start(bf16[32,2048]{1,0:T(8,128)(2,1)S(1)} %get-tuple-element.19.refs_4_), channel_id=1, source_target_pairs={{0,4},{2,6},{4,0},{6,2},{1,5},{3,7},{5,1},{7,3},{8,12},{10,14},{12... | collective-permute-start | bytes 393224 | tf_op jit(solution)/shard_map/ppermute | solution.py:170
  20.4 0.0 collective-permute-done.4.refs_3_.refs_7_
  20.4 1.3 %attend.6 = (bf16[32,2048]{1,0:T(8,128)(2,1)S(1)}, bf16[32,2048]{1,0:T(8,128)(2,1)S(1)}, bf16[32,2048]{1,0:T(8,128)(2,1)S(1)}) custom-call(bf16[1,128,4096]{2,1,0:T(8,128)(2,1)S(1)} %collective-permute-done.q, f32[128,512]{1,0:T(8,128)S(1)} %bias.1, bf16[2,128,256]{2,1,0:T(8,128)(2,1)S(1)} %collective-permute-done.1.refs_0_.refs_4_, ...), custom_call_target="tpu_custom_call" | custom-call | flops 1610612736 | bytes 786432 | tf_op jit(solution)/shard_map/attend/pallas_call | solution.py:145
  21.7 1.6 %collective-permute-start.7 = (bf16[32,2048]{1,0:T(8,128)(2,1)S(1)}, bf16[32,2048]{1,0:T(8,128)(2,1)S(1)}, u32[]{:S(2)}, u32[]{:S(2)}) collective-permute-start(bf16[32,2048]{1,0:T(8,128)(2,1)S(1)} %get-tuple-element.20), channel_id=1, source_target_pairs={{0,2},{2,0},{4,6},{6,4},{1,3},{3,1},{5,7},{7,5},{8,10},{10,8},{12,... | collective-permute-start | bytes 393224 | tf_op jit(solution)/shard_map/ppermute | solution.py:170
  23.3 1.5 %collective-permute-start.10 = (bf16[32,2048]{1,0:T(8,128)(2,1)S(1)}, bf16[32,2048]{1,0:T(8,128)(2,1)S(1)}, u32[]{:S(2)}, u32[]{:S(2)}) collective-permute-start(bf16[32,2048]{1,0:T(8,128)(2,1)S(1)} %get-tuple-element.24), channel_id=1, source_target_pairs={{0,6},{2,4},{4,2},{6,0},{1,7},{3,5},{5,3},{7,1},{8,14},{10,12},{12... | collective-permute-start | bytes 393224 | tf_op jit(solution)/shard_map/ppermute | solution.py:170
  24.8 1.1 %collective-permute-done.8.refs_1_ = bf16[32,2048]{1,0:T(8,128)(2,1)S(1)} collective-permute-done((bf16[32,2048]{1,0:T(8,128)(2,1)S(1)}, bf16[32,2048]{1,0:T(8,128)(2,1)S(1)}, u32[]{:S(2)}, u32[]{:S(2)}) %collective-permute-start.8) | collective-permute-done | bytes 131104 | tf_op jit(solution)/shard_map/ppermute | solution.py:170
  25.8 0.2 collective-permute-start.9
  26.0 1.0 %attend.7 = (bf16[32,2048]{1,0:T(8,128)(2,1)S(1)}, bf16[32,2048]{1,0:T(8,128)(2,1)S(1)}) custom-call(bf16[1,128,4096]{2,1,0:T(8,128)(2,1)S(1)} %collective-permute-done.q, f32[128,512]{1,0:T(8,128)S(1)} %bias.1, bf16[2,128,256]{2,1,0:T(8,128)(2,1)S(1)} %collective-permute-done.1.refs_0_.refs_4_, ...), custom_call_target="tpu_custom_call" | custom-call | flops 1073741824 | bytes 524288 | tf_op jit(solution)/shard_map/attend/pallas_call | solution.py:145
  27.0 0.0 collective-permute-done.11.refs_0_
  27.1 0.0 collective-permute-done.12.refs_2_
  27.1 0.9 %place.3.refs_1_ = bf16[1,32,16384]{2,1,0:T(8,128)(2,1)} custom-call(bf16[32,2048]{1,0:T(8,128)(2,1)S(1)} %collective-permute-done.11.refs_0_, bf16[32,2048]{1,0:T(8,128)(2,1)S(1)} %collective-permute-done.8.refs_1_, bf16[32,2048]{1,0:T(8,128)(2,1)S(1)} %collective-permute-done.12.refs_2_, bf16[32,2048]{1,0:T(8,128)(2,1)S(1)} %get-tuple-element.25.refs_3_, ...), custom_call_target="tpu_custom_call" | custom-call | tf_op jit(solution)/shard_map/place/pallas_call | solution.py:179
  28.0 2.7 %collective-permute-done.10.refs_0_ = bf16[32,2048]{1,0:T(8,128)(2,1)S(1)} collective-permute-done((bf16[32,2048]{1,0:T(8,128)(2,1)S(1)}, bf16[32,2048]{1,0:T(8,128)(2,1)S(1)}, u32[]{:S(2)}, u32[]{:S(2)}) %collective-permute-start.10) | collective-permute-done | bytes 131104 | tf_op jit(solution)/shard_map/ppermute | solution.py:170
  30.7 0.7 %place.4.refs_2_ = bf16[1,32,16384]{2,1,0:T(8,128)(2,1)} custom-call(bf16[32,2048]{1,0:T(8,128)(2,1)S(1)} %collective-permute-done.10.refs_0_, bf16[1,32,16384]{2,1,0:T(8,128)(2,1)} %place.3.refs_1_), custom_call_target="tpu_custom_call", output_to_operand_aliasing={{}: (1, {})} | custom-call | tf_op jit(solution)/shard_map/place/pallas_call | solution.py:179
  31.3 0.0 collective-permute-done.7.refs_0_
  31.3 0.8 %collective-permute-done.9.refs_1_ = bf16[32,2048]{1,0:T(8,128)(2,1)S(1)} collective-permute-done((bf16[32,2048]{1,0:T(8,128)(2,1)S(1)}, bf16[32,2048]{1,0:T(8,128)(2,1)S(1)}, u32[]{:S(2)}, u32[]{:S(2)}) %collective-permute-start.9) | collective-permute-done | bytes 131104 | tf_op jit(solution)/shard_map/ppermute | solution.py:170
  32.1 0.7 %place.5 = bf16[1,32,16384]{2,1,0:T(8,128)(2,1)} custom-call(bf16[32,2048]{1,0:T(8,128)(2,1)S(1)} %collective-permute-done.7.refs_0_, bf16[32,2048]{1,0:T(8,128)(2,1)S(1)} %collective-permute-done.9.refs_1_, bf16[1,32,16384]{2,1,0:T(8,128)(2,1)} %place.4.refs_2_), custom_call_target="tpu_custom_call", output_to_operand_aliasing={{}: (2, {})} | custom-call | tf_op jit(solution)/shard_map/place/pallas_call | solution.py:179
  (3 shorter events, 0.0 us)
Async XLA Ops:
  0.0 15.1 %collective-permute-start = (bf16[1,128,4096]{2,1,0:T(8,128)(2,1)}, bf16[1,128,4096]{2,1,0:T(8,128)(2,1)S(1)}, u32[]{:S(2)}, u32[]{:S(2)}) collective-permute-start(bf16[1,128,4096]{2,1,0:T(8,128)(2,1)} %param.5), channel_id=1, source_target_pairs={{0,1},{1,0},{8,9},{9,8},{16,17},{17,16},{24,25},{25,24},{2,3},{3,2... | collective-permute-start | bytes 3145736 | tf_op jit(solution)/shard_map/ppermute | solution.py:107
  1.3 7.6 %collective-permute-start.5 = (bf16[128,256]{1,0:T(8,128)(2,1)S(1)}, bf16[128,256]{1,0:T(8,128)(2,1)S(1)}, u32[]{:S(2)}, u32[]{:S(2)}) collective-permute-start(bf16[128,256]{1,0:T(8,128)(2,1)S(1)} %get-tuple-element.27), channel_id=1, source_target_pairs={{0,17},{1,16},{8,25},{9,24},{16,1},{17,0},{24,9},{25,8},{2,19},{3,... | collective-permute-start | bytes 196616 | tf_op jit(solution)/shard_map/ppermute | solution.py:107
  5.1 0.7 %copy-start = (s32[512]{0:T(512)S(1)}, s32[512]{0:T(512)}, u32[]{:S(2)}) copy-start(s32[512]{0:T(512)} %param.8) | copy-start | bytes 6148
  5.1 0.7 %copy-start.1 = (s32[16]{0:T(128)S(1)}, s32[16]{0:T(128)}, u32[]{:S(2)}) copy-start(s32[16]{0:T(128)} %lengths.1) | copy-start | bytes 196
  6.4 8.7 %collective-permute-start.2 = (bf16[2,128,256]{2,1,0:T(8,128)(2,1)S(1)}, bf16[2,128,256]{2,1,0:T(8,128)(2,1)S(1)}, u32[]{:S(2)}, u32[]{:S(2)}) collective-permute-start(bf16[2,128,256]{2,1,0:T(8,128)(2,1)S(1)} %pad_maximum_fusion), channel_id=1, source_target_pairs={{0,9},{1,8},{8,1},{9,0},{16,25},{17,24},{24,17},{25,16},{2,11},{3,... | collective-permute-start | bytes 393224 | tf_op jit(solution)/shard_map/ppermute | solution.py:107
  7.7 7.4 %collective-permute-start.1 = (bf16[2,128,256]{2,1,0:T(8,128)(2,1)S(1)}, bf16[2,128,256]{2,1,0:T(8,128)(2,1)S(1)}, u32[]{:S(2)}, u32[]{:S(2)}) collective-permute-start(bf16[2,128,256]{2,1,0:T(8,128)(2,1)S(1)} %pad_maximum_fusion), channel_id=1, source_target_pairs={{0,1},{1,0},{8,9},{9,8},{16,17},{17,16},{24,25},{25,24},{2,3},{3,2... | collective-permute-start | bytes 393224 | tf_op jit(solution)/shard_map/ppermute | solution.py:107
  8.2 6.7 %collective-permute-start.3 = (bf16[128,256]{1,0:T(8,128)(2,1)S(1)}, bf16[128,256]{1,0:T(8,128)(2,1)S(1)}, u32[]{:S(2)}, u32[]{:S(2)}) collective-permute-start(bf16[128,256]{1,0:T(8,128)(2,1)S(1)} %get-tuple-element.29), channel_id=1, source_target_pairs={{0,17},{1,16},{8,25},{9,24},{16,1},{17,0},{24,9},{25,8},{2,19},{3,... | collective-permute-start | bytes 196616 | tf_op jit(solution)/shard_map/ppermute | solution.py:107
  8.9 6.2 %collective-permute-start.6 = (bf16[128,256]{1,0:T(8,128)(2,1)S(1)}, bf16[128,256]{1,0:T(8,128)(2,1)S(1)}, u32[]{:S(2)}, u32[]{:S(2)}) collective-permute-start(bf16[128,256]{1,0:T(8,128)(2,1)S(1)} %collective-permute-done.5.refs_2_), channel_id=1, source_target_pairs={{0,8},{8,0},{16,24},{24,16},{1,9},{9,1},{17,25},{25,17},{2,10},{10... | collective-permute-start | bytes 196616 | tf_op jit(solution)/shard_map/ppermute | solution.py:110
  14.9 5.6 %collective-permute-start.4 = (bf16[128,256]{1,0:T(8,128)(2,1)S(1)}, bf16[128,256]{1,0:T(8,128)(2,1)S(1)}, u32[]{:S(2)}, u32[]{:S(2)}) collective-permute-start(bf16[128,256]{1,0:T(8,128)(2,1)S(1)} %collective-permute-done.3.refs_2_.refs_6_), channel_id=1, source_target_pairs={{0,8},{8,0},{16,24},{24,16},{1,9},{9,1},{17,25},{25,17},{2,10},{10... | collective-permute-start | bytes 196616 | tf_op jit(solution)/shard_map/ppermute | solution.py:110
  15.8 11.2 %collective-permute-start.11 = (bf16[32,2048]{1,0:T(8,128)(2,1)S(1)}, bf16[32,2048]{1,0:T(8,128)(2,1)S(1)}, u32[]{:S(2)}, u32[]{:S(2)}) collective-permute-start(bf16[32,2048]{1,0:T(8,128)(2,1)S(1)} %attend.4.refs_4_), channel_id=1, source_target_pairs={{0,6},{2,4},{4,2},{6,0},{1,7},{3,5},{5,3},{7,1},{8,14},{10,12},{12... | collective-permute-start | bytes 393224 | tf_op jit(solution)/shard_map/ppermute | solution.py:170
  19.3 6.5 %collective-permute-start.8 = (bf16[32,2048]{1,0:T(8,128)(2,1)S(1)}, bf16[32,2048]{1,0:T(8,128)(2,1)S(1)}, u32[]{:S(2)}, u32[]{:S(2)}) collective-permute-start(bf16[32,2048]{1,0:T(8,128)(2,1)S(1)} %get-tuple-element.22), channel_id=1, source_target_pairs={{0,2},{2,0},{4,6},{6,4},{1,3},{3,1},{5,7},{7,5},{8,10},{10,8},{12,... | collective-permute-start | bytes 393224 | tf_op jit(solution)/shard_map/ppermute | solution.py:170
  19.9 7.1 %collective-permute-start.12 = (bf16[32,2048]{1,0:T(8,128)(2,1)S(1)}, bf16[32,2048]{1,0:T(8,128)(2,1)S(1)}, u32[]{:S(2)}, u32[]{:S(2)}) collective-permute-start(bf16[32,2048]{1,0:T(8,128)(2,1)S(1)} %get-tuple-element.19.refs_4_), channel_id=1, source_target_pairs={{0,4},{2,6},{4,0},{6,2},{1,5},{3,7},{5,1},{7,3},{8,12},{10,14},{12... | collective-permute-start | bytes 393224 | tf_op jit(solution)/shard_map/ppermute | solution.py:170
  21.7 9.6 %collective-permute-start.7 = (bf16[32,2048]{1,0:T(8,128)(2,1)S(1)}, bf16[32,2048]{1,0:T(8,128)(2,1)S(1)}, u32[]{:S(2)}, u32[]{:S(2)}) collective-permute-start(bf16[32,2048]{1,0:T(8,128)(2,1)S(1)} %get-tuple-element.20), channel_id=1, source_target_pairs={{0,2},{2,0},{4,6},{6,4},{1,3},{3,1},{5,7},{7,5},{8,10},{10,8},{12,... | collective-permute-start | bytes 393224 | tf_op jit(solution)/shard_map/ppermute | solution.py:170
  23.3 7.4 %collective-permute-start.10 = (bf16[32,2048]{1,0:T(8,128)(2,1)S(1)}, bf16[32,2048]{1,0:T(8,128)(2,1)S(1)}, u32[]{:S(2)}, u32[]{:S(2)}) collective-permute-start(bf16[32,2048]{1,0:T(8,128)(2,1)S(1)} %get-tuple-element.24), channel_id=1, source_target_pairs={{0,6},{2,4},{4,2},{6,0},{1,7},{3,5},{5,3},{7,1},{8,14},{10,12},{12... | collective-permute-start | bytes 393224 | tf_op jit(solution)/shard_map/ppermute | solution.py:170
  25.8 6.3 %collective-permute-start.9 = (bf16[32,2048]{1,0:T(8,128)(2,1)S(1)}, bf16[32,2048]{1,0:T(8,128)(2,1)S(1)}, u32[]{:S(2)}, u32[]{:S(2)}) collective-permute-start(bf16[32,2048]{1,0:T(8,128)(2,1)S(1)} %get-tuple-element.23.refs_8_), channel_id=1, source_target_pairs={{0,4},{2,6},{4,0},{6,2},{1,5},{3,7},{5,1},{7,3},{8,12},{10,14},{12... | collective-permute-start | bytes 393224 | tf_op jit(solution)/shard_map/ppermute | solution.py:170

commit v3 on v2

--- a/solution.py
+++ b/solution.py
@@ -149,7 +149,7 @@
             out_specs=[vmem] * len(slots),
             compiler_params=params,
             cost_estimate=pl.CostEstimate(
-                flops=16 * part * width * rows * shards * len(slots),
+                flops=6 * part * width * rows * shards * len(slots),
                 bytes_accessed=4 * part * width * len(slots),
                 transcendentals=rows * shards * part * width // HD * len(slots),
             ),
@@ -166,7 +166,7 @@
             last = [pieces[-1]]
             for (d, _), piece in zip(slots, pieces):
                 if g and d == 2:
-                    piece = after(piece, arrived[1, g - 1])
+                    piece = after(piece, arrived[3, g - 1])
                 arrived[d, g] = lax.ppermute(piece, "head", [(h, h ^ d) for h in range(heads)])
     slots = [(0, g) for g in range(groups)]
     for slot, piece in zip(slots, attend(slots, *last)):

time: 33 us -> 33 us (level)
  waiting for transfers between devices: 10.5 us -> 5.95 us
  starting transfers between devices: 13.8 us -> 18.3 us
    ppermute x5, waiting for transfers between devices: 5.75 us -> 0.75 us  [handed(): return lax.ppermute(value, ('ctx', 'section'), pairs)]
    ppermute x5, starting transfers between devices: 5.99 us -> 8.72 us  [handed(): return lax.ppermute(value, ('ctx', 'section'), pairs)]
    ppermute x2, starting transfers between devices: 0.91 us -> 2.43 us  [passed(): return lax.ppermute(value, 'ctx', [(c, c ^ step) for c in range(shards)])]
    ppermute x2, waiting for transfers between devices: 0.25 us -> 1.76 us  [passed(): return lax.ppermute(value, 'ctx', [(c, c ^ step) for c in range(shards)])]
    ppermute x6, waiting for transfers between devices: 4.52 us -> 3.44 us  [local(): lax.ppermute(piece, 'head', [(h, h ^ d) for h in range(heads)])]
  transfers between devices with their start and end apart: 13 -> 13, of which waited for: 6 -> 5; matrix products, arithmetic and copies ran while one was open for 3% -> 3% of each run, Pallas kernels for 19% -> 19%
where the time goes in v3:
time: 33 us; the launch traced here: 32.8 us
  starting transfers between devices  18.3 us (55%)
  Pallas kernels  6.88 us (21%)
  waiting for transfers between devices  5.95 us (18%)
  local copies, waits for them, and re-layouts  1.47 us (4%)
    ppermute x5, starting transfers between devices, handed(): return lax.ppermute(value, ('ctx', 'section'), pairs)  8.72 us
    ppermute x6, starting transfers between devices, local(): lax.ppermute(piece, 'head', [(h, h ^ d) for h in range(heads)])  7.17 us
    pallas_call x4, Pallas kernels, attend(): pl.pallas_call(functools.partial(attend_kernel, LOG2E / HD ** 0.5, slots,...  3.96 us
    ppermute x6, waiting for transfers between devices, local(): lax.ppermute(piece, 'head', [(h, h ^ d) for h in range(heads)])  3.44 us
    ppermute x2, starting transfers between devices, passed(): return lax.ppermute(value, 'ctx', [(c, c ^ step) for c in range(shards)])  2.43 us
    pallas_call x3, Pallas kernels, local(): pl.pallas_call(functools.partial(place_kernel, slots, groups), out_shape=...  2.26 us
    ppermute x2, waiting for transfers between devices, passed(): return lax.ppermute(value, 'ctx', [(c, c ^ step) for c in range(shards)])  1.76 us
    squeeze x1, local copies, waits for them, and re-layouts, local(): kv[0, :, g * HD:(g + 1) * HD]  0.82 us
  transfers between devices with their start and end apart: 13, of which 5 were waited for; matrix products, arithmetic and copies ran while one was open for 3% of the time, Pallas kernels for 19%

profile of v3, /device:TPU:0, one launch (start us, length us, event | category | flops | bytes accessed | tf_op | source)
XLA Modules:
  0.0 32.8 jit_solution(6837316185744893563)
XLA Ops:
  0.0 0.5 %collective-permute-start = (bf16[1,128,4096]{2,1,0:T(8,128)(2,1)}, bf16[1,128,4096]{2,1,0:T(8,128)(2,1)S(1)}, u32[]{:S(2)}, u32[]{:S(2)}) collective-permute-start(bf16[1,128,4096]{2,1,0:T(8,128)(2,1)} %param.5), channel_id=1, source_target_pairs={{0,1},{1,0},{8,9},{9,8},{16,17},{17,16},{24,25},{25,24},{2,3},{3,2... | collective-permute-start | bytes 3145736 | tf_op jit(solution)/shard_map/ppermute | solution.py:107
  0.5 0.8 %slice_bitcast_fusion.2 = (bf16[128,128]{1,0:T(8,128)(2,1)S(1)}, bf16[128,128]{1,0:T(8,128)(2,1)S(1)}, bf16[128,128]{1,0:T(8,128)(2,1)S(1)}, bf16[128,128]{1,0:T(8,128)(2,1)S(1)}) fusion(bf16[1,128,256]{2,1,0:T(8,128)(2,1)} %param.7, bf16[1,128,256]{2,1,0:T(8,128)(2,1)} %param.6), kind=kLoop, calls=%fused_computation.5 | loop fusion | bytes 262144 | tf_op jit(solution)/shard_map/squeeze | solution.py:126
  1.3 3.8 %collective-permute-start.5 = (bf16[128,256]{1,0:T(8,128)(2,1)S(1)}, bf16[128,256]{1,0:T(8,128)(2,1)S(1)}, u32[]{:S(2)}, u32[]{:S(2)}) collective-permute-start(bf16[128,256]{1,0:T(8,128)(2,1)S(1)} %get-tuple-element.27), channel_id=1, source_target_pairs={{0,17},{1,16},{8,25},{9,24},{16,1},{17,0},{24,9},{25,8},{2,19},{3,... | collective-permute-start | bytes 196616 | tf_op jit(solution)/shard_map/ppermute | solution.py:107
  5.1 0.0 copy-start
  5.1 0.0 copy-start.1
  5.1 0.6 %copy-done = s32[512]{0:T(512)S(1)} copy-done((s32[512]{0:T(512)S(1)}, s32[512]{0:T(512)}, u32[]{:S(2)}) %copy-start) | copy-done | bytes 2072
  5.8 0.0 copy-done.1
  5.8 0.7 %bias.1 = f32[128,512]{1,0:T(8,128)S(1)} custom-call(s32[16]{0:T(128)S(1)} %copy-done.1, s32[4,128]{1,0:T(4,128)S(1)} %bitcast.13), custom_call_target="tpu_custom_call" | custom-call | tf_op jit(solution)/shard_map/bias/pallas_call | solution.py:116
  6.4 1.2 %collective-permute-start.2 = (bf16[2,128,256]{2,1,0:T(8,128)(2,1)S(1)}, bf16[2,128,256]{2,1,0:T(8,128)(2,1)S(1)}, u32[]{:S(2)}, u32[]{:S(2)}) collective-permute-start(bf16[2,128,256]{2,1,0:T(8,128)(2,1)S(1)} %pad_maximum_fusion), channel_id=1, source_target_pairs={{0,9},{1,8},{8,1},{9,0},{16,25},{17,24},{24,17},{25,16},{2,11},{3,... | collective-permute-start | bytes 393224 | tf_op jit(solution)/shard_map/ppermute | solution.py:107
  7.7 0.5 %collective-permute-start.1 = (bf16[2,128,256]{2,1,0:T(8,128)(2,1)S(1)}, bf16[2,128,256]{2,1,0:T(8,128)(2,1)S(1)}, u32[]{:S(2)}, u32[]{:S(2)}) collective-permute-start(bf16[2,128,256]{2,1,0:T(8,128)(2,1)S(1)} %pad_maximum_fusion), channel_id=1, source_target_pairs={{0,1},{1,0},{8,9},{9,8},{16,17},{17,16},{24,25},{25,24},{2,3},{3,2... | collective-permute-start | bytes 393224 | tf_op jit(solution)/shard_map/ppermute | solution.py:107
  8.2 0.7 %collective-permute-done.5.refs_2_ = bf16[128,256]{1,0:T(8,128)(2,1)S(1)} collective-permute-done((bf16[128,256]{1,0:T(8,128)(2,1)S(1)}, bf16[128,256]{1,0:T(8,128)(2,1)S(1)}, u32[]{:S(2)}, u32[]{:S(2)}) %collective-permute-start.5) | collective-permute-done | bytes 65568 | tf_op jit(solution)/shard_map/ppermute | solution.py:107
  8.9 0.9 %collective-permute-start.6 = (bf16[128,256]{1,0:T(8,128)(2,1)S(1)}, bf16[128,256]{1,0:T(8,128)(2,1)S(1)}, u32[]{:S(2)}, u32[]{:S(2)}) collective-permute-start(bf16[128,256]{1,0:T(8,128)(2,1)S(1)} %collective-permute-done.5.refs_2_), channel_id=1, source_target_pairs={{0,8},{8,0},{16,24},{24,16},{1,9},{9,1},{17,25},{25,17},{2,10},{10... | collective-permute-start | bytes 196616 | tf_op jit(solution)/shard_map/ppermute | solution.py:110
  9.8 2.7 %collective-permute-start.3 = (bf16[128,256]{1,0:T(8,128)(2,1)S(1)}, bf16[128,256]{1,0:T(8,128)(2,1)S(1)}, u32[]{:S(2)}, u32[]{:S(2)}) collective-permute-start(bf16[128,256]{1,0:T(8,128)(2,1)S(1)} %get-tuple-element.29), channel_id=1, source_target_pairs={{0,17},{1,16},{8,25},{9,24},{16,1},{17,0},{24,9},{25,8},{2,19},{3,... | collective-permute-start | bytes 196616 | tf_op jit(solution)/shard_map/ppermute | solution.py:107
  12.5 1.2 %collective-permute-done.6.refs_3_ = bf16[128,256]{1,0:T(8,128)(2,1)S(1)} collective-permute-done((bf16[128,256]{1,0:T(8,128)(2,1)S(1)}, bf16[128,256]{1,0:T(8,128)(2,1)S(1)}, u32[]{:S(2)}, u32[]{:S(2)}) %collective-permute-start.6) | collective-permute-done | bytes 65568 | tf_op jit(solution)/shard_map/ppermute | solution.py:110
  13.7 0.0 collective-permute-done.2.refs_1_.refs_5_
  13.7 0.0 collective-permute-done.1.refs_0_.refs_4_
  13.7 0.0 collective-permute-done.q
  13.7 0.7 %attend.4.refs_4_ = bf16[32,2048]{1,0:T(8,128)(2,1)S(1)} custom-call(bf16[1,128,4096]{2,1,0:T(8,128)(2,1)S(1)} %collective-permute-done.q, f32[128,512]{1,0:T(8,128)S(1)} %bias.1, bf16[2,128,256]{2,1,0:T(8,128)(2,1)S(1)} %collective-permute-done.1.refs_0_.refs_4_, bf16[2,128,256]{2,1,0:T(8,128)(2,1)S(1)} %collective-permute-done.2.refs_1_.refs_5_, ...), custom_call_target="tpu_custom_call" | custom-call | flops 201326592 | bytes 262144 | tf_op jit(solution)/shard_map/attend/pallas_call | solution.py:145
  14.4 2.5 %collective-permute-start.8 = (bf16[32,2048]{1,0:T(8,128)(2,1)S(1)}, bf16[32,2048]{1,0:T(8,128)(2,1)S(1)}, u32[]{:S(2)}, u32[]{:S(2)}) collective-permute-start(bf16[32,2048]{1,0:T(8,128)(2,1)S(1)} %attend.4.refs_4_), channel_id=1, source_target_pairs={{0,6},{2,4},{4,2},{6,0},{1,7},{3,5},{5,3},{7,1},{8,14},{10,12},{12... | collective-permute-start | bytes 393224 | tf_op jit(solution)/shard_map/ppermute | solution.py:170
  16.9 0.0 collective-permute-done.3.refs_2_.refs_6_
  16.9 1.6 %collective-permute-start.4 = (bf16[128,256]{1,0:T(8,128)(2,1)S(1)}, bf16[128,256]{1,0:T(8,128)(2,1)S(1)}, u32[]{:S(2)}, u32[]{:S(2)}) collective-permute-start(bf16[128,256]{1,0:T(8,128)(2,1)S(1)} %collective-permute-done.3.refs_2_.refs_6_), channel_id=1, source_target_pairs={{0,8},{8,0},{16,24},{24,16},{1,9},{9,1},{17,25},{25,17},{2,10},{10... | collective-permute-start | bytes 196616 | tf_op jit(solution)/shard_map/ppermute | solution.py:110
  18.5 1.0 %attend.5 = (bf16[32,2048]{1,0:T(8,128)(2,1)S(1)}, bf16[32,2048]{1,0:T(8,128)(2,1)S(1)}) custom-call(bf16[1,128,4096]{2,1,0:T(8,128)(2,1)S(1)} %collective-permute-done.q, f32[128,512]{1,0:T(8,128)S(1)} %bias.1, bf16[2,128,256]{2,1,0:T(8,128)(2,1)S(1)} %collective-permute-done.1.refs_0_.refs_4_, ...), custom_call_target="tpu_custom_call" | custom-call | flops 402653184 | bytes 524288 | tf_op jit(solution)/shard_map/attend/pallas_call | solution.py:145
  19.5 0.6 %collective-permute-start.11 = (bf16[32,2048]{1,0:T(8,128)(2,1)S(1)}, bf16[32,2048]{1,0:T(8,128)(2,1)S(1)}, u32[]{:S(2)}, u32[]{:S(2)}) collective-permute-start(bf16[32,2048]{1,0:T(8,128)(2,1)S(1)} %get-tuple-element.24), channel_id=1, source_target_pairs={{0,2},{2,0},{4,6},{6,4},{1,3},{3,1},{5,7},{7,5},{8,10},{10,8},{12,... | collective-permute-start | bytes 393224 | tf_op jit(solution)/shard_map/ppermute | solution.py:170
  20.1 0.5 %collective-permute-start.12 = (bf16[32,2048]{1,0:T(8,128)(2,1)S(1)}, bf16[32,2048]{1,0:T(8,128)(2,1)S(1)}, u32[]{:S(2)}, u32[]{:S(2)}) collective-permute-start(bf16[32,2048]{1,0:T(8,128)(2,1)S(1)} %get-tuple-element.19.refs_4_), channel_id=1, source_target_pairs={{0,4},{2,6},{4,0},{6,2},{1,5},{3,7},{5,1},{7,3},{8,12},{10,14},{12... | collective-permute-start | bytes 393224 | tf_op jit(solution)/shard_map/ppermute | solution.py:170
  20.6 0.6 %collective-permute-done.4.refs_3_.refs_7_ = bf16[128,256]{1,0:T(8,128)(2,1)S(1)} collective-permute-done((bf16[128,256]{1,0:T(8,128)(2,1)S(1)}, bf16[128,256]{1,0:T(8,128)(2,1)S(1)}, u32[]{:S(2)}, u32[]{:S(2)}) %collective-permute-start.4) | collective-permute-done | bytes 65568 | tf_op jit(solution)/shard_map/ppermute | solution.py:110
  21.2 1.3 %attend.6 = (bf16[32,2048]{1,0:T(8,128)(2,1)S(1)}, bf16[32,2048]{1,0:T(8,128)(2,1)S(1)}, bf16[32,2048]{1,0:T(8,128)(2,1)S(1)}) custom-call(bf16[1,128,4096]{2,1,0:T(8,128)(2,1)S(1)} %collective-permute-done.q, f32[128,512]{1,0:T(8,128)S(1)} %bias.1, bf16[2,128,256]{2,1,0:T(8,128)(2,1)S(1)} %collective-permute-done.1.refs_0_.refs_4_, ...), custom_call_target="tpu_custom_call" | custom-call | flops 603979776 | bytes 786432 | tf_op jit(solution)/shard_map/attend/pallas_call | solution.py:145
  22.5 1.0 %collective-permute-start.7 = (bf16[32,2048]{1,0:T(8,128)(2,1)S(1)}, bf16[32,2048]{1,0:T(8,128)(2,1)S(1)}, u32[]{:S(2)}, u32[]{:S(2)}) collective-permute-start(bf16[32,2048]{1,0:T(8,128)(2,1)S(1)} %get-tuple-element.20), channel_id=1, source_target_pairs={{0,2},{2,0},{4,6},{6,4},{1,3},{3,1},{5,7},{7,5},{8,10},{10,8},{12,... | collective-permute-start | bytes 393224 | tf_op jit(solution)/shard_map/ppermute | solution.py:170
  23.5 1.5 %collective-permute-start.10 = (bf16[32,2048]{1,0:T(8,128)(2,1)S(1)}, bf16[32,2048]{1,0:T(8,128)(2,1)S(1)}, u32[]{:S(2)}, u32[]{:S(2)}) collective-permute-start(bf16[32,2048]{1,0:T(8,128)(2,1)S(1)} %get-tuple-element.23), channel_id=1, source_target_pairs={{0,6},{2,4},{4,2},{6,0},{1,7},{3,5},{5,3},{7,1},{8,14},{10,12},{12... | collective-permute-start | bytes 393224 | tf_op jit(solution)/shard_map/ppermute | solution.py:170
  24.9 0.0 collective-permute-done.8.refs_0_
  25.0 1.1 %collective-permute-start.9 = (bf16[32,2048]{1,0:T(8,128)(2,1)S(1)}, bf16[32,2048]{1,0:T(8,128)(2,1)S(1)}, u32[]{:S(2)}, u32[]{:S(2)}) collective-permute-start(bf16[32,2048]{1,0:T(8,128)(2,1)S(1)} %get-tuple-element.22.refs_8_), channel_id=1, source_target_pairs={{0,4},{2,6},{4,0},{6,2},{1,5},{3,7},{5,1},{7,3},{8,12},{10,14},{12... | collective-permute-start | bytes 393224 | tf_op jit(solution)/shard_map/ppermute | solution.py:170
  26.0 1.0 %attend.7 = (bf16[32,2048]{1,0:T(8,128)(2,1)S(1)}, bf16[32,2048]{1,0:T(8,128)(2,1)S(1)}) custom-call(bf16[1,128,4096]{2,1,0:T(8,128)(2,1)S(1)} %collective-permute-done.q, f32[128,512]{1,0:T(8,128)S(1)} %bias.1, bf16[2,128,256]{2,1,0:T(8,128)(2,1)S(1)} %collective-permute-done.1.refs_0_.refs_4_, ...), custom_call_target="tpu_custom_call" | custom-call | flops 402653184 | bytes 524288 | tf_op jit(solution)/shard_map/attend/pallas_call | solution.py:145
  27.0 0.0 collective-permute-done.11.refs_1_
  27.1 0.0 collective-permute-done.12.refs_2_
  27.1 0.9 %place.3.refs_1_ = bf16[1,32,16384]{2,1,0:T(8,128)(2,1)} custom-call(bf16[32,2048]{1,0:T(8,128)(2,1)S(1)} %collective-permute-done.8.refs_0_, bf16[32,2048]{1,0:T(8,128)(2,1)S(1)} %collective-permute-done.11.refs_1_, bf16[32,2048]{1,0:T(8,128)(2,1)S(1)} %collective-permute-done.12.refs_2_, bf16[32,2048]{1,0:T(8,128)(2,1)S(1)} %get-tuple-element.25.refs_3_, ...), custom_call_target="tpu_custom_call" | custom-call | tf_op jit(solution)/shard_map/place/pallas_call | solution.py:179
  28.0 2.8 %collective-permute-done.10.refs_0_ = bf16[32,2048]{1,0:T(8,128)(2,1)S(1)} collective-permute-done((bf16[32,2048]{1,0:T(8,128)(2,1)S(1)}, bf16[32,2048]{1,0:T(8,128)(2,1)S(1)}, u32[]{:S(2)}, u32[]{:S(2)}) %collective-permute-start.10) | collective-permute-done | bytes 131104 | tf_op jit(solution)/shard_map/ppermute | solution.py:170
  30.7 0.7 %place.4.refs_2_ = bf16[1,32,16384]{2,1,0:T(8,128)(2,1)} custom-call(bf16[32,2048]{1,0:T(8,128)(2,1)S(1)} %collective-permute-done.10.refs_0_, bf16[1,32,16384]{2,1,0:T(8,128)(2,1)} %place.3.refs_1_), custom_call_target="tpu_custom_call", output_to_operand_aliasing={{}: (1, {})} | custom-call | tf_op jit(solution)/shard_map/place/pallas_call | solution.py:179
  31.4 0.0 collective-permute-done.7.refs_0_
  31.4 0.7 %collective-permute-done.9.refs_1_ = bf16[32,2048]{1,0:T(8,128)(2,1)S(1)} collective-permute-done((bf16[32,2048]{1,0:T(8,128)(2,1)S(1)}, bf16[32,2048]{1,0:T(8,128)(2,1)S(1)}, u32[]{:S(2)}, u32[]{:S(2)}) %collective-permute-start.9) | collective-permute-done | bytes 131104 | tf_op jit(solution)/shard_map/ppermute | solution.py:170
  32.1 0.7 %place.5 = bf16[1,32,16384]{2,1,0:T(8,128)(2,1)} custom-call(bf16[32,2048]{1,0:T(8,128)(2,1)S(1)} %collective-permute-done.7.refs_0_, bf16[32,2048]{1,0:T(8,128)(2,1)S(1)} %collective-permute-done.9.refs_1_, bf16[1,32,16384]{2,1,0:T(8,128)(2,1)} %place.4.refs_2_), custom_call_target="tpu_custom_call", output_to_operand_aliasing={{}: (2, {})} | custom-call | tf_op jit(solution)/shard_map/place/pallas_call | solution.py:179
  (3 shorter events, 0.0 us)
Async XLA Ops:
  0.0 13.7 %collective-permute-start = (bf16[1,128,4096]{2,1,0:T(8,128)(2,1)}, bf16[1,128,4096]{2,1,0:T(8,128)(2,1)S(1)}, u32[]{:S(2)}, u32[]{:S(2)}) collective-permute-start(bf16[1,128,4096]{2,1,0:T(8,128)(2,1)} %param.5), channel_id=1, source_target_pairs={{0,1},{1,0},{8,9},{9,8},{16,17},{17,16},{24,25},{25,24},{2,3},{3,2... | collective-permute-start | bytes 3145736 | tf_op jit(solution)/shard_map/ppermute | solution.py:107
  1.3 7.6 %collective-permute-start.5 = (bf16[128,256]{1,0:T(8,128)(2,1)S(1)}, bf16[128,256]{1,0:T(8,128)(2,1)S(1)}, u32[]{:S(2)}, u32[]{:S(2)}) collective-permute-start(bf16[128,256]{1,0:T(8,128)(2,1)S(1)} %get-tuple-element.27), channel_id=1, source_target_pairs={{0,17},{1,16},{8,25},{9,24},{16,1},{17,0},{24,9},{25,8},{2,19},{3,... | collective-permute-start | bytes 196616 | tf_op jit(solution)/shard_map/ppermute | solution.py:107
  5.1 0.7 %copy-start = (s32[512]{0:T(512)S(1)}, s32[512]{0:T(512)}, u32[]{:S(2)}) copy-start(s32[512]{0:T(512)} %param.8) | copy-start | bytes 6148
  5.1 0.7 %copy-start.1 = (s32[16]{0:T(128)S(1)}, s32[16]{0:T(128)}, u32[]{:S(2)}) copy-start(s32[16]{0:T(128)} %lengths.1) | copy-start | bytes 196
  6.4 7.3 %collective-permute-start.2 = (bf16[2,128,256]{2,1,0:T(8,128)(2,1)S(1)}, bf16[2,128,256]{2,1,0:T(8,128)(2,1)S(1)}, u32[]{:S(2)}, u32[]{:S(2)}) collective-permute-start(bf16[2,128,256]{2,1,0:T(8,128)(2,1)S(1)} %pad_maximum_fusion), channel_id=1, source_target_pairs={{0,9},{1,8},{8,1},{9,0},{16,25},{17,24},{24,17},{25,16},{2,11},{3,... | collective-permute-start | bytes 393224 | tf_op jit(solution)/shard_map/ppermute | solution.py:107
  7.7 6.0 %collective-permute-start.1 = (bf16[2,128,256]{2,1,0:T(8,128)(2,1)S(1)}, bf16[2,128,256]{2,1,0:T(8,128)(2,1)S(1)}, u32[]{:S(2)}, u32[]{:S(2)}) collective-permute-start(bf16[2,128,256]{2,1,0:T(8,128)(2,1)S(1)} %pad_maximum_fusion), channel_id=1, source_target_pairs={{0,1},{1,0},{8,9},{9,8},{16,17},{17,16},{24,25},{25,24},{2,3},{3,2... | collective-permute-start | bytes 393224 | tf_op jit(solution)/shard_map/ppermute | solution.py:107
  8.9 4.8 %collective-permute-start.6 = (bf16[128,256]{1,0:T(8,128)(2,1)S(1)}, bf16[128,256]{1,0:T(8,128)(2,1)S(1)}, u32[]{:S(2)}, u32[]{:S(2)}) collective-permute-start(bf16[128,256]{1,0:T(8,128)(2,1)S(1)} %collective-permute-done.5.refs_2_), channel_id=1, source_target_pairs={{0,8},{8,0},{16,24},{24,16},{1,9},{9,1},{17,25},{25,17},{2,10},{10... | collective-permute-start | bytes 196616 | tf_op jit(solution)/shard_map/ppermute | solution.py:110
  9.8 7.2 %collective-permute-start.3 = (bf16[128,256]{1,0:T(8,128)(2,1)S(1)}, bf16[128,256]{1,0:T(8,128)(2,1)S(1)}, u32[]{:S(2)}, u32[]{:S(2)}) collective-permute-start(bf16[128,256]{1,0:T(8,128)(2,1)S(1)} %get-tuple-element.29), channel_id=1, source_target_pairs={{0,17},{1,16},{8,25},{9,24},{16,1},{17,0},{24,9},{25,8},{2,19},{3,... | collective-permute-start | bytes 196616 | tf_op jit(solution)/shard_map/ppermute | solution.py:107
  14.4 10.5 %collective-permute-start.8 = (bf16[32,2048]{1,0:T(8,128)(2,1)S(1)}, bf16[32,2048]{1,0:T(8,128)(2,1)S(1)}, u32[]{:S(2)}, u32[]{:S(2)}) collective-permute-start(bf16[32,2048]{1,0:T(8,128)(2,1)S(1)} %attend.4.refs_4_), channel_id=1, source_target_pairs={{0,6},{2,4},{4,2},{6,0},{1,7},{3,5},{5,3},{7,1},{8,14},{10,12},{12... | collective-permute-start | bytes 393224 | tf_op jit(solution)/shard_map/ppermute | solution.py:170
  16.9 4.3 %collective-permute-start.4 = (bf16[128,256]{1,0:T(8,128)(2,1)S(1)}, bf16[128,256]{1,0:T(8,128)(2,1)S(1)}, u32[]{:S(2)}, u32[]{:S(2)}) collective-permute-start(bf16[128,256]{1,0:T(8,128)(2,1)S(1)} %collective-permute-done.3.refs_2_.refs_6_), channel_id=1, source_target_pairs={{0,8},{8,0},{16,24},{24,16},{1,9},{9,1},{17,25},{25,17},{2,10},{10... | collective-permute-start | bytes 196616 | tf_op jit(solution)/shard_map/ppermute | solution.py:110
  19.5 7.5 %collective-permute-start.11 = (bf16[32,2048]{1,0:T(8,128)(2,1)S(1)}, bf16[32,2048]{1,0:T(8,128)(2,1)S(1)}, u32[]{:S(2)}, u32[]{:S(2)}) collective-permute-start(bf16[32,2048]{1,0:T(8,128)(2,1)S(1)} %get-tuple-element.24), channel_id=1, source_target_pairs={{0,2},{2,0},{4,6},{6,4},{1,3},{3,1},{5,7},{7,5},{8,10},{10,8},{12,... | collective-permute-start | bytes 393224 | tf_op jit(solution)/shard_map/ppermute | solution.py:170
  20.1 6.9 %collective-permute-start.12 = (bf16[32,2048]{1,0:T(8,128)(2,1)S(1)}, bf16[32,2048]{1,0:T(8,128)(2,1)S(1)}, u32[]{:S(2)}, u32[]{:S(2)}) collective-permute-start(bf16[32,2048]{1,0:T(8,128)(2,1)S(1)} %get-tuple-element.19.refs_4_), channel_id=1, source_target_pairs={{0,4},{2,6},{4,0},{6,2},{1,5},{3,7},{5,1},{7,3},{8,12},{10,14},{12... | collective-permute-start | bytes 393224 | tf_op jit(solution)/shard_map/ppermute | solution.py:170
  22.5 8.9 %collective-permute-start.7 = (bf16[32,2048]{1,0:T(8,128)(2,1)S(1)}, bf16[32,2048]{1,0:T(8,128)(2,1)S(1)}, u32[]{:S(2)}, u32[]{:S(2)}) collective-permute-start(bf16[32,2048]{1,0:T(8,128)(2,1)S(1)} %get-tuple-element.20), channel_id=1, source_target_pairs={{0,2},{2,0},{4,6},{6,4},{1,3},{3,1},{5,7},{7,5},{8,10},{10,8},{12,... | collective-permute-start | bytes 393224 | tf_op jit(solution)/shard_map/ppermute | solution.py:170
  23.5 7.3 %collective-permute-start.10 = (bf16[32,2048]{1,0:T(8,128)(2,1)S(1)}, bf16[32,2048]{1,0:T(8,128)(2,1)S(1)}, u32[]{:S(2)}, u32[]{:S(2)}) collective-permute-start(bf16[32,2048]{1,0:T(8,128)(2,1)S(1)} %get-tuple-element.23), channel_id=1, source_target_pairs={{0,6},{2,4},{4,2},{6,0},{1,7},{3,5},{5,3},{7,1},{8,14},{10,12},{12... | collective-permute-start | bytes 393224 | tf_op jit(solution)/shard_map/ppermute | solution.py:170
  25.0 7.1 %collective-permute-start.9 = (bf16[32,2048]{1,0:T(8,128)(2,1)S(1)}, bf16[32,2048]{1,0:T(8,128)(2,1)S(1)}, u32[]{:S(2)}, u32[]{:S(2)}) collective-permute-start(bf16[32,2048]{1,0:T(8,128)(2,1)S(1)} %get-tuple-element.22.refs_8_), channel_id=1, source_target_pairs={{0,4},{2,6},{4,0},{6,2},{1,5},{3,7},{5,1},{7,3},{8,12},{10,14},{12... | collective-permute-start | bytes 393224 | tf_op jit(solution)/shard_map/ppermute | solution.py:170

commit v4 on v1

--- a/solution.py
+++ b/solution.py
@@ -134,7 +134,7 @@
         step //= 2
         for other in sorted(blocks):
             blocks[other ^ step] = [passed(after(block, bias), step) for block in blocks[other]]
-        blocks[step] = [handed(after(stacked, bias), step)]
+        blocks[step] = [handed(stacked, step)]
     kvs = [
         [own] + [blocks[step][g % len(blocks[step])] for step in range(1, shards)]
         for g in range(groups)

time: 31.6 us -> 31.6 us (level)
  starting transfers between devices: 18.3 us -> 19.5 us
  local copies, waits for them, and re-layouts: 1.47 us -> 0.83 us
  waiting for transfers between devices: 4.62 us -> 4.04 us
    ppermute x2, waiting for transfers between devices: 1.76 us -> 0.3 us  [passed(): return lax.ppermute(value, 'ctx', [(c, c ^ step) for c in range(shards)])]
    ppermute x6, starting transfers between devices: 7.17 us -> 8.12 us  [local(): lax.ppermute(piece, 'head', [(h, h ^ d) for h in range(heads)])]
    ppermute x6, waiting for transfers between devices: 2.11 us -> 2.78 us  [local(): lax.ppermute(piece, 'head', [(h, h ^ d) for h in range(heads)])]
    unnamed x4, local copies, waits for them, and re-layouts: 0.65 us -> 0.01 us
  transfers between devices with their start and end apart: 13 -> 13, of which waited for: 6 -> 4; matrix products, arithmetic and copies ran while one was open for 3% -> 3% of each run, Pallas kernels for 20% -> 20%
where the time goes in v4:
time: 31.6 us; the launch traced here: 31.4 us
  starting transfers between devices  19.5 us (62%)
  Pallas kernels  6.92 us (22%)
  waiting for transfers between devices  4.04 us (13%)
  local copies, waits for them, and re-layouts  0.83 us (3%)
    ppermute x5, starting transfers between devices, handed(): return lax.ppermute(value, ('ctx', 'section'), pairs)  8.78 us
    ppermute x6, starting transfers between devices, local(): lax.ppermute(piece, 'head', [(h, h ^ d) for h in range(heads)])  8.12 us
    pallas_call x4, Pallas kernels, attend(): pl.pallas_call(functools.partial(attend_kernel, LOG2E / HD ** 0.5, slots,...  4 us
    ppermute x6, waiting for transfers between devices, local(): lax.ppermute(piece, 'head', [(h, h ^ d) for h in range(heads)])  2.78 us
    ppermute x2, starting transfers between devices, passed(): return lax.ppermute(value, 'ctx', [(c, c ^ step) for c in range(shards)])  2.57 us
    pallas_call x3, Pallas kernels, local(): pl.pallas_call(functools.partial(place_kernel, slots, groups), out_shape=...  2.26 us
    ppermute x5, waiting for transfers between devices, handed(): return lax.ppermute(value, ('ctx', 'section'), pairs)  0.96 us
    squeeze x1, local copies, waits for them, and re-layouts, local(): kv[0, :, g * HD:(g + 1) * HD]  0.82 us
  transfers between devices with their start and end apart: 13, of which 4 were waited for; matrix products, arithmetic and copies ran while one was open for 3% of the time, Pallas kernels for 20%

profile of v4, /device:TPU:0, one launch (start us, length us, event | category | flops | bytes accessed | tf_op | source)
XLA Modules:
  0.0 31.4 jit_solution(2272087852538679729)
XLA Ops:
  0.0 0.5 %collective-permute-start = (bf16[1,128,4096]{2,1,0:T(8,128)(2,1)}, bf16[1,128,4096]{2,1,0:T(8,128)(2,1)S(1)}, u32[]{:S(2)}, u32[]{:S(2)}) collective-permute-start(bf16[1,128,4096]{2,1,0:T(8,128)(2,1)} %param.5), channel_id=1, source_target_pairs={{0,1},{1,0},{8,9},{9,8},{16,17},{17,16},{24,25},{25,24},{2,3},{3,2... | collective-permute-start | bytes 3145736 | tf_op jit(solution)/shard_map/ppermute | solution.py:107
  0.5 0.8 %slice_bitcast_fusion.2 = (bf16[128,128]{1,0:T(8,128)(2,1)S(1)}, bf16[128,128]{1,0:T(8,128)(2,1)S(1)}, bf16[128,128]{1,0:T(8,128)(2,1)S(1)}, bf16[128,128]{1,0:T(8,128)(2,1)S(1)}) fusion(bf16[1,128,256]{2,1,0:T(8,128)(2,1)} %param.7, bf16[1,128,256]{2,1,0:T(8,128)(2,1)} %param.6), kind=kLoop, calls=%fused_computation.5 | loop fusion | bytes 262144 | tf_op jit(solution)/shard_map/squeeze | solution.py:126
  1.3 3.8 %collective-permute-start.5 = (bf16[128,256]{1,0:T(8,128)(2,1)S(1)}, bf16[128,256]{1,0:T(8,128)(2,1)S(1)}, u32[]{:S(2)}, u32[]{:S(2)}) collective-permute-start(bf16[128,256]{1,0:T(8,128)(2,1)S(1)} %get-tuple-element.25), channel_id=1, source_target_pairs={{0,17},{1,16},{8,25},{9,24},{16,1},{17,0},{24,9},{25,8},{2,19},{3,... | collective-permute-start | bytes 196616 | tf_op jit(solution)/shard_map/ppermute | solution.py:107
  5.1 0.0 copy-start
  5.1 0.0 copy-start.1
  5.1 1.2 %collective-permute-start.2 = (bf16[2,128,256]{2,1,0:T(8,128)(2,1)S(1)}, bf16[2,128,256]{2,1,0:T(8,128)(2,1)S(1)}, u32[]{:S(2)}, u32[]{:S(2)}) collective-permute-start(bf16[2,128,256]{2,1,0:T(8,128)(2,1)S(1)} %pad_maximum_fusion), channel_id=1, source_target_pairs={{0,9},{1,8},{8,1},{9,0},{16,25},{17,24},{24,17},{25,16},{2,11},{3,... | collective-permute-start | bytes 393224 | tf_op jit(solution)/shard_map/ppermute | solution.py:107
  6.4 0.0 copy-done
  6.4 0.0 copy-done.1
  6.4 0.7 %bias.1 = f32[128,512]{1,0:T(8,128)S(1)} custom-call(s32[16]{0:T(128)S(1)} %copy-done.1, s32[4,128]{1,0:T(4,128)S(1)} %bitcast.13), custom_call_target="tpu_custom_call" | custom-call | tf_op jit(solution)/shard_map/bias/pallas_call | solution.py:116
  7.0 0.6 %collective-permute-start.1 = (bf16[2,128,256]{2,1,0:T(8,128)(2,1)S(1)}, bf16[2,128,256]{2,1,0:T(8,128)(2,1)S(1)}, u32[]{:S(2)}, u32[]{:S(2)}) collective-permute-start(bf16[2,128,256]{2,1,0:T(8,128)(2,1)S(1)} %pad_maximum_fusion), channel_id=1, source_target_pairs={{0,1},{1,0},{8,9},{9,8},{16,17},{17,16},{24,25},{25,24},{2,3},{3,2... | collective-permute-start | bytes 393224 | tf_op jit(solution)/shard_map/ppermute | solution.py:107
  7.6 0.9 %collective-permute-done.5.refs_2_ = bf16[128,256]{1,0:T(8,128)(2,1)S(1)} collective-permute-done((bf16[128,256]{1,0:T(8,128)(2,1)S(1)}, bf16[128,256]{1,0:T(8,128)(2,1)S(1)}, u32[]{:S(2)}, u32[]{:S(2)}) %collective-permute-start.5) | collective-permute-done | bytes 65568 | tf_op jit(solution)/shard_map/ppermute | solution.py:107
  8.6 1.2 %collective-permute-start.6 = (bf16[128,256]{1,0:T(8,128)(2,1)S(1)}, bf16[128,256]{1,0:T(8,128)(2,1)S(1)}, u32[]{:S(2)}, u32[]{:S(2)}) collective-permute-start(bf16[128,256]{1,0:T(8,128)(2,1)S(1)} %collective-permute-done.5.refs_2_), channel_id=1, source_target_pairs={{0,8},{8,0},{16,24},{24,16},{1,9},{9,1},{17,25},{25,17},{2,10},{10... | collective-permute-start | bytes 196616 | tf_op jit(solution)/shard_map/ppermute | solution.py:110
  9.8 2.7 %collective-permute-start.3 = (bf16[128,256]{1,0:T(8,128)(2,1)S(1)}, bf16[128,256]{1,0:T(8,128)(2,1)S(1)}, u32[]{:S(2)}, u32[]{:S(2)}) collective-permute-start(bf16[128,256]{1,0:T(8,128)(2,1)S(1)} %get-tuple-element.27), channel_id=1, source_target_pairs={{0,17},{1,16},{8,25},{9,24},{16,1},{17,0},{24,9},{25,8},{2,19},{3,... | collective-permute-start | bytes 196616 | tf_op jit(solution)/shard_map/ppermute | solution.py:107
  12.5 0.0 collective-permute-done.2.refs_1_.refs_5_
  12.5 0.3 collective-permute-done.6.refs_3_
  12.8 0.0 collective-permute-done.1.refs_0_.refs_4_
  12.8 0.0 collective-permute-done.q
  12.8 0.7 %attend.4.refs_4_ = bf16[32,2048]{1,0:T(8,128)(2,1)S(1)} custom-call(bf16[1,128,4096]{2,1,0:T(8,128)(2,1)S(1)} %collective-permute-done.q, f32[128,512]{1,0:T(8,128)S(1)} %bias.1, bf16[2,128,256]{2,1,0:T(8,128)(2,1)S(1)} %collective-permute-done.1.refs_0_.refs_4_, bf16[2,128,256]{2,1,0:T(8,128)(2,1)S(1)} %collective-permute-done.2.refs_1_.refs_5_, ...), custom_call_target="tpu_custom_call" | custom-call | flops 134217728 | bytes 262144 | tf_op jit(solution)/shard_map/attend/pallas_call | solution.py:145
  13.5 2.4 %collective-permute-start.7 = (bf16[32,2048]{1,0:T(8,128)(2,1)S(1)}, bf16[32,2048]{1,0:T(8,128)(2,1)S(1)}, u32[]{:S(2)}, u32[]{:S(2)}) collective-permute-start(bf16[32,2048]{1,0:T(8,128)(2,1)S(1)} %attend.4.refs_4_), channel_id=1, source_target_pairs={{0,6},{2,4},{4,2},{6,0},{1,7},{3,5},{5,3},{7,1},{8,14},{10,12},{12... | collective-permute-start | bytes 393224 | tf_op jit(solution)/shard_map/ppermute | solution.py:170
  15.9 0.0 collective-permute-done.3.refs_2_.refs_6_
  15.9 1.4 %collective-permute-start.4 = (bf16[128,256]{1,0:T(8,128)(2,1)S(1)}, bf16[128,256]{1,0:T(8,128)(2,1)S(1)}, u32[]{:S(2)}, u32[]{:S(2)}) collective-permute-start(bf16[128,256]{1,0:T(8,128)(2,1)S(1)} %collective-permute-done.3.refs_2_.refs_6_), channel_id=1, source_target_pairs={{0,8},{8,0},{16,24},{24,16},{1,9},{9,1},{17,25},{25,17},{2,10},{10... | collective-permute-start | bytes 196616 | tf_op jit(solution)/shard_map/ppermute | solution.py:110
  17.3 1.0 %attend.5 = (bf16[32,2048]{1,0:T(8,128)(2,1)S(1)}, bf16[32,2048]{1,0:T(8,128)(2,1)S(1)}) custom-call(bf16[1,128,4096]{2,1,0:T(8,128)(2,1)S(1)} %collective-permute-done.q, f32[128,512]{1,0:T(8,128)S(1)} %bias.1, bf16[2,128,256]{2,1,0:T(8,128)(2,1)S(1)} %collective-permute-done.1.refs_0_.refs_4_, ...), custom_call_target="tpu_custom_call" | custom-call | flops 268435456 | bytes 524288 | tf_op jit(solution)/shard_map/attend/pallas_call | solution.py:145
  18.3 0.7 %collective-permute-start.11 = (bf16[32,2048]{1,0:T(8,128)(2,1)S(1)}, bf16[32,2048]{1,0:T(8,128)(2,1)S(1)}, u32[]{:S(2)}, u32[]{:S(2)}) collective-permute-start(bf16[32,2048]{1,0:T(8,128)(2,1)S(1)} %get-tuple-element.22), channel_id=1, source_target_pairs={{0,2},{2,0},{4,6},{6,4},{1,3},{3,1},{5,7},{7,5},{8,10},{10,8},{12,... | collective-permute-start | bytes 393224 | tf_op jit(solution)/shard_map/ppermute | solution.py:170
  19.0 1.5 %collective-permute-start.12 = (bf16[32,2048]{1,0:T(8,128)(2,1)S(1)}, bf16[32,2048]{1,0:T(8,128)(2,1)S(1)}, u32[]{:S(2)}, u32[]{:S(2)}) collective-permute-start(bf16[32,2048]{1,0:T(8,128)(2,1)S(1)} %get-tuple-element.18.refs_4_), channel_id=1, source_target_pairs={{0,4},{2,6},{4,0},{6,2},{1,5},{3,7},{5,1},{7,3},{8,12},{10,14},{12... | collective-permute-start | bytes 393224 | tf_op jit(solution)/shard_map/ppermute | solution.py:170
  20.5 0.0 collective-permute-done.4.refs_3_.refs_7_
  20.5 0.0 collective-permute-done.7.refs_5_.refs_0_
  20.5 1.3 %attend.6 = (bf16[32,2048]{1,0:T(8,128)(2,1)S(1)}, bf16[32,2048]{1,0:T(8,128)(2,1)S(1)}, bf16[32,2048]{1,0:T(8,128)(2,1)S(1)}) custom-call(bf16[1,128,4096]{2,1,0:T(8,128)(2,1)S(1)} %collective-permute-done.q, f32[128,512]{1,0:T(8,128)S(1)} %bias.1, bf16[2,128,256]{2,1,0:T(8,128)(2,1)S(1)} %collective-permute-done.1.refs_0_.refs_4_, ...), custom_call_target="tpu_custom_call" | custom-call | flops 402653184 | bytes 786432 | tf_op jit(solution)/shard_map/attend/pallas_call | solution.py:145
  21.8 2.5 %collective-permute-start.10 = (bf16[32,2048]{1,0:T(8,128)(2,1)S(1)}, bf16[32,2048]{1,0:T(8,128)(2,1)S(1)}, u32[]{:S(2)}, u32[]{:S(2)}) collective-permute-start(bf16[32,2048]{1,0:T(8,128)(2,1)S(1)} %get-tuple-element.21), channel_id=1, source_target_pairs={{0,6},{2,4},{4,2},{6,0},{1,7},{3,5},{5,3},{7,1},{8,14},{10,12},{12... | collective-permute-start | bytes 393224 | tf_op jit(solution)/shard_map/ppermute | solution.py:170
  24.3 0.6 %collective-permute-start.8 = (bf16[32,2048]{1,0:T(8,128)(2,1)S(1)}, bf16[32,2048]{1,0:T(8,128)(2,1)S(1)}, u32[]{:S(2)}, u32[]{:S(2)}) collective-permute-start(bf16[32,2048]{1,0:T(8,128)(2,1)S(1)} %get-tuple-element.19), channel_id=1, source_target_pairs={{0,2},{2,0},{4,6},{6,4},{1,3},{3,1},{5,7},{7,5},{8,10},{10,8},{12,... | collective-permute-start | bytes 393224 | tf_op jit(solution)/shard_map/ppermute | solution.py:170
  24.9 0.5 %collective-permute-start.9 = (bf16[32,2048]{1,0:T(8,128)(2,1)S(1)}, bf16[32,2048]{1,0:T(8,128)(2,1)S(1)}, u32[]{:S(2)}, u32[]{:S(2)}) collective-permute-start(bf16[32,2048]{1,0:T(8,128)(2,1)S(1)} %get-tuple-element.20.refs_8_), channel_id=1, source_target_pairs={{0,4},{2,6},{4,0},{6,2},{1,5},{3,7},{5,1},{7,3},{8,12},{10,14},{12... | collective-permute-start | bytes 393224 | tf_op jit(solution)/shard_map/ppermute | solution.py:170
  25.3 1.0 %attend.7 = (bf16[32,2048]{1,0:T(8,128)(2,1)S(1)}, bf16[32,2048]{1,0:T(8,128)(2,1)S(1)}) custom-call(bf16[1,128,4096]{2,1,0:T(8,128)(2,1)S(1)} %collective-permute-done.q, f32[128,512]{1,0:T(8,128)S(1)} %bias.1, bf16[2,128,256]{2,1,0:T(8,128)(2,1)S(1)} %collective-permute-done.1.refs_0_.refs_4_, ...), custom_call_target="tpu_custom_call" | custom-call | flops 268435456 | bytes 524288 | tf_op jit(solution)/shard_map/attend/pallas_call | solution.py:145
  26.3 0.0 collective-permute-done.11.refs_1_
  26.3 0.0 collective-permute-done.12.refs_2_
  26.4 0.9 %place.3.refs_1_ = bf16[1,32,16384]{2,1,0:T(8,128)(2,1)} custom-call(bf16[32,2048]{1,0:T(8,128)(2,1)S(1)} %collective-permute-done.7.refs_5_.refs_0_, bf16[32,2048]{1,0:T(8,128)(2,1)S(1)} %collective-permute-done.11.refs_1_, bf16[32,2048]{1,0:T(8,128)(2,1)S(1)} %collective-permute-done.12.refs_2_, bf16[32,2048]{1,0:T(8,128)(2,1)S(1)} %get-tuple-element.23.refs_3_, ...), custom_call_target="tpu_custom_call" | custom-call | tf_op jit(solution)/shard_map/place/pallas_call | solution.py:179
  27.2 1.9 %collective-permute-done.10.refs_0_ = bf16[32,2048]{1,0:T(8,128)(2,1)S(1)} collective-permute-done((bf16[32,2048]{1,0:T(8,128)(2,1)S(1)}, bf16[32,2048]{1,0:T(8,128)(2,1)S(1)}, u32[]{:S(2)}, u32[]{:S(2)}) %collective-permute-start.10) | collective-permute-done | bytes 131104 | tf_op jit(solution)/shard_map/ppermute | solution.py:170
  29.1 0.7 %place.4.refs_2_ = bf16[1,32,16384]{2,1,0:T(8,128)(2,1)} custom-call(bf16[32,2048]{1,0:T(8,128)(2,1)S(1)} %collective-permute-done.10.refs_0_, bf16[1,32,16384]{2,1,0:T(8,128)(2,1)} %place.3.refs_1_), custom_call_target="tpu_custom_call", output_to_operand_aliasing={{}: (1, {})} | custom-call | tf_op jit(solution)/shard_map/place/pallas_call | solution.py:179
  29.8 0.9 %collective-permute-done.8.refs_0_ = bf16[32,2048]{1,0:T(8,128)(2,1)S(1)} collective-permute-done((bf16[32,2048]{1,0:T(8,128)(2,1)S(1)}, bf16[32,2048]{1,0:T(8,128)(2,1)S(1)}, u32[]{:S(2)}, u32[]{:S(2)}) %collective-permute-start.8) | collective-permute-done | bytes 131104 | tf_op jit(solution)/shard_map/ppermute | solution.py:170
  30.7 0.0 collective-permute-done.9.refs_1_
  30.7 0.7 %place.5 = bf16[1,32,16384]{2,1,0:T(8,128)(2,1)} custom-call(bf16[32,2048]{1,0:T(8,128)(2,1)S(1)} %collective-permute-done.8.refs_0_, bf16[32,2048]{1,0:T(8,128)(2,1)S(1)} %collective-permute-done.9.refs_1_, bf16[1,32,16384]{2,1,0:T(8,128)(2,1)} %place.4.refs_2_), custom_call_target="tpu_custom_call", output_to_operand_aliasing={{}: (2, {})} | custom-call | tf_op jit(solution)/shard_map/place/pallas_call | solution.py:179
  (3 shorter events, 0.0 us)
Async XLA Ops:
  0.0 12.8 %collective-permute-start = (bf16[1,128,4096]{2,1,0:T(8,128)(2,1)}, bf16[1,128,4096]{2,1,0:T(8,128)(2,1)S(1)}, u32[]{:S(2)}, u32[]{:S(2)}) collective-permute-start(bf16[1,128,4096]{2,1,0:T(8,128)(2,1)} %param.5), channel_id=1, source_target_pairs={{0,1},{1,0},{8,9},{9,8},{16,17},{17,16},{24,25},{25,24},{2,3},{3,2... | collective-permute-start | bytes 3145736 | tf_op jit(solution)/shard_map/ppermute | solution.py:107
  1.3 7.3 %collective-permute-start.5 = (bf16[128,256]{1,0:T(8,128)(2,1)S(1)}, bf16[128,256]{1,0:T(8,128)(2,1)S(1)}, u32[]{:S(2)}, u32[]{:S(2)}) collective-permute-start(bf16[128,256]{1,0:T(8,128)(2,1)S(1)} %get-tuple-element.25), channel_id=1, source_target_pairs={{0,17},{1,16},{8,25},{9,24},{16,1},{17,0},{24,9},{25,8},{2,19},{3,... | collective-permute-start | bytes 196616 | tf_op jit(solution)/shard_map/ppermute | solution.py:107
  5.1 1.3 %copy-start = (s32[512]{0:T(512)S(1)}, s32[512]{0:T(512)}, u32[]{:S(2)}) copy-start(s32[512]{0:T(512)} %param.8) | copy-start | bytes 6148
  5.1 1.3 %copy-start.1 = (s32[16]{0:T(128)S(1)}, s32[16]{0:T(128)}, u32[]{:S(2)}) copy-start(s32[16]{0:T(128)} %lengths.1) | copy-start | bytes 196
  5.1 7.4 %collective-permute-start.2 = (bf16[2,128,256]{2,1,0:T(8,128)(2,1)S(1)}, bf16[2,128,256]{2,1,0:T(8,128)(2,1)S(1)}, u32[]{:S(2)}, u32[]{:S(2)}) collective-permute-start(bf16[2,128,256]{2,1,0:T(8,128)(2,1)S(1)} %pad_maximum_fusion), channel_id=1, source_target_pairs={{0,9},{1,8},{8,1},{9,0},{16,25},{17,24},{24,17},{25,16},{2,11},{3,... | collective-permute-start | bytes 393224 | tf_op jit(solution)/shard_map/ppermute | solution.py:107
  7.0 5.8 %collective-permute-start.1 = (bf16[2,128,256]{2,1,0:T(8,128)(2,1)S(1)}, bf16[2,128,256]{2,1,0:T(8,128)(2,1)S(1)}, u32[]{:S(2)}, u32[]{:S(2)}) collective-permute-start(bf16[2,128,256]{2,1,0:T(8,128)(2,1)S(1)} %pad_maximum_fusion), channel_id=1, source_target_pairs={{0,1},{1,0},{8,9},{9,8},{16,17},{17,16},{24,25},{25,24},{2,3},{3,2... | collective-permute-start | bytes 393224 | tf_op jit(solution)/shard_map/ppermute | solution.py:107
  8.6 4.3 %collective-permute-start.6 = (bf16[128,256]{1,0:T(8,128)(2,1)S(1)}, bf16[128,256]{1,0:T(8,128)(2,1)S(1)}, u32[]{:S(2)}, u32[]{:S(2)}) collective-permute-start(bf16[128,256]{1,0:T(8,128)(2,1)S(1)} %collective-permute-done.5.refs_2_), channel_id=1, source_target_pairs={{0,8},{8,0},{16,24},{24,16},{1,9},{9,1},{17,25},{25,17},{2,10},{10... | collective-permute-start | bytes 196616 | tf_op jit(solution)/shard_map/ppermute | solution.py:110
  9.8 6.1 %collective-permute-start.3 = (bf16[128,256]{1,0:T(8,128)(2,1)S(1)}, bf16[128,256]{1,0:T(8,128)(2,1)S(1)}, u32[]{:S(2)}, u32[]{:S(2)}) collective-permute-start(bf16[128,256]{1,0:T(8,128)(2,1)S(1)} %get-tuple-element.27), channel_id=1, source_target_pairs={{0,17},{1,16},{8,25},{9,24},{16,1},{17,0},{24,9},{25,8},{2,19},{3,... | collective-permute-start | bytes 196616 | tf_op jit(solution)/shard_map/ppermute | solution.py:107
  13.5 6.9 %collective-permute-start.7 = (bf16[32,2048]{1,0:T(8,128)(2,1)S(1)}, bf16[32,2048]{1,0:T(8,128)(2,1)S(1)}, u32[]{:S(2)}, u32[]{:S(2)}) collective-permute-start(bf16[32,2048]{1,0:T(8,128)(2,1)S(1)} %attend.4.refs_4_), channel_id=1, source_target_pairs={{0,6},{2,4},{4,2},{6,0},{1,7},{3,5},{5,3},{7,1},{8,14},{10,12},{12... | collective-permute-start | bytes 393224 | tf_op jit(solution)/shard_map/ppermute | solution.py:170
  15.9 4.5 %collective-permute-start.4 = (bf16[128,256]{1,0:T(8,128)(2,1)S(1)}, bf16[128,256]{1,0:T(8,128)(2,1)S(1)}, u32[]{:S(2)}, u32[]{:S(2)}) collective-permute-start(bf16[128,256]{1,0:T(8,128)(2,1)S(1)} %collective-permute-done.3.refs_2_.refs_6_), channel_id=1, source_target_pairs={{0,8},{8,0},{16,24},{24,16},{1,9},{9,1},{17,25},{25,17},{2,10},{10... | collective-permute-start | bytes 196616 | tf_op jit(solution)/shard_map/ppermute | solution.py:110
  18.3 8.0 %collective-permute-start.11 = (bf16[32,2048]{1,0:T(8,128)(2,1)S(1)}, bf16[32,2048]{1,0:T(8,128)(2,1)S(1)}, u32[]{:S(2)}, u32[]{:S(2)}) collective-permute-start(bf16[32,2048]{1,0:T(8,128)(2,1)S(1)} %get-tuple-element.22), channel_id=1, source_target_pairs={{0,2},{2,0},{4,6},{6,4},{1,3},{3,1},{5,7},{7,5},{8,10},{10,8},{12,... | collective-permute-start | bytes 393224 | tf_op jit(solution)/shard_map/ppermute | solution.py:170
  19.0 7.4 %collective-permute-start.12 = (bf16[32,2048]{1,0:T(8,128)(2,1)S(1)}, bf16[32,2048]{1,0:T(8,128)(2,1)S(1)}, u32[]{:S(2)}, u32[]{:S(2)}) collective-permute-start(bf16[32,2048]{1,0:T(8,128)(2,1)S(1)} %get-tuple-element.18.refs_4_), channel_id=1, source_target_pairs={{0,4},{2,6},{4,0},{6,2},{1,5},{3,7},{5,1},{7,3},{8,12},{10,14},{12... | collective-permute-start | bytes 393224 | tf_op jit(solution)/shard_map/ppermute | solution.py:170
  21.8 7.4 %collective-permute-start.10 = (bf16[32,2048]{1,0:T(8,128)(2,1)S(1)}, bf16[32,2048]{1,0:T(8,128)(2,1)S(1)}, u32[]{:S(2)}, u32[]{:S(2)}) collective-permute-start(bf16[32,2048]{1,0:T(8,128)(2,1)S(1)} %get-tuple-element.21), channel_id=1, source_target_pairs={{0,6},{2,4},{4,2},{6,0},{1,7},{3,5},{5,3},{7,1},{8,14},{10,12},{12... | collective-permute-start | bytes 393224 | tf_op jit(solution)/shard_map/ppermute | solution.py:170
  24.3 6.4 %collective-permute-start.8 = (bf16[32,2048]{1,0:T(8,128)(2,1)S(1)}, bf16[32,2048]{1,0:T(8,128)(2,1)S(1)}, u32[]{:S(2)}, u32[]{:S(2)}) collective-permute-start(bf16[32,2048]{1,0:T(8,128)(2,1)S(1)} %get-tuple-element.19), channel_id=1, source_target_pairs={{0,2},{2,0},{4,6},{6,4},{1,3},{3,1},{5,7},{7,5},{8,10},{10,8},{12,... | collective-permute-start | bytes 393224 | tf_op jit(solution)/shard_map/ppermute | solution.py:170
  24.9 5.8 %collective-permute-start.9 = (bf16[32,2048]{1,0:T(8,128)(2,1)S(1)}, bf16[32,2048]{1,0:T(8,128)(2,1)S(1)}, u32[]{:S(2)}, u32[]{:S(2)}) collective-permute-start(bf16[32,2048]{1,0:T(8,128)(2,1)S(1)} %get-tuple-element.20.refs_8_), channel_id=1, source_target_pairs={{0,4},{2,6},{4,0},{6,2},{1,5},{3,7},{5,1},{7,3},{8,12},{10,14},{12... | collective-permute-start | bytes 393224 | tf_op jit(solution)/shard_map/ppermute | solution.py:170

commit v5 on v4

--- a/solution.py
+++ b/solution.py
@@ -161,12 +161,12 @@
     for g in range(groups):
         parts = ((3,), (1, 2)) if g + 1 < groups else ((3, 1, 2),)
         for index, partners in enumerate(parts):
-            for d in [(3,)][index] if g else ():
-                last.append(arrived[d, g - 1])
             slots = [(d, g) for d in partners]
             pieces = attend(slots, *last)
             last = [pieces[-1]]
             for (d, _), piece in zip(slots, pieces):
+                if g and d == 1:
+                    piece = after(piece, arrived[3, g - 1])
                 arrived[d, g] = lax.ppermute(piece, "head", [(h, h ^ d) for h in range(heads)])
     slots = [(0, g) for g in range(groups)]
     for slot, piece in zip(slots, attend(slots, *last)):

time: 31.6 us -> 31.5 us (level)
  no operation moved by 1% of the time
where the time goes in v5:
time: 31.5 us; the launch traced here: 31.3 us
  starting transfers between devices  19.5 us (62%)
  Pallas kernels  6.91 us (22%)
  waiting for transfers between devices  3.98 us (13%)
  local copies, waits for them, and re-layouts  0.83 us (3%)
    ppermute x5, starting transfers between devices, handed(): return lax.ppermute(value, ('ctx', 'section'), pairs)  8.78 us
    ppermute x6, starting transfers between devices, local(): lax.ppermute(piece, 'head', [(h, h ^ d) for h in range(heads)])  8.12 us
    pallas_call x4, Pallas kernels, attend(): pl.pallas_call(functools.partial(attend_kernel, LOG2E / HD ** 0.5, slots,...  3.99 us
    ppermute x6, waiting for transfers between devices, local(): lax.ppermute(piece, 'head', [(h, h ^ d) for h in range(heads)])  2.72 us
    ppermute x2, starting transfers between devices, passed(): return lax.ppermute(value, 'ctx', [(c, c ^ step) for c in range(shards)])  2.57 us
    pallas_call x3, Pallas kernels, local(): pl.pallas_call(functools.partial(place_kernel, slots, groups), out_shape=...  2.26 us
    ppermute x5, waiting for transfers between devices, handed(): return lax.ppermute(value, ('ctx', 'section'), pairs)  0.96 us
    squeeze x1, local copies, waits for them, and re-layouts, local(): kv[0, :, g * HD:(g + 1) * HD]  0.82 us
  transfers between devices with their start and end apart: 13, of which 4 were waited for; matrix products, arithmetic and copies ran while one was open for 3% of the time, Pallas kernels for 20%

profile of v5, /device:TPU:0, one launch (start us, length us, event | category | flops | bytes accessed | tf_op | source)
XLA Modules:
  0.0 31.3 jit_solution(13121821569970693217)
XLA Ops:
  0.0 0.5 %collective-permute-start = (bf16[1,128,4096]{2,1,0:T(8,128)(2,1)}, bf16[1,128,4096]{2,1,0:T(8,128)(2,1)S(1)}, u32[]{:S(2)}, u32[]{:S(2)}) collective-permute-start(bf16[1,128,4096]{2,1,0:T(8,128)(2,1)} %param.5), channel_id=1, source_target_pairs={{0,1},{1,0},{8,9},{9,8},{16,17},{17,16},{24,25},{25,24},{2,3},{3,2... | collective-permute-start | bytes 3145736 | tf_op jit(solution)/shard_map/ppermute | solution.py:107
  0.5 0.8 %slice_bitcast_fusion.2 = (bf16[128,128]{1,0:T(8,128)(2,1)S(1)}, bf16[128,128]{1,0:T(8,128)(2,1)S(1)}, bf16[128,128]{1,0:T(8,128)(2,1)S(1)}, bf16[128,128]{1,0:T(8,128)(2,1)S(1)}) fusion(bf16[1,128,256]{2,1,0:T(8,128)(2,1)} %param.7, bf16[1,128,256]{2,1,0:T(8,128)(2,1)} %param.6), kind=kLoop, calls=%fused_computation.5 | loop fusion | bytes 262144 | tf_op jit(solution)/shard_map/squeeze | solution.py:126
  1.3 3.8 %collective-permute-start.5 = (bf16[128,256]{1,0:T(8,128)(2,1)S(1)}, bf16[128,256]{1,0:T(8,128)(2,1)S(1)}, u32[]{:S(2)}, u32[]{:S(2)}) collective-permute-start(bf16[128,256]{1,0:T(8,128)(2,1)S(1)} %get-tuple-element.27), channel_id=1, source_target_pairs={{0,17},{1,16},{8,25},{9,24},{16,1},{17,0},{24,9},{25,8},{2,19},{3,... | collective-permute-start | bytes 196616 | tf_op jit(solution)/shard_map/ppermute | solution.py:107
  5.1 0.0 copy-start
  5.1 0.0 copy-start.1
  5.1 1.2 %collective-permute-start.2 = (bf16[2,128,256]{2,1,0:T(8,128)(2,1)S(1)}, bf16[2,128,256]{2,1,0:T(8,128)(2,1)S(1)}, u32[]{:S(2)}, u32[]{:S(2)}) collective-permute-start(bf16[2,128,256]{2,1,0:T(8,128)(2,1)S(1)} %pad_maximum_fusion), channel_id=1, source_target_pairs={{0,9},{1,8},{8,1},{9,0},{16,25},{17,24},{24,17},{25,16},{2,11},{3,... | collective-permute-start | bytes 393224 | tf_op jit(solution)/shard_map/ppermute | solution.py:107
  6.4 0.0 copy-done
  6.4 0.0 copy-done.1
  6.4 0.7 %bias.1 = f32[128,512]{1,0:T(8,128)S(1)} custom-call(s32[16]{0:T(128)S(1)} %copy-done.1, s32[4,128]{1,0:T(4,128)S(1)} %bitcast.13), custom_call_target="tpu_custom_call" | custom-call | tf_op jit(solution)/shard_map/bias/pallas_call | solution.py:116
  7.0 0.6 %collective-permute-start.1 = (bf16[2,128,256]{2,1,0:T(8,128)(2,1)S(1)}, bf16[2,128,256]{2,1,0:T(8,128)(2,1)S(1)}, u32[]{:S(2)}, u32[]{:S(2)}) collective-permute-start(bf16[2,128,256]{2,1,0:T(8,128)(2,1)S(1)} %pad_maximum_fusion), channel_id=1, source_target_pairs={{0,1},{1,0},{8,9},{9,8},{16,17},{17,16},{24,25},{25,24},{2,3},{3,2... | collective-permute-start | bytes 393224 | tf_op jit(solution)/shard_map/ppermute | solution.py:107
  7.6 0.9 %collective-permute-done.5.refs_2_ = bf16[128,256]{1,0:T(8,128)(2,1)S(1)} collective-permute-done((bf16[128,256]{1,0:T(8,128)(2,1)S(1)}, bf16[128,256]{1,0:T(8,128)(2,1)S(1)}, u32[]{:S(2)}, u32[]{:S(2)}) %collective-permute-start.5) | collective-permute-done | bytes 65568 | tf_op jit(solution)/shard_map/ppermute | solution.py:107
  8.6 1.2 %collective-permute-start.6 = (bf16[128,256]{1,0:T(8,128)(2,1)S(1)}, bf16[128,256]{1,0:T(8,128)(2,1)S(1)}, u32[]{:S(2)}, u32[]{:S(2)}) collective-permute-start(bf16[128,256]{1,0:T(8,128)(2,1)S(1)} %collective-permute-done.5.refs_2_), channel_id=1, source_target_pairs={{0,8},{8,0},{16,24},{24,16},{1,9},{9,1},{17,25},{25,17},{2,10},{10... | collective-permute-start | bytes 196616 | tf_op jit(solution)/shard_map/ppermute | solution.py:110
  9.8 2.7 %collective-permute-start.3 = (bf16[128,256]{1,0:T(8,128)(2,1)S(1)}, bf16[128,256]{1,0:T(8,128)(2,1)S(1)}, u32[]{:S(2)}, u32[]{:S(2)}) collective-permute-start(bf16[128,256]{1,0:T(8,128)(2,1)S(1)} %get-tuple-element.29), channel_id=1, source_target_pairs={{0,17},{1,16},{8,25},{9,24},{16,1},{17,0},{24,9},{25,8},{2,19},{3,... | collective-permute-start | bytes 196616 | tf_op jit(solution)/shard_map/ppermute | solution.py:107
  12.5 0.0 collective-permute-done.2.refs_1_.refs_5_
  12.5 0.3 collective-permute-done.6.refs_3_
  12.8 0.0 collective-permute-done.1.refs_0_.refs_4_
  12.8 0.0 collective-permute-done.q
  12.8 0.7 %attend.4.refs_4_ = bf16[32,2048]{1,0:T(8,128)(2,1)S(1)} custom-call(bf16[1,128,4096]{2,1,0:T(8,128)(2,1)S(1)} %collective-permute-done.q, f32[128,512]{1,0:T(8,128)S(1)} %bias.1, bf16[2,128,256]{2,1,0:T(8,128)(2,1)S(1)} %collective-permute-done.1.refs_0_.refs_4_, bf16[2,128,256]{2,1,0:T(8,128)(2,1)S(1)} %collective-permute-done.2.refs_1_.refs_5_, ...), custom_call_target="tpu_custom_call" | custom-call | flops 134217728 | bytes 262144 | tf_op jit(solution)/shard_map/attend/pallas_call | solution.py:145
  13.5 2.4 %collective-permute-start.7 = (bf16[32,2048]{1,0:T(8,128)(2,1)S(1)}, bf16[32,2048]{1,0:T(8,128)(2,1)S(1)}, u32[]{:S(2)}, u32[]{:S(2)}) collective-permute-start(bf16[32,2048]{1,0:T(8,128)(2,1)S(1)} %attend.4.refs_4_), channel_id=1, source_target_pairs={{0,6},{2,4},{4,2},{6,0},{1,7},{3,5},{5,3},{7,1},{8,14},{10,12},{12... | collective-permute-start | bytes 393224 | tf_op jit(solution)/shard_map/ppermute | solution.py:170
  15.9 0.0 collective-permute-done.3.refs_2_.refs_6_
  15.9 1.4 %collective-permute-start.4 = (bf16[128,256]{1,0:T(8,128)(2,1)S(1)}, bf16[128,256]{1,0:T(8,128)(2,1)S(1)}, u32[]{:S(2)}, u32[]{:S(2)}) collective-permute-start(bf16[128,256]{1,0:T(8,128)(2,1)S(1)} %collective-permute-done.3.refs_2_.refs_6_), channel_id=1, source_target_pairs={{0,8},{8,0},{16,24},{24,16},{1,9},{9,1},{17,25},{25,17},{2,10},{10... | collective-permute-start | bytes 196616 | tf_op jit(solution)/shard_map/ppermute | solution.py:110
  17.3 1.0 %attend.5 = (bf16[32,2048]{1,0:T(8,128)(2,1)S(1)}, bf16[32,2048]{1,0:T(8,128)(2,1)S(1)}) custom-call(bf16[1,128,4096]{2,1,0:T(8,128)(2,1)S(1)} %collective-permute-done.q, f32[128,512]{1,0:T(8,128)S(1)} %bias.1, bf16[2,128,256]{2,1,0:T(8,128)(2,1)S(1)} %collective-permute-done.1.refs_0_.refs_4_, ...), custom_call_target="tpu_custom_call" | custom-call | flops 268435456 | bytes 524288 | tf_op jit(solution)/shard_map/attend/pallas_call | solution.py:145
  18.3 0.7 %collective-permute-start.11 = (bf16[32,2048]{1,0:T(8,128)(2,1)S(1)}, bf16[32,2048]{1,0:T(8,128)(2,1)S(1)}, u32[]{:S(2)}, u32[]{:S(2)}) collective-permute-start(bf16[32,2048]{1,0:T(8,128)(2,1)S(1)} %get-tuple-element.24), channel_id=1, source_target_pairs={{0,2},{2,0},{4,6},{6,4},{1,3},{3,1},{5,7},{7,5},{8,10},{10,8},{12,... | collective-permute-start | bytes 393224 | tf_op jit(solution)/shard_map/ppermute | solution.py:170
  19.0 1.5 %collective-permute-start.12 = (bf16[32,2048]{1,0:T(8,128)(2,1)S(1)}, bf16[32,2048]{1,0:T(8,128)(2,1)S(1)}, u32[]{:S(2)}, u32[]{:S(2)}) collective-permute-start(bf16[32,2048]{1,0:T(8,128)(2,1)S(1)} %get-tuple-element.19.refs_4_), channel_id=1, source_target_pairs={{0,4},{2,6},{4,0},{6,2},{1,5},{3,7},{5,1},{7,3},{8,12},{10,14},{12... | collective-permute-start | bytes 393224 | tf_op jit(solution)/shard_map/ppermute | solution.py:170
  20.5 0.0 collective-permute-done.4.refs_3_.refs_7_
  20.5 1.3 %attend.6 = (bf16[32,2048]{1,0:T(8,128)(2,1)S(1)}, bf16[32,2048]{1,0:T(8,128)(2,1)S(1)}, bf16[32,2048]{1,0:T(8,128)(2,1)S(1)}) custom-call(bf16[1,128,4096]{2,1,0:T(8,128)(2,1)S(1)} %collective-permute-done.q, f32[128,512]{1,0:T(8,128)S(1)} %bias.1, bf16[2,128,256]{2,1,0:T(8,128)(2,1)S(1)} %collective-permute-done.1.refs_0_.refs_4_, ...), custom_call_target="tpu_custom_call" | custom-call | flops 402653184 | bytes 786432 | tf_op jit(solution)/shard_map/attend/pallas_call | solution.py:145
  21.8 1.6 %collective-permute-start.10 = (bf16[32,2048]{1,0:T(8,128)(2,1)S(1)}, bf16[32,2048]{1,0:T(8,128)(2,1)S(1)}, u32[]{:S(2)}, u32[]{:S(2)}) collective-permute-start(bf16[32,2048]{1,0:T(8,128)(2,1)S(1)} %get-tuple-element.23), channel_id=1, source_target_pairs={{0,6},{2,4},{4,2},{6,0},{1,7},{3,5},{5,3},{7,1},{8,14},{10,12},{12... | collective-permute-start | bytes 393224 | tf_op jit(solution)/shard_map/ppermute | solution.py:170
  23.3 0.5 %collective-permute-start.9 = (bf16[32,2048]{1,0:T(8,128)(2,1)S(1)}, bf16[32,2048]{1,0:T(8,128)(2,1)S(1)}, u32[]{:S(2)}, u32[]{:S(2)}) collective-permute-start(bf16[32,2048]{1,0:T(8,128)(2,1)S(1)} %get-tuple-element.22.refs_8_), channel_id=1, source_target_pairs={{0,4},{2,6},{4,0},{6,2},{1,5},{3,7},{5,1},{7,3},{8,12},{10,14},{12... | collective-permute-start | bytes 393224 | tf_op jit(solution)/shard_map/ppermute | solution.py:170
  23.9 0.0 collective-permute-done.7.refs_0_
  23.9 1.5 %collective-permute-start.8 = (bf16[32,2048]{1,0:T(8,128)(2,1)S(1)}, bf16[32,2048]{1,0:T(8,128)(2,1)S(1)}, u32[]{:S(2)}, u32[]{:S(2)}) collective-permute-start(bf16[32,2048]{1,0:T(8,128)(2,1)S(1)} %get-tuple-element.21), channel_id=1, source_target_pairs={{0,2},{2,0},{4,6},{6,4},{1,3},{3,1},{5,7},{7,5},{8,10},{10,8},{12,... | collective-permute-start | bytes 393224 | tf_op jit(solution)/shard_map/ppermute | solution.py:170
  25.3 1.0 %attend.7 = (bf16[32,2048]{1,0:T(8,128)(2,1)S(1)}, bf16[32,2048]{1,0:T(8,128)(2,1)S(1)}) custom-call(bf16[1,128,4096]{2,1,0:T(8,128)(2,1)S(1)} %collective-permute-done.q, f32[128,512]{1,0:T(8,128)S(1)} %bias.1, bf16[2,128,256]{2,1,0:T(8,128)(2,1)S(1)} %collective-permute-done.1.refs_0_.refs_4_, ...), custom_call_target="tpu_custom_call" | custom-call | flops 268435456 | bytes 524288 | tf_op jit(solution)/shard_map/attend/pallas_call | solution.py:145
  26.3 0.0 collective-permute-done.11.refs_1_
  26.3 0.0 collective-permute-done.12.refs_2_
  26.4 0.9 %place.3.refs_1_ = bf16[1,32,16384]{2,1,0:T(8,128)(2,1)} custom-call(bf16[32,2048]{1,0:T(8,128)(2,1)S(1)} %collective-permute-done.7.refs_0_, bf16[32,2048]{1,0:T(8,128)(2,1)S(1)} %collective-permute-done.11.refs_1_, bf16[32,2048]{1,0:T(8,128)(2,1)S(1)} %collective-permute-done.12.refs_2_, bf16[32,2048]{1,0:T(8,128)(2,1)S(1)} %get-tuple-element.25.refs_3_, ...), custom_call_target="tpu_custom_call" | custom-call | tf_op jit(solution)/shard_map/place/pallas_call | solution.py:179
  27.2 1.0 %collective-permute-done.10.refs_0_ = bf16[32,2048]{1,0:T(8,128)(2,1)S(1)} collective-permute-done((bf16[32,2048]{1,0:T(8,128)(2,1)S(1)}, bf16[32,2048]{1,0:T(8,128)(2,1)S(1)}, u32[]{:S(2)}, u32[]{:S(2)}) %collective-permute-start.10) | collective-permute-done | bytes 131104 | tf_op jit(solution)/shard_map/ppermute | solution.py:170
  28.2 0.7 %place.4.refs_2_ = bf16[1,32,16384]{2,1,0:T(8,128)(2,1)} custom-call(bf16[32,2048]{1,0:T(8,128)(2,1)S(1)} %collective-permute-done.10.refs_0_, bf16[1,32,16384]{2,1,0:T(8,128)(2,1)} %place.3.refs_1_), custom_call_target="tpu_custom_call", output_to_operand_aliasing={{}: (1, {})} | custom-call | tf_op jit(solution)/shard_map/place/pallas_call | solution.py:179
  28.9 1.7 %collective-permute-done.9.refs_1_ = bf16[32,2048]{1,0:T(8,128)(2,1)S(1)} collective-permute-done((bf16[32,2048]{1,0:T(8,128)(2,1)S(1)}, bf16[32,2048]{1,0:T(8,128)(2,1)S(1)}, u32[]{:S(2)}, u32[]{:S(2)}) %collective-permute-start.9) | collective-permute-done | bytes 131104 | tf_op jit(solution)/shard_map/ppermute | solution.py:170
  30.6 0.0 collective-permute-done.8.refs_0_
  30.6 0.7 %place.5 = bf16[1,32,16384]{2,1,0:T(8,128)(2,1)} custom-call(bf16[32,2048]{1,0:T(8,128)(2,1)S(1)} %collective-permute-done.8.refs_0_, bf16[32,2048]{1,0:T(8,128)(2,1)S(1)} %collective-permute-done.9.refs_1_, bf16[1,32,16384]{2,1,0:T(8,128)(2,1)} %place.4.refs_2_), custom_call_target="tpu_custom_call", output_to_operand_aliasing={{}: (2, {})} | custom-call | tf_op jit(solution)/shard_map/place/pallas_call | solution.py:179
  (3 shorter events, 0.0 us)
Async XLA Ops:
  0.0 12.8 %collective-permute-start = (bf16[1,128,4096]{2,1,0:T(8,128)(2,1)}, bf16[1,128,4096]{2,1,0:T(8,128)(2,1)S(1)}, u32[]{:S(2)}, u32[]{:S(2)}) collective-permute-start(bf16[1,128,4096]{2,1,0:T(8,128)(2,1)} %param.5), channel_id=1, source_target_pairs={{0,1},{1,0},{8,9},{9,8},{16,17},{17,16},{24,25},{25,24},{2,3},{3,2... | collective-permute-start | bytes 3145736 | tf_op jit(solution)/shard_map/ppermute | solution.py:107
  1.3 7.3 %collective-permute-start.5 = (bf16[128,256]{1,0:T(8,128)(2,1)S(1)}, bf16[128,256]{1,0:T(8,128)(2,1)S(1)}, u32[]{:S(2)}, u32[]{:S(2)}) collective-permute-start(bf16[128,256]{1,0:T(8,128)(2,1)S(1)} %get-tuple-element.27), channel_id=1, source_target_pairs={{0,17},{1,16},{8,25},{9,24},{16,1},{17,0},{24,9},{25,8},{2,19},{3,... | collective-permute-start | bytes 196616 | tf_op jit(solution)/shard_map/ppermute | solution.py:107
  5.1 1.3 %copy-start = (s32[512]{0:T(512)S(1)}, s32[512]{0:T(512)}, u32[]{:S(2)}) copy-start(s32[512]{0:T(512)} %param.8) | copy-start | bytes 6148
  5.1 1.3 %copy-start.1 = (s32[16]{0:T(128)S(1)}, s32[16]{0:T(128)}, u32[]{:S(2)}) copy-start(s32[16]{0:T(128)} %lengths.1) | copy-start | bytes 196
  5.1 7.4 %collective-permute-start.2 = (bf16[2,128,256]{2,1,0:T(8,128)(2,1)S(1)}, bf16[2,128,256]{2,1,0:T(8,128)(2,1)S(1)}, u32[]{:S(2)}, u32[]{:S(2)}) collective-permute-start(bf16[2,128,256]{2,1,0:T(8,128)(2,1)S(1)} %pad_maximum_fusion), channel_id=1, source_target_pairs={{0,9},{1,8},{8,1},{9,0},{16,25},{17,24},{24,17},{25,16},{2,11},{3,... | collective-permute-start | bytes 393224 | tf_op jit(solution)/shard_map/ppermute | solution.py:107
  7.0 5.8 %collective-permute-start.1 = (bf16[2,128,256]{2,1,0:T(8,128)(2,1)S(1)}, bf16[2,128,256]{2,1,0:T(8,128)(2,1)S(1)}, u32[]{:S(2)}, u32[]{:S(2)}) collective-permute-start(bf16[2,128,256]{2,1,0:T(8,128)(2,1)S(1)} %pad_maximum_fusion), channel_id=1, source_target_pairs={{0,1},{1,0},{8,9},{9,8},{16,17},{17,16},{24,25},{25,24},{2,3},{3,2... | collective-permute-start | bytes 393224 | tf_op jit(solution)/shard_map/ppermute | solution.py:107
  8.6 4.3 %collective-permute-start.6 = (bf16[128,256]{1,0:T(8,128)(2,1)S(1)}, bf16[128,256]{1,0:T(8,128)(2,1)S(1)}, u32[]{:S(2)}, u32[]{:S(2)}) collective-permute-start(bf16[128,256]{1,0:T(8,128)(2,1)S(1)} %collective-permute-done.5.refs_2_), channel_id=1, source_target_pairs={{0,8},{8,0},{16,24},{24,16},{1,9},{9,1},{17,25},{25,17},{2,10},{10... | collective-permute-start | bytes 196616 | tf_op jit(solution)/shard_map/ppermute | solution.py:110
  9.8 6.1 %collective-permute-start.3 = (bf16[128,256]{1,0:T(8,128)(2,1)S(1)}, bf16[128,256]{1,0:T(8,128)(2,1)S(1)}, u32[]{:S(2)}, u32[]{:S(2)}) collective-permute-start(bf16[128,256]{1,0:T(8,128)(2,1)S(1)} %get-tuple-element.29), channel_id=1, source_target_pairs={{0,17},{1,16},{8,25},{9,24},{16,1},{17,0},{24,9},{25,8},{2,19},{3,... | collective-permute-start | bytes 196616 | tf_op jit(solution)/shard_map/ppermute | solution.py:107
  13.5 10.3 %collective-permute-start.7 = (bf16[32,2048]{1,0:T(8,128)(2,1)S(1)}, bf16[32,2048]{1,0:T(8,128)(2,1)S(1)}, u32[]{:S(2)}, u32[]{:S(2)}) collective-permute-start(bf16[32,2048]{1,0:T(8,128)(2,1)S(1)} %attend.4.refs_4_), channel_id=1, source_target_pairs={{0,6},{2,4},{4,2},{6,0},{1,7},{3,5},{5,3},{7,1},{8,14},{10,12},{12... | collective-permute-start | bytes 393224 | tf_op jit(solution)/shard_map/ppermute | solution.py:170
  15.9 4.5 %collective-permute-start.4 = (bf16[128,256]{1,0:T(8,128)(2,1)S(1)}, bf16[128,256]{1,0:T(8,128)(2,1)S(1)}, u32[]{:S(2)}, u32[]{:S(2)}) collective-permute-start(bf16[128,256]{1,0:T(8,128)(2,1)S(1)} %collective-permute-done.3.refs_2_.refs_6_), channel_id=1, source_target_pairs={{0,8},{8,0},{16,24},{24,16},{1,9},{9,1},{17,25},{25,17},{2,10},{10... | collective-permute-start | bytes 196616 | tf_op jit(solution)/shard_map/ppermute | solution.py:110
  18.3 8.0 %collective-permute-start.11 = (bf16[32,2048]{1,0:T(8,128)(2,1)S(1)}, bf16[32,2048]{1,0:T(8,128)(2,1)S(1)}, u32[]{:S(2)}, u32[]{:S(2)}) collective-permute-start(bf16[32,2048]{1,0:T(8,128)(2,1)S(1)} %get-tuple-element.24), channel_id=1, source_target_pairs={{0,2},{2,0},{4,6},{6,4},{1,3},{3,1},{5,7},{7,5},{8,10},{10,8},{12,... | collective-permute-start | bytes 393224 | tf_op jit(solution)/shard_map/ppermute | solution.py:170
  19.0 7.4 %collective-permute-start.12 = (bf16[32,2048]{1,0:T(8,128)(2,1)S(1)}, bf16[32,2048]{1,0:T(8,128)(2,1)S(1)}, u32[]{:S(2)}, u32[]{:S(2)}) collective-permute-start(bf16[32,2048]{1,0:T(8,128)(2,1)S(1)} %get-tuple-element.19.refs_4_), channel_id=1, source_target_pairs={{0,4},{2,6},{4,0},{6,2},{1,5},{3,7},{5,1},{7,3},{8,12},{10,14},{12... | collective-permute-start | bytes 393224 | tf_op jit(solution)/shard_map/ppermute | solution.py:170
  21.8 6.5 %collective-permute-start.10 = (bf16[32,2048]{1,0:T(8,128)(2,1)S(1)}, bf16[32,2048]{1,0:T(8,128)(2,1)S(1)}, u32[]{:S(2)}, u32[]{:S(2)}) collective-permute-start(bf16[32,2048]{1,0:T(8,128)(2,1)S(1)} %get-tuple-element.23), channel_id=1, source_target_pairs={{0,6},{2,4},{4,2},{6,0},{1,7},{3,5},{5,3},{7,1},{8,14},{10,12},{12... | collective-permute-start | bytes 393224 | tf_op jit(solution)/shard_map/ppermute | solution.py:170
  23.3 7.3 %collective-permute-start.9 = (bf16[32,2048]{1,0:T(8,128)(2,1)S(1)}, bf16[32,2048]{1,0:T(8,128)(2,1)S(1)}, u32[]{:S(2)}, u32[]{:S(2)}) collective-permute-start(bf16[32,2048]{1,0:T(8,128)(2,1)S(1)} %get-tuple-element.22.refs_8_), channel_id=1, source_target_pairs={{0,4},{2,6},{4,0},{6,2},{1,5},{3,7},{5,1},{7,3},{8,12},{10,14},{12... | collective-permute-start | bytes 393224 | tf_op jit(solution)/shard_map/ppermute | solution.py:170
  23.9 6.8 %collective-permute-start.8 = (bf16[32,2048]{1,0:T(8,128)(2,1)S(1)}, bf16[32,2048]{1,0:T(8,128)(2,1)S(1)}, u32[]{:S(2)}, u32[]{:S(2)}) collective-permute-start(bf16[32,2048]{1,0:T(8,128)(2,1)S(1)} %get-tuple-element.21), channel_id=1, source_target_pairs={{0,2},{2,0},{4,6},{6,4},{1,3},{3,1},{5,7},{7,5},{8,10},{10,8},{12,... | collective-permute-start | bytes 393224 | tf_op jit(solution)/shard_map/ppermute | solution.py:170

commit v6 on v5

--- a/solution.py
+++ b/solution.py
@@ -159,7 +159,7 @@
     arrived = {}
     last = []
     for g in range(groups):
-        parts = ((3,), (1, 2)) if g + 1 < groups else ((3, 1, 2),)
+        parts = ((3, 1, 2),) if g + 1 < groups else ((3, 1, 2),)
         for index, partners in enumerate(parts):
             slots = [(d, g) for d in partners]
             pieces = attend(slots, *last)

time: 31.5 us -> 32 us (1.016)
  waiting for transfers between devices: 3.98 us -> 5.47 us
  starting transfers between devices: 19.5 us -> 18.8 us
  Pallas kernels: 6.91 us -> 6.5 us
    ppermute x2, waiting for transfers between devices: 0.3 us -> 1.71 us  [passed(): return lax.ppermute(value, 'ctx', [(c, c ^ step) for c in range(shards)])]
    ppermute x6, starting transfers between devices: 8.12 us -> 7.47 us  [local(): lax.ppermute(piece, 'head', [(h, h ^ d) for h in range(heads)])]
    pallas_call x4 -> x3, Pallas kernels: 3.99 us -> 3.58 us  [attend(): pl.pallas_call(functools.partial(attend_kernel, LOG2E / HD ** 0.5, slots,...]
  transfers between devices with their start and end apart: 13 -> 13, of which waited for: 4 -> 6; matrix products, arithmetic and copies ran while one was open for 3% -> 3% of each run, Pallas kernels for 20% -> 18%
where the time goes in v6:
time: 32 us; the launch traced here: 31.8 us
  starting transfers between devices  18.8 us (59%)
  Pallas kernels  6.5 us (20%)
  waiting for transfers between devices  5.47 us (17%)
  local copies, waits for them, and re-layouts  0.83 us (3%)
    ppermute x5, starting transfers between devices, handed(): return lax.ppermute(value, ('ctx', 'section'), pairs)  8.78 us
    ppermute x6, starting transfers between devices, local(): lax.ppermute(piece, 'head', [(h, h ^ d) for h in range(heads)])  7.47 us
    pallas_call x3, Pallas kernels, attend(): pl.pallas_call(functools.partial(attend_kernel, LOG2E / HD ** 0.5, slots,...  3.58 us
    ppermute x6, waiting for transfers between devices, local(): lax.ppermute(piece, 'head', [(h, h ^ d) for h in range(heads)])  2.8 us
    ppermute x2, starting transfers between devices, passed(): return lax.ppermute(value, 'ctx', [(c, c ^ step) for c in range(shards)])  2.57 us
    pallas_call x3, Pallas kernels, local(): pl.pallas_call(functools.partial(place_kernel, slots, groups), out_shape=...  2.26 us
    ppermute x2, waiting for transfers between devices, passed(): return lax.ppermute(value, 'ctx', [(c, c ^ step) for c in range(shards)])  1.71 us
    ppermute x5, waiting for transfers between devices, handed(): return lax.ppermute(value, ('ctx', 'section'), pairs)  0.96 us
  transfers between devices with their start and end apart: 13, of which 6 were waited for; matrix products, arithmetic and copies ran while one was open for 3% of the time, Pallas kernels for 18%

profile of v6, /device:TPU:0, one launch (start us, length us, event | category | flops | bytes accessed | tf_op | source)
XLA Modules:
  0.0 31.8 jit_solution(3618538261948134520)
XLA Ops:
  0.0 0.5 %collective-permute-start = (bf16[1,128,4096]{2,1,0:T(8,128)(2,1)}, bf16[1,128,4096]{2,1,0:T(8,128)(2,1)S(1)}, u32[]{:S(2)}, u32[]{:S(2)}) collective-permute-start(bf16[1,128,4096]{2,1,0:T(8,128)(2,1)} %param.5), channel_id=1, source_target_pairs={{0,1},{1,0},{8,9},{9,8},{16,17},{17,16},{24,25},{25,24},{2,3},{3,2... | collective-permute-start | bytes 3145736 | tf_op jit(solution)/shard_map/ppermute | solution.py:107
  0.5 0.8 %slice_bitcast_fusion.2 = (bf16[128,128]{1,0:T(8,128)(2,1)S(1)}, bf16[128,128]{1,0:T(8,128)(2,1)S(1)}, bf16[128,128]{1,0:T(8,128)(2,1)S(1)}, bf16[128,128]{1,0:T(8,128)(2,1)S(1)}) fusion(bf16[1,128,256]{2,1,0:T(8,128)(2,1)} %param.7, bf16[1,128,256]{2,1,0:T(8,128)(2,1)} %param.6), kind=kLoop, calls=%fused_computation.5 | loop fusion | bytes 262144 | tf_op jit(solution)/shard_map/squeeze | solution.py:126
  1.3 3.8 %collective-permute-start.5 = (bf16[128,256]{1,0:T(8,128)(2,1)S(1)}, bf16[128,256]{1,0:T(8,128)(2,1)S(1)}, u32[]{:S(2)}, u32[]{:S(2)}) collective-permute-start(bf16[128,256]{1,0:T(8,128)(2,1)S(1)} %get-tuple-element.29), channel_id=1, source_target_pairs={{0,17},{1,16},{8,25},{9,24},{16,1},{17,0},{24,9},{25,8},{2,19},{3,... | collective-permute-start | bytes 196616 | tf_op jit(solution)/shard_map/ppermute | solution.py:107
  5.1 0.0 copy-start
  5.1 0.0 copy-start.1
  5.1 1.2 %collective-permute-start.2 = (bf16[2,128,256]{2,1,0:T(8,128)(2,1)S(1)}, bf16[2,128,256]{2,1,0:T(8,128)(2,1)S(1)}, u32[]{:S(2)}, u32[]{:S(2)}) collective-permute-start(bf16[2,128,256]{2,1,0:T(8,128)(2,1)S(1)} %pad_maximum_fusion), channel_id=1, source_target_pairs={{0,9},{1,8},{8,1},{9,0},{16,25},{17,24},{24,17},{25,16},{2,11},{3,... | collective-permute-start | bytes 393224 | tf_op jit(solution)/shard_map/ppermute | solution.py:107
  6.4 0.0 copy-done
  6.4 0.0 copy-done.1
  6.4 0.7 %bias.1 = f32[128,512]{1,0:T(8,128)S(1)} custom-call(s32[16]{0:T(128)S(1)} %copy-done.1, s32[4,128]{1,0:T(4,128)S(1)} %bitcast.13), custom_call_target="tpu_custom_call" | custom-call | tf_op jit(solution)/shard_map/bias/pallas_call | solution.py:116
  7.0 0.6 %collective-permute-start.1 = (bf16[2,128,256]{2,1,0:T(8,128)(2,1)S(1)}, bf16[2,128,256]{2,1,0:T(8,128)(2,1)S(1)}, u32[]{:S(2)}, u32[]{:S(2)}) collective-permute-start(bf16[2,128,256]{2,1,0:T(8,128)(2,1)S(1)} %pad_maximum_fusion), channel_id=1, source_target_pairs={{0,1},{1,0},{8,9},{9,8},{16,17},{17,16},{24,25},{25,24},{2,3},{3,2... | collective-permute-start | bytes 393224 | tf_op jit(solution)/shard_map/ppermute | solution.py:107
  7.6 0.9 %collective-permute-done.5.refs_2_ = bf16[128,256]{1,0:T(8,128)(2,1)S(1)} collective-permute-done((bf16[128,256]{1,0:T(8,128)(2,1)S(1)}, bf16[128,256]{1,0:T(8,128)(2,1)S(1)}, u32[]{:S(2)}, u32[]{:S(2)}) %collective-permute-start.5) | collective-permute-done | bytes 65568 | tf_op jit(solution)/shard_map/ppermute | solution.py:107
  8.6 1.2 %collective-permute-start.6 = (bf16[128,256]{1,0:T(8,128)(2,1)S(1)}, bf16[128,256]{1,0:T(8,128)(2,1)S(1)}, u32[]{:S(2)}, u32[]{:S(2)}) collective-permute-start(bf16[128,256]{1,0:T(8,128)(2,1)S(1)} %collective-permute-done.5.refs_2_), channel_id=1, source_target_pairs={{0,8},{8,0},{16,24},{24,16},{1,9},{9,1},{17,25},{25,17},{2,10},{10... | collective-permute-start | bytes 196616 | tf_op jit(solution)/shard_map/ppermute | solution.py:110
  9.8 2.7 %collective-permute-start.3 = (bf16[128,256]{1,0:T(8,128)(2,1)S(1)}, bf16[128,256]{1,0:T(8,128)(2,1)S(1)}, u32[]{:S(2)}, u32[]{:S(2)}) collective-permute-start(bf16[128,256]{1,0:T(8,128)(2,1)S(1)} %get-tuple-element.31), channel_id=1, source_target_pairs={{0,17},{1,16},{8,25},{9,24},{16,1},{17,0},{24,9},{25,8},{2,19},{3,... | collective-permute-start | bytes 196616 | tf_op jit(solution)/shard_map/ppermute | solution.py:107
  12.5 0.0 collective-permute-done.2.refs_1_.refs_5_
  12.5 0.3 collective-permute-done.6.refs_3_
  12.8 0.0 collective-permute-done.1.refs_0_.refs_4_
  12.8 0.0 collective-permute-done.q
  12.8 1.3 %attend.3 = (bf16[32,2048]{1,0:T(8,128)(2,1)S(1)}, bf16[32,2048]{1,0:T(8,128)(2,1)S(1)}, bf16[32,2048]{1,0:T(8,128)(2,1)S(1)}) custom-call(bf16[1,128,4096]{2,1,0:T(8,128)(2,1)S(1)} %collective-permute-done.q, f32[128,512]{1,0:T(8,128)S(1)} %bias.1, bf16[2,128,256]{2,1,0:T(8,128)(2,1)S(1)} %collective-permute-done.1.refs_0_.refs_4_, ...), custom_call_target="tpu_custom_call" | custom-call | flops 402653184 | bytes 786432 | tf_op jit(solution)/shard_map/attend/pallas_call | solution.py:145
  14.1 2.4 %collective-permute-start.7 = (bf16[32,2048]{1,0:T(8,128)(2,1)S(1)}, bf16[32,2048]{1,0:T(8,128)(2,1)S(1)}, u32[]{:S(2)}, u32[]{:S(2)}) collective-permute-start(bf16[32,2048]{1,0:T(8,128)(2,1)S(1)} %get-tuple-element.22), channel_id=1, source_target_pairs={{0,6},{2,4},{4,2},{6,0},{1,7},{3,5},{5,3},{7,1},{8,14},{10,12},{12... | collective-permute-start | bytes 393224 | tf_op jit(solution)/shard_map/ppermute | solution.py:170
  16.5 0.0 collective-permute-done.3.refs_2_.refs_6_
  16.5 1.4 %collective-permute-start.4 = (bf16[128,256]{1,0:T(8,128)(2,1)S(1)}, bf16[128,256]{1,0:T(8,128)(2,1)S(1)}, u32[]{:S(2)}, u32[]{:S(2)}) collective-permute-start(bf16[128,256]{1,0:T(8,128)(2,1)S(1)} %collective-permute-done.3.refs_2_.refs_6_), channel_id=1, source_target_pairs={{0,8},{8,0},{16,24},{24,16},{1,9},{9,1},{17,25},{25,17},{2,10},{10... | collective-permute-start | bytes 196616 | tf_op jit(solution)/shard_map/ppermute | solution.py:110
  17.9 0.5 %collective-permute-start.11 = (bf16[32,2048]{1,0:T(8,128)(2,1)S(1)}, bf16[32,2048]{1,0:T(8,128)(2,1)S(1)}, u32[]{:S(2)}, u32[]{:S(2)}) collective-permute-start(bf16[32,2048]{1,0:T(8,128)(2,1)S(1)} %get-tuple-element.26), channel_id=1, source_target_pairs={{0,2},{2,0},{4,6},{6,4},{1,3},{3,1},{5,7},{7,5},{8,10},{10,8},{12,... | collective-permute-start | bytes 393224 | tf_op jit(solution)/shard_map/ppermute | solution.py:170
  18.4 1.0 %collective-permute-start.12 = (bf16[32,2048]{1,0:T(8,128)(2,1)S(1)}, bf16[32,2048]{1,0:T(8,128)(2,1)S(1)}, u32[]{:S(2)}, u32[]{:S(2)}) collective-permute-start(bf16[32,2048]{1,0:T(8,128)(2,1)S(1)} %get-tuple-element.20.refs_4_), channel_id=1, source_target_pairs={{0,4},{2,6},{4,0},{6,2},{1,5},{3,7},{5,1},{7,3},{8,12},{10,14},{12... | collective-permute-start | bytes 393224 | tf_op jit(solution)/shard_map/ppermute | solution.py:170
  19.4 1.4 %collective-permute-done.4.refs_3_.refs_7_ = bf16[128,256]{1,0:T(8,128)(2,1)S(1)} collective-permute-done((bf16[128,256]{1,0:T(8,128)(2,1)S(1)}, bf16[128,256]{1,0:T(8,128)(2,1)S(1)}, u32[]{:S(2)}, u32[]{:S(2)}) %collective-permute-start.4) | collective-permute-done | bytes 65568 | tf_op jit(solution)/shard_map/ppermute | solution.py:110
  20.8 1.3 %attend.4 = (bf16[32,2048]{1,0:T(8,128)(2,1)S(1)}, bf16[32,2048]{1,0:T(8,128)(2,1)S(1)}, bf16[32,2048]{1,0:T(8,128)(2,1)S(1)}) custom-call(bf16[1,128,4096]{2,1,0:T(8,128)(2,1)S(1)} %collective-permute-done.q, f32[128,512]{1,0:T(8,128)S(1)} %bias.1, bf16[2,128,256]{2,1,0:T(8,128)(2,1)S(1)} %collective-permute-done.1.refs_0_.refs_4_, ...), custom_call_target="tpu_custom_call" | custom-call | flops 402653184 | bytes 786432 | tf_op jit(solution)/shard_map/attend/pallas_call | solution.py:145
  22.1 1.2 %collective-permute-start.10 = (bf16[32,2048]{1,0:T(8,128)(2,1)S(1)}, bf16[32,2048]{1,0:T(8,128)(2,1)S(1)}, u32[]{:S(2)}, u32[]{:S(2)}) collective-permute-start(bf16[32,2048]{1,0:T(8,128)(2,1)S(1)} %get-tuple-element.25), channel_id=1, source_target_pairs={{0,6},{2,4},{4,2},{6,0},{1,7},{3,5},{5,3},{7,1},{8,14},{10,12},{12... | collective-permute-start | bytes 393224 | tf_op jit(solution)/shard_map/ppermute | solution.py:170
  23.3 1.4 %collective-permute-start.9 = (bf16[32,2048]{1,0:T(8,128)(2,1)S(1)}, bf16[32,2048]{1,0:T(8,128)(2,1)S(1)}, u32[]{:S(2)}, u32[]{:S(2)}) collective-permute-start(bf16[32,2048]{1,0:T(8,128)(2,1)S(1)} %get-tuple-element.24.refs_8_), channel_id=1, source_target_pairs={{0,4},{2,6},{4,0},{6,2},{1,5},{3,7},{5,1},{7,3},{8,12},{10,14},{12... | collective-permute-start | bytes 393224 | tf_op jit(solution)/shard_map/ppermute | solution.py:170
  24.8 0.0 collective-permute-done.7.refs_0_
  24.8 0.9 %collective-permute-start.8 = (bf16[32,2048]{1,0:T(8,128)(2,1)S(1)}, bf16[32,2048]{1,0:T(8,128)(2,1)S(1)}, u32[]{:S(2)}, u32[]{:S(2)}) collective-permute-start(bf16[32,2048]{1,0:T(8,128)(2,1)S(1)} %get-tuple-element.23), channel_id=1, source_target_pairs={{0,2},{2,0},{4,6},{6,4},{1,3},{3,1},{5,7},{7,5},{8,10},{10,8},{12,... | collective-permute-start | bytes 393224 | tf_op jit(solution)/shard_map/ppermute | solution.py:170
  25.7 1.0 %attend.5 = (bf16[32,2048]{1,0:T(8,128)(2,1)S(1)}, bf16[32,2048]{1,0:T(8,128)(2,1)S(1)}) custom-call(bf16[1,128,4096]{2,1,0:T(8,128)(2,1)S(1)} %collective-permute-done.q, f32[128,512]{1,0:T(8,128)S(1)} %bias.1, bf16[2,128,256]{2,1,0:T(8,128)(2,1)S(1)} %collective-permute-done.1.refs_0_.refs_4_, ...), custom_call_target="tpu_custom_call" | custom-call | flops 268435456 | bytes 524288 | tf_op jit(solution)/shard_map/attend/pallas_call | solution.py:145
  26.7 0.0 collective-permute-done.11.refs_1_
  26.7 0.0 collective-permute-done.12.refs_2_
  26.7 0.9 %place.3.refs_1_ = bf16[1,32,16384]{2,1,0:T(8,128)(2,1)} custom-call(bf16[32,2048]{1,0:T(8,128)(2,1)S(1)} %collective-permute-done.7.refs_0_, bf16[32,2048]{1,0:T(8,128)(2,1)S(1)} %collective-permute-done.11.refs_1_, bf16[32,2048]{1,0:T(8,128)(2,1)S(1)} %collective-permute-done.12.refs_2_, bf16[32,2048]{1,0:T(8,128)(2,1)S(1)} %get-tuple-element.27.refs_3_, ...), custom_call_target="tpu_custom_call" | custom-call | tf_op jit(solution)/shard_map/place/pallas_call | solution.py:179
  27.6 1.2 %collective-permute-done.10.refs_0_ = bf16[32,2048]{1,0:T(8,128)(2,1)S(1)} collective-permute-done((bf16[32,2048]{1,0:T(8,128)(2,1)S(1)}, bf16[32,2048]{1,0:T(8,128)(2,1)S(1)}, u32[]{:S(2)}, u32[]{:S(2)}) %collective-permute-start.10) | collective-permute-done | bytes 131104 | tf_op jit(solution)/shard_map/ppermute | solution.py:170
  28.8 0.7 %place.4.refs_2_ = bf16[1,32,16384]{2,1,0:T(8,128)(2,1)} custom-call(bf16[32,2048]{1,0:T(8,128)(2,1)S(1)} %collective-permute-done.10.refs_0_, bf16[1,32,16384]{2,1,0:T(8,128)(2,1)} %place.3.refs_1_), custom_call_target="tpu_custom_call", output_to_operand_aliasing={{}: (1, {})} | custom-call | tf_op jit(solution)/shard_map/place/pallas_call | solution.py:179
  29.4 1.3 %collective-permute-done.9.refs_1_ = bf16[32,2048]{1,0:T(8,128)(2,1)S(1)} collective-permute-done((bf16[32,2048]{1,0:T(8,128)(2,1)S(1)}, bf16[32,2048]{1,0:T(8,128)(2,1)S(1)}, u32[]{:S(2)}, u32[]{:S(2)}) %collective-permute-start.9) | collective-permute-done | bytes 131104 | tf_op jit(solution)/shard_map/ppermute | solution.py:170
  30.8 0.3 collective-permute-done.8.refs_0_
  31.1 0.7 %place.5 = bf16[1,32,16384]{2,1,0:T(8,128)(2,1)} custom-call(bf16[32,2048]{1,0:T(8,128)(2,1)S(1)} %collective-permute-done.8.refs_0_, bf16[32,2048]{1,0:T(8,128)(2,1)S(1)} %collective-permute-done.9.refs_1_, bf16[1,32,16384]{2,1,0:T(8,128)(2,1)} %place.4.refs_2_), custom_call_target="tpu_custom_call", output_to_operand_aliasing={{}: (2, {})} | custom-call | tf_op jit(solution)/shard_map/place/pallas_call | solution.py:179
  (3 shorter events, 0.0 us)
Async XLA Ops:
  0.0 12.8 %collective-permute-start = (bf16[1,128,4096]{2,1,0:T(8,128)(2,1)}, bf16[1,128,4096]{2,1,0:T(8,128)(2,1)S(1)}, u32[]{:S(2)}, u32[]{:S(2)}) collective-permute-start(bf16[1,128,4096]{2,1,0:T(8,128)(2,1)} %param.5), channel_id=1, source_target_pairs={{0,1},{1,0},{8,9},{9,8},{16,17},{17,16},{24,25},{25,24},{2,3},{3,2... | collective-permute-start | bytes 3145736 | tf_op jit(solution)/shard_map/ppermute | solution.py:107
  1.3 7.3 %collective-permute-start.5 = (bf16[128,256]{1,0:T(8,128)(2,1)S(1)}, bf16[128,256]{1,0:T(8,128)(2,1)S(1)}, u32[]{:S(2)}, u32[]{:S(2)}) collective-permute-start(bf16[128,256]{1,0:T(8,128)(2,1)S(1)} %get-tuple-element.29), channel_id=1, source_target_pairs={{0,17},{1,16},{8,25},{9,24},{16,1},{17,0},{24,9},{25,8},{2,19},{3,... | collective-permute-start | bytes 196616 | tf_op jit(solution)/shard_map/ppermute | solution.py:107
  5.1 1.3 %copy-start = (s32[512]{0:T(512)S(1)}, s32[512]{0:T(512)}, u32[]{:S(2)}) copy-start(s32[512]{0:T(512)} %param.8) | copy-start | bytes 6148
  5.1 1.3 %copy-start.1 = (s32[16]{0:T(128)S(1)}, s32[16]{0:T(128)}, u32[]{:S(2)}) copy-start(s32[16]{0:T(128)} %lengths.1) | copy-start | bytes 196
  5.1 7.4 %collective-permute-start.2 = (bf16[2,128,256]{2,1,0:T(8,128)(2,1)S(1)}, bf16[2,128,256]{2,1,0:T(8,128)(2,1)S(1)}, u32[]{:S(2)}, u32[]{:S(2)}) collective-permute-start(bf16[2,128,256]{2,1,0:T(8,128)(2,1)S(1)} %pad_maximum_fusion), channel_id=1, source_target_pairs={{0,9},{1,8},{8,1},{9,0},{16,25},{17,24},{24,17},{25,16},{2,11},{3,... | collective-permute-start | bytes 393224 | tf_op jit(solution)/shard_map/ppermute | solution.py:107
  7.0 5.8 %collective-permute-start.1 = (bf16[2,128,256]{2,1,0:T(8,128)(2,1)S(1)}, bf16[2,128,256]{2,1,0:T(8,128)(2,1)S(1)}, u32[]{:S(2)}, u32[]{:S(2)}) collective-permute-start(bf16[2,128,256]{2,1,0:T(8,128)(2,1)S(1)} %pad_maximum_fusion), channel_id=1, source_target_pairs={{0,1},{1,0},{8,9},{9,8},{16,17},{17,16},{24,25},{25,24},{2,3},{3,2... | collective-permute-start | bytes 393224 | tf_op jit(solution)/shard_map/ppermute | solution.py:107
  8.6 4.3 %collective-permute-start.6 = (bf16[128,256]{1,0:T(8,128)(2,1)S(1)}, bf16[128,256]{1,0:T(8,128)(2,1)S(1)}, u32[]{:S(2)}, u32[]{:S(2)}) collective-permute-start(bf16[128,256]{1,0:T(8,128)(2,1)S(1)} %collective-permute-done.5.refs_2_), channel_id=1, source_target_pairs={{0,8},{8,0},{16,24},{24,16},{1,9},{9,1},{17,25},{25,17},{2,10},{10... | collective-permute-start | bytes 196616 | tf_op jit(solution)/shard_map/ppermute | solution.py:110
  9.8 6.7 %collective-permute-start.3 = (bf16[128,256]{1,0:T(8,128)(2,1)S(1)}, bf16[128,256]{1,0:T(8,128)(2,1)S(1)}, u32[]{:S(2)}, u32[]{:S(2)}) collective-permute-start(bf16[128,256]{1,0:T(8,128)(2,1)S(1)} %get-tuple-element.31), channel_id=1, source_target_pairs={{0,17},{1,16},{8,25},{9,24},{16,1},{17,0},{24,9},{25,8},{2,19},{3,... | collective-permute-start | bytes 196616 | tf_op jit(solution)/shard_map/ppermute | solution.py:107
  14.1 10.6 %collective-permute-start.7 = (bf16[32,2048]{1,0:T(8,128)(2,1)S(1)}, bf16[32,2048]{1,0:T(8,128)(2,1)S(1)}, u32[]{:S(2)}, u32[]{:S(2)}) collective-permute-start(bf16[32,2048]{1,0:T(8,128)(2,1)S(1)} %get-tuple-element.22), channel_id=1, source_target_pairs={{0,6},{2,4},{4,2},{6,0},{1,7},{3,5},{5,3},{7,1},{8,14},{10,12},{12... | collective-permute-start | bytes 393224 | tf_op jit(solution)/shard_map/ppermute | solution.py:170
  16.5 4.3 %collective-permute-start.4 = (bf16[128,256]{1,0:T(8,128)(2,1)S(1)}, bf16[128,256]{1,0:T(8,128)(2,1)S(1)}, u32[]{:S(2)}, u32[]{:S(2)}) collective-permute-start(bf16[128,256]{1,0:T(8,128)(2,1)S(1)} %collective-permute-done.3.refs_2_.refs_6_), channel_id=1, source_target_pairs={{0,8},{8,0},{16,24},{24,16},{1,9},{9,1},{17,25},{25,17},{2,10},{10... | collective-permute-start | bytes 196616 | tf_op jit(solution)/shard_map/ppermute | solution.py:110
  17.9 8.8 %collective-permute-start.11 = (bf16[32,2048]{1,0:T(8,128)(2,1)S(1)}, bf16[32,2048]{1,0:T(8,128)(2,1)S(1)}, u32[]{:S(2)}, u32[]{:S(2)}) collective-permute-start(bf16[32,2048]{1,0:T(8,128)(2,1)S(1)} %get-tuple-element.26), channel_id=1, source_target_pairs={{0,2},{2,0},{4,6},{6,4},{1,3},{3,1},{5,7},{7,5},{8,10},{10,8},{12,... | collective-permute-start | bytes 393224 | tf_op jit(solution)/shard_map/ppermute | solution.py:170
  18.4 8.3 %collective-permute-start.12 = (bf16[32,2048]{1,0:T(8,128)(2,1)S(1)}, bf16[32,2048]{1,0:T(8,128)(2,1)S(1)}, u32[]{:S(2)}, u32[]{:S(2)}) collective-permute-start(bf16[32,2048]{1,0:T(8,128)(2,1)S(1)} %get-tuple-element.20.refs_4_), channel_id=1, source_target_pairs={{0,4},{2,6},{4,0},{6,2},{1,5},{3,7},{5,1},{7,3},{8,12},{10,14},{12... | collective-permute-start | bytes 393224 | tf_op jit(solution)/shard_map/ppermute | solution.py:170
  22.1 6.6 %collective-permute-start.10 = (bf16[32,2048]{1,0:T(8,128)(2,1)S(1)}, bf16[32,2048]{1,0:T(8,128)(2,1)S(1)}, u32[]{:S(2)}, u32[]{:S(2)}) collective-permute-start(bf16[32,2048]{1,0:T(8,128)(2,1)S(1)} %get-tuple-element.25), channel_id=1, source_target_pairs={{0,6},{2,4},{4,2},{6,0},{1,7},{3,5},{5,3},{7,1},{8,14},{10,12},{12... | collective-permute-start | bytes 393224 | tf_op jit(solution)/shard_map/ppermute | solution.py:170
  23.3 7.4 %collective-permute-start.9 = (bf16[32,2048]{1,0:T(8,128)(2,1)S(1)}, bf16[32,2048]{1,0:T(8,128)(2,1)S(1)}, u32[]{:S(2)}, u32[]{:S(2)}) collective-permute-start(bf16[32,2048]{1,0:T(8,128)(2,1)S(1)} %get-tuple-element.24.refs_8_), channel_id=1, source_target_pairs={{0,4},{2,6},{4,0},{6,2},{1,5},{3,7},{5,1},{7,3},{8,12},{10,14},{12... | collective-permute-start | bytes 393224 | tf_op jit(solution)/shard_map/ppermute | solution.py:170
  24.8 6.3 %collective-permute-start.8 = (bf16[32,2048]{1,0:T(8,128)(2,1)S(1)}, bf16[32,2048]{1,0:T(8,128)(2,1)S(1)}, u32[]{:S(2)}, u32[]{:S(2)}) collective-permute-start(bf16[32,2048]{1,0:T(8,128)(2,1)S(1)} %get-tuple-element.23), channel_id=1, source_target_pairs={{0,2},{2,0},{4,6},{6,4},{1,3},{3,1},{5,7},{7,5},{8,10},{10,8},{12,... | collective-permute-start | bytes 393224 | tf_op jit(solution)/shard_map/ppermute | solution.py:170

commit v7 on v5

--- a/solution.py
+++ b/solution.py
@@ -116,11 +116,11 @@
     bias = pl.pallas_call(
         bias_kernel,
         out_shape=jax.ShapeDtypeStruct((rows, rows * shards), jnp.float32),
-        in_specs=[smem, vmem],
+        in_specs=[smem, vmem, anywhere],
         out_specs=vmem,
         compiler_params=params,
         name="bias",
-    )(doc_lengths, order.reshape(shards, rows))
+    )(doc_lengths, order.reshape(shards, rows), rows_q)
 
     packed = [
         jnp.concatenate([kv[0, :, g * HD : (g + 1) * HD] for kv in (keys, values)], axis=1)
@@ -129,11 +129,14 @@
     stacked = jnp.stack(packed)
     step = shards // 2
     blocks = {step: [handed(block, step) for block in packed]}
-    own = handed(after(stacked, bias), 0)
+    own = handed(stacked, 0)
     while step > 1:
         step //= 2
         for other in sorted(blocks):
-            blocks[other ^ step] = [passed(after(block, bias), step) for block in blocks[other]]
+            ahead = [handed(packed[0], other ^ step)] if len(blocks[other]) > 1 else []
+            blocks[other ^ step] = ahead + [
+                passed(after(block, bias), step) for block in blocks[other][len(ahead) :]
+            ]
         blocks[step] = [handed(stacked, step)]
     kvs = [
         [own] + [blocks[step][g % len(blocks[step])] for step in range(1, shards)]

time: 31.5 us -> 32 us (1.016)
  waiting for transfers between devices: 3.98 us -> 6.83 us
  starting transfers between devices: 19.5 us -> 17.1 us
    ppermute x5 -> x6, waiting for transfers between devices: 0.96 us -> 4.21 us  [handed(): return lax.ppermute(value, ('ctx', 'section'), pairs)]
    ppermute x5 -> x6, starting transfers between devices: 8.78 us -> 7.54 us  [handed(): return lax.ppermute(value, ('ctx', 'section'), pairs)]
    ppermute x6, starting transfers between devices: 8.12 us -> 7.17 us  [local(): lax.ppermute(piece, 'head', [(h, h ^ d) for h in range(heads)])]
    ppermute x2 -> x1, starting transfers between devices: 2.57 us -> 2.4 us  [passed(): return lax.ppermute(value, 'ctx', [(c, c ^ step) for c in range(shards)])]
  transfers between devices with their start and end apart: 13 -> 13, of which waited for: 4 -> 7; matrix products, arithmetic and copies ran while one was open for 3% -> 3% of each run, Pallas kernels for 20% -> 20%
where the time goes in v7:
time: 32 us; the launch traced here: 31.9 us
  starting transfers between devices  17.1 us (53%)
  Pallas kernels  6.97 us (22%)
  waiting for transfers between devices  6.83 us (21%)
  local copies, waits for them, and re-layouts  0.82 us (3%)
    ppermute x6, starting transfers between devices, handed(): return lax.ppermute(value, ('ctx', 'section'), pairs)  7.54 us
    ppermute x6, starting transfers between devices, local(): lax.ppermute(piece, 'head', [(h, h ^ d) for h in range(heads)])  7.17 us
    ppermute x6, waiting for transfers between devices, handed(): return lax.ppermute(value, ('ctx', 'section'), pairs)  4.21 us
    pallas_call x4, Pallas kernels, attend(): pl.pallas_call(functools.partial(attend_kernel, LOG2E / HD ** 0.5, slots,...  4.07 us
    ppermute x6, waiting for transfers between devices, local(): lax.ppermute(piece, 'head', [(h, h ^ d) for h in range(heads)])  2.5 us
    ppermute x1, starting transfers between devices, passed(): return lax.ppermute(value, 'ctx', [(c, c ^ step) for c in range(shards)])  2.4 us
    pallas_call x3, Pallas kernels, local(): pl.pallas_call(functools.partial(place_kernel, slots, groups), out_shape=...  2.25 us
    squeeze x1, local copies, waits for them, and re-layouts, local(): kv[0, :, g * HD:(g + 1) * HD]  0.82 us
  transfers between devices with their start and end apart: 13, of which 7 were waited for; matrix products, arithmetic and copies ran while one was open for 3% of the time, Pallas kernels for 20%

profile of v7, /device:TPU:0, one launch (start us, length us, event | category | flops | bytes accessed | tf_op | source)
XLA Modules:
  0.0 31.9 jit_solution(9128358619043749074)
XLA Ops:
  0.0 0.5 %collective-permute-start = (bf16[1,128,4096]{2,1,0:T(8,128)(2,1)}, bf16[1,128,4096]{2,1,0:T(8,128)(2,1)S(1)}, u32[]{:S(2)}, u32[]{:S(2)}) collective-permute-start(bf16[1,128,4096]{2,1,0:T(8,128)(2,1)} %param.5), channel_id=1, source_target_pairs={{0,1},{1,0},{8,9},{9,8},{16,17},{17,16},{24,25},{25,24},{2,3},{3,2... | collective-permute-start | bytes 3145736 | tf_op jit(solution)/shard_map/ppermute | solution.py:107
  0.5 0.8 %slice_bitcast_fusion.2 = (bf16[128,128]{1,0:T(8,128)(2,1)S(1)}, bf16[128,128]{1,0:T(8,128)(2,1)S(1)}, bf16[128,128]{1,0:T(8,128)(2,1)S(1)}, bf16[128,128]{1,0:T(8,128)(2,1)S(1)}) fusion(bf16[1,128,256]{2,1,0:T(8,128)(2,1)} %param.7, bf16[1,128,256]{2,1,0:T(8,128)(2,1)} %param.6), kind=kLoop, calls=%fused_computation.5 | loop fusion | bytes 262144 | tf_op jit(solution)/shard_map/squeeze | solution.py:126
  1.3 2.8 %collective-permute-start.2 = (bf16[2,128,256]{2,1,0:T(8,128)(2,1)S(1)}, bf16[2,128,256]{2,1,0:T(8,128)(2,1)S(1)}, u32[]{:S(2)}, u32[]{:S(2)}) collective-permute-start(bf16[2,128,256]{2,1,0:T(8,128)(2,1)S(1)} %pad_maximum_fusion), channel_id=1, source_target_pairs={{0,9},{1,8},{8,1},{9,0},{16,25},{17,24},{24,17},{25,16},{2,11},{3,... | collective-permute-start | bytes 393224 | tf_op jit(solution)/shard_map/ppermute | solution.py:107
  4.1 0.0 collective-permute-start.1
  4.1 0.0 copy-start
  4.1 2.7 %collective-permute-start.5 = (bf16[128,256]{1,0:T(8,128)(2,1)S(1)}, bf16[128,256]{1,0:T(8,128)(2,1)S(1)}, u32[]{:S(2)}, u32[]{:S(2)}) collective-permute-start(bf16[128,256]{1,0:T(8,128)(2,1)S(1)} %get-tuple-element.23), channel_id=1, source_target_pairs={{0,17},{1,16},{8,25},{9,24},{16,1},{17,0},{24,9},{25,8},{2,19},{3,... | collective-permute-start | bytes 196616 | tf_op jit(solution)/shard_map/ppermute | solution.py:107
  6.8 0.0 collective-permute-start.6
  6.8 0.0 collective-permute-done.refs_0_.q
  6.8 0.0 copy-start.1
  6.8 1.6 %collective-permute-start.3 = (bf16[128,256]{1,0:T(8,128)(2,1)S(1)}, bf16[128,256]{1,0:T(8,128)(2,1)S(1)}, u32[]{:S(2)}, u32[]{:S(2)}) collective-permute-start(bf16[128,256]{1,0:T(8,128)(2,1)S(1)} %get-tuple-element.25), channel_id=1, source_target_pairs={{0,17},{1,16},{8,25},{9,24},{16,1},{17,0},{24,9},{25,8},{2,19},{3,... | collective-permute-start | bytes 196616 | tf_op jit(solution)/shard_map/ppermute | solution.py:107
  8.4 0.0 copy-done
  8.4 0.0 copy-done.1
  8.4 0.7 %bias.1 = f32[128,512]{1,0:T(8,128)S(1)} custom-call(s32[16]{0:T(128)S(1)} %copy-done.1, s32[4,128]{1,0:T(4,128)S(1)} %bitcast.13, bf16[1,128,4096]{2,1,0:T(8,128)(2,1)S(1)} %collective-permute-done.refs_0_.q), custom_call_target="tpu_custom_call" | custom-call | tf_op jit(solution)/shard_map/bias/pallas_call | solution.py:116
  9.1 0.2 collective-permute-done.5.refs_2_
  9.3 3.7 %collective-permute-done.6.refs_3_ = bf16[128,256]{1,0:T(8,128)(2,1)S(1)} collective-permute-done((bf16[128,256]{1,0:T(8,128)(2,1)S(1)}, bf16[128,256]{1,0:T(8,128)(2,1)S(1)}, u32[]{:S(2)}, u32[]{:S(2)}) %collective-permute-start.6) | collective-permute-done | bytes 65568 | tf_op jit(solution)/shard_map/ppermute | solution.py:107
  13.0 0.0 collective-permute-done.2.refs_1_.refs_5_
  13.0 0.0 collective-permute-done.1.refs_0_.refs_4_
  13.0 0.7 %attend.4.refs_4_ = bf16[32,2048]{1,0:T(8,128)(2,1)S(1)} custom-call(bf16[1,128,4096]{2,1,0:T(8,128)(2,1)S(1)} %collective-permute-done.refs_0_.q, f32[128,512]{1,0:T(8,128)S(1)} %bias.1, bf16[2,128,256]{2,1,0:T(8,128)(2,1)S(1)} %collective-permute-done.1.refs_0_.refs_4_, bf16[2,128,256]{2,1,0:T(8,128)(2,1)S(1)} %collective-permute-done.2.refs_1_.refs_5_, ...), custom_call_target="tpu_custom_call" | custom-call | flops 134217728 | bytes 262144 | tf_op jit(solution)/shard_map/attend/pallas_call | solution.py:148
  13.7 2.5 %collective-permute-start.7 = (bf16[32,2048]{1,0:T(8,128)(2,1)S(1)}, bf16[32,2048]{1,0:T(8,128)(2,1)S(1)}, u32[]{:S(2)}, u32[]{:S(2)}) collective-permute-start(bf16[32,2048]{1,0:T(8,128)(2,1)S(1)} %attend.4.refs_4_), channel_id=1, source_target_pairs={{0,6},{2,4},{4,2},{6,0},{1,7},{3,5},{5,3},{7,1},{8,14},{10,12},{12... | collective-permute-start | bytes 393224 | tf_op jit(solution)/shard_map/ppermute | solution.py:173
  16.2 0.3 %collective-permute-done.3.refs_2_.refs_6_ = bf16[128,256]{1,0:T(8,128)(2,1)S(1)} collective-permute-done((bf16[128,256]{1,0:T(8,128)(2,1)S(1)}, bf16[128,256]{1,0:T(8,128)(2,1)S(1)}, u32[]{:S(2)}, u32[]{:S(2)}) %collective-permute-start.3) | collective-permute-done | bytes 65568 | tf_op jit(solution)/shard_map/ppermute | solution.py:107
  16.5 2.4 %collective-permute-start.4 = (bf16[128,256]{1,0:T(8,128)(2,1)S(1)}, bf16[128,256]{1,0:T(8,128)(2,1)S(1)}, u32[]{:S(2)}, u32[]{:S(2)}) collective-permute-start(bf16[128,256]{1,0:T(8,128)(2,1)S(1)} %collective-permute-done.3.refs_2_.refs_6_), channel_id=1, source_target_pairs={{0,8},{8,0},{16,24},{24,16},{1,9},{9,1},{17,25},{25,17},{2,10},{10... | collective-permute-start | bytes 196616 | tf_op jit(solution)/shard_map/ppermute | solution.py:110
  18.9 1.0 %attend.5 = (bf16[32,2048]{1,0:T(8,128)(2,1)S(1)}, bf16[32,2048]{1,0:T(8,128)(2,1)S(1)}) custom-call(bf16[1,128,4096]{2,1,0:T(8,128)(2,1)S(1)} %collective-permute-done.refs_0_.q, f32[128,512]{1,0:T(8,128)S(1)} %bias.1, bf16[2,128,256]{2,1,0:T(8,128)(2,1)S(1)} %collective-permute-done.1.refs_0_.refs_4_, ...), custom_call_target="tpu_custom_call" | custom-call | flops 268435456 | bytes 524288 | tf_op jit(solution)/shard_map/attend/pallas_call | solution.py:148
  20.0 0.6 %collective-permute-start.11 = (bf16[32,2048]{1,0:T(8,128)(2,1)S(1)}, bf16[32,2048]{1,0:T(8,128)(2,1)S(1)}, u32[]{:S(2)}, u32[]{:S(2)}) collective-permute-start(bf16[32,2048]{1,0:T(8,128)(2,1)S(1)} %get-tuple-element.20), channel_id=1, source_target_pairs={{0,2},{2,0},{4,6},{6,4},{1,3},{3,1},{5,7},{7,5},{8,10},{10,8},{12,... | collective-permute-start | bytes 393224 | tf_op jit(solution)/shard_map/ppermute | solution.py:173
  20.6 0.5 %collective-permute-start.12 = (bf16[32,2048]{1,0:T(8,128)(2,1)S(1)}, bf16[32,2048]{1,0:T(8,128)(2,1)S(1)}, u32[]{:S(2)}, u32[]{:S(2)}) collective-permute-start(bf16[32,2048]{1,0:T(8,128)(2,1)S(1)} %get-tuple-element.15.refs_4_), channel_id=1, source_target_pairs={{0,4},{2,6},{4,0},{6,2},{1,5},{3,7},{5,1},{7,3},{8,12},{10,14},{12... | collective-permute-start | bytes 393224 | tf_op jit(solution)/shard_map/ppermute | solution.py:173
  21.1 0.1 collective-permute-done.4.refs_3_.refs_7_
  21.2 1.3 %attend.6 = (bf16[32,2048]{1,0:T(8,128)(2,1)S(1)}, bf16[32,2048]{1,0:T(8,128)(2,1)S(1)}, bf16[32,2048]{1,0:T(8,128)(2,1)S(1)}) custom-call(bf16[1,128,4096]{2,1,0:T(8,128)(2,1)S(1)} %collective-permute-done.refs_0_.q, f32[128,512]{1,0:T(8,128)S(1)} %bias.1, bf16[2,128,256]{2,1,0:T(8,128)(2,1)S(1)} %collective-permute-done.1.refs_0_.refs_4_, ...), custom_call_target="tpu_custom_call" | custom-call | flops 402653184 | bytes 786432 | tf_op jit(solution)/shard_map/attend/pallas_call | solution.py:148
  22.5 2.4 %collective-permute-start.10 = (bf16[32,2048]{1,0:T(8,128)(2,1)S(1)}, bf16[32,2048]{1,0:T(8,128)(2,1)S(1)}, u32[]{:S(2)}, u32[]{:S(2)}) collective-permute-start(bf16[32,2048]{1,0:T(8,128)(2,1)S(1)} %get-tuple-element.19), channel_id=1, source_target_pairs={{0,6},{2,4},{4,2},{6,0},{1,7},{3,5},{5,3},{7,1},{8,14},{10,12},{12... | collective-permute-start | bytes 393224 | tf_op jit(solution)/shard_map/ppermute | solution.py:173
  24.9 0.5 %collective-permute-start.9 = (bf16[32,2048]{1,0:T(8,128)(2,1)S(1)}, bf16[32,2048]{1,0:T(8,128)(2,1)S(1)}, u32[]{:S(2)}, u32[]{:S(2)}) collective-permute-start(bf16[32,2048]{1,0:T(8,128)(2,1)S(1)} %get-tuple-element.18.refs_8_), channel_id=1, source_target_pairs={{0,4},{2,6},{4,0},{6,2},{1,5},{3,7},{5,1},{7,3},{8,12},{10,14},{12... | collective-permute-start | bytes 393224 | tf_op jit(solution)/shard_map/ppermute | solution.py:173
  25.4 0.0 collective-permute-done.7.refs_0_
  25.4 0.6 %collective-permute-start.8 = (bf16[32,2048]{1,0:T(8,128)(2,1)S(1)}, bf16[32,2048]{1,0:T(8,128)(2,1)S(1)}, u32[]{:S(2)}, u32[]{:S(2)}) collective-permute-start(bf16[32,2048]{1,0:T(8,128)(2,1)S(1)} %get-tuple-element.17), channel_id=1, source_target_pairs={{0,2},{2,0},{4,6},{6,4},{1,3},{3,1},{5,7},{7,5},{8,10},{10,8},{12,... | collective-permute-start | bytes 393224 | tf_op jit(solution)/shard_map/ppermute | solution.py:173
  26.1 1.0 %attend.7 = (bf16[32,2048]{1,0:T(8,128)(2,1)S(1)}, bf16[32,2048]{1,0:T(8,128)(2,1)S(1)}) custom-call(bf16[1,128,4096]{2,1,0:T(8,128)(2,1)S(1)} %collective-permute-done.refs_0_.q, f32[128,512]{1,0:T(8,128)S(1)} %bias.1, bf16[2,128,256]{2,1,0:T(8,128)(2,1)S(1)} %collective-permute-done.1.refs_0_.refs_4_, ...), custom_call_target="tpu_custom_call" | custom-call | flops 268435456 | bytes 524288 | tf_op jit(solution)/shard_map/attend/pallas_call | solution.py:148
  27.1 0.0 collective-permute-done.11.refs_1_
  27.1 0.4 %collective-permute-done.12.refs_2_ = bf16[32,2048]{1,0:T(8,128)(2,1)S(1)} collective-permute-done((bf16[32,2048]{1,0:T(8,128)(2,1)S(1)}, bf16[32,2048]{1,0:T(8,128)(2,1)S(1)}, u32[]{:S(2)}, u32[]{:S(2)}) %collective-permute-start.12) | collective-permute-done | bytes 131104 | tf_op jit(solution)/shard_map/ppermute | solution.py:173
  27.5 0.9 %place.3.refs_1_ = bf16[1,32,16384]{2,1,0:T(8,128)(2,1)} custom-call(bf16[32,2048]{1,0:T(8,128)(2,1)S(1)} %collective-permute-done.7.refs_0_, bf16[32,2048]{1,0:T(8,128)(2,1)S(1)} %collective-permute-done.11.refs_1_, bf16[32,2048]{1,0:T(8,128)(2,1)S(1)} %collective-permute-done.12.refs_2_, bf16[32,2048]{1,0:T(8,128)(2,1)S(1)} %get-tuple-element.21.refs_3_, ...), custom_call_target="tpu_custom_call" | custom-call | tf_op jit(solution)/shard_map/place/pallas_call | solution.py:182
  28.4 1.2 %collective-permute-done.10.refs_0_ = bf16[32,2048]{1,0:T(8,128)(2,1)S(1)} collective-permute-done((bf16[32,2048]{1,0:T(8,128)(2,1)S(1)}, bf16[32,2048]{1,0:T(8,128)(2,1)S(1)}, u32[]{:S(2)}, u32[]{:S(2)}) %collective-permute-start.10) | collective-permute-done | bytes 131104 | tf_op jit(solution)/shard_map/ppermute | solution.py:173
  29.6 0.7 %place.4.refs_2_ = bf16[1,32,16384]{2,1,0:T(8,128)(2,1)} custom-call(bf16[32,2048]{1,0:T(8,128)(2,1)S(1)} %collective-permute-done.10.refs_0_, bf16[1,32,16384]{2,1,0:T(8,128)(2,1)} %place.3.refs_1_), custom_call_target="tpu_custom_call", output_to_operand_aliasing={{}: (1, {})} | custom-call | tf_op jit(solution)/shard_map/place/pallas_call | solution.py:182
  30.2 0.9 %collective-permute-done.9.refs_1_ = bf16[32,2048]{1,0:T(8,128)(2,1)S(1)} collective-permute-done((bf16[32,2048]{1,0:T(8,128)(2,1)S(1)}, bf16[32,2048]{1,0:T(8,128)(2,1)S(1)}, u32[]{:S(2)}, u32[]{:S(2)}) %collective-permute-start.9) | collective-permute-done | bytes 131104 | tf_op jit(solution)/shard_map/ppermute | solution.py:173
  31.1 0.0 collective-permute-done.8.refs_0_
  31.2 0.7 %place.5 = bf16[1,32,16384]{2,1,0:T(8,128)(2,1)} custom-call(bf16[32,2048]{1,0:T(8,128)(2,1)S(1)} %collective-permute-done.8.refs_0_, bf16[32,2048]{1,0:T(8,128)(2,1)S(1)} %collective-permute-done.9.refs_1_, bf16[1,32,16384]{2,1,0:T(8,128)(2,1)} %place.4.refs_2_), custom_call_target="tpu_custom_call", output_to_operand_aliasing={{}: (2, {})} | custom-call | tf_op jit(solution)/shard_map/place/pallas_call | solution.py:182
  (3 shorter events, 0.0 us)
Async XLA Ops:
  0.0 6.8 %collective-permute-start = (bf16[1,128,4096]{2,1,0:T(8,128)(2,1)}, bf16[1,128,4096]{2,1,0:T(8,128)(2,1)S(1)}, u32[]{:S(2)}, u32[]{:S(2)}) collective-permute-start(bf16[1,128,4096]{2,1,0:T(8,128)(2,1)} %param.5), channel_id=1, source_target_pairs={{0,1},{1,0},{8,9},{9,8},{16,17},{17,16},{24,25},{25,24},{2,3},{3,2... | collective-permute-start | bytes 3145736 | tf_op jit(solution)/shard_map/ppermute | solution.py:107
  1.3 11.7 %collective-permute-start.2 = (bf16[2,128,256]{2,1,0:T(8,128)(2,1)S(1)}, bf16[2,128,256]{2,1,0:T(8,128)(2,1)S(1)}, u32[]{:S(2)}, u32[]{:S(2)}) collective-permute-start(bf16[2,128,256]{2,1,0:T(8,128)(2,1)S(1)} %pad_maximum_fusion), channel_id=1, source_target_pairs={{0,9},{1,8},{8,1},{9,0},{16,25},{17,24},{24,17},{25,16},{2,11},{3,... | collective-permute-start | bytes 393224 | tf_op jit(solution)/shard_map/ppermute | solution.py:107
  4.1 8.9 %collective-permute-start.1 = (bf16[2,128,256]{2,1,0:T(8,128)(2,1)S(1)}, bf16[2,128,256]{2,1,0:T(8,128)(2,1)S(1)}, u32[]{:S(2)}, u32[]{:S(2)}) collective-permute-start(bf16[2,128,256]{2,1,0:T(8,128)(2,1)S(1)} %pad_maximum_fusion), channel_id=1, source_target_pairs={{0,1},{1,0},{8,9},{9,8},{16,17},{17,16},{24,25},{25,24},{2,3},{3,2... | collective-permute-start | bytes 393224 | tf_op jit(solution)/shard_map/ppermute | solution.py:107
  4.1 4.3 %copy-start = (s32[512]{0:T(512)S(1)}, s32[512]{0:T(512)}, u32[]{:S(2)}) copy-start(s32[512]{0:T(512)} %param.8) | copy-start | bytes 6148
  4.1 5.2 %collective-permute-start.5 = (bf16[128,256]{1,0:T(8,128)(2,1)S(1)}, bf16[128,256]{1,0:T(8,128)(2,1)S(1)}, u32[]{:S(2)}, u32[]{:S(2)}) collective-permute-start(bf16[128,256]{1,0:T(8,128)(2,1)S(1)} %get-tuple-element.23), channel_id=1, source_target_pairs={{0,17},{1,16},{8,25},{9,24},{16,1},{17,0},{24,9},{25,8},{2,19},{3,... | collective-permute-start | bytes 196616 | tf_op jit(solution)/shard_map/ppermute | solution.py:107
  6.8 6.2 %collective-permute-start.6 = (bf16[128,256]{1,0:T(8,128)(2,1)S(1)}, bf16[128,256]{1,0:T(8,128)(2,1)S(1)}, u32[]{:S(2)}, u32[]{:S(2)}) collective-permute-start(bf16[128,256]{1,0:T(8,128)(2,1)S(1)} %get-tuple-element.23), channel_id=1, source_target_pairs={{0,25},{1,24},{8,17},{9,16},{16,9},{17,8},{24,1},{25,0},{2,27},{3,... | collective-permute-start | bytes 196616 | tf_op jit(solution)/shard_map/ppermute | solution.py:107
  6.8 1.6 %copy-start.1 = (s32[16]{0:T(128)S(1)}, s32[16]{0:T(128)}, u32[]{:S(2)}) copy-start(s32[16]{0:T(128)} %lengths.1) | copy-start | bytes 196
  6.8 9.7 %collective-permute-start.3 = (bf16[128,256]{1,0:T(8,128)(2,1)S(1)}, bf16[128,256]{1,0:T(8,128)(2,1)S(1)}, u32[]{:S(2)}, u32[]{:S(2)}) collective-permute-start(bf16[128,256]{1,0:T(8,128)(2,1)S(1)} %get-tuple-element.25), channel_id=1, source_target_pairs={{0,17},{1,16},{8,25},{9,24},{16,1},{17,0},{24,9},{25,8},{2,19},{3,... | collective-permute-start | bytes 196616 | tf_op jit(solution)/shard_map/ppermute | solution.py:107
  13.7 11.7 %collective-permute-start.7 = (bf16[32,2048]{1,0:T(8,128)(2,1)S(1)}, bf16[32,2048]{1,0:T(8,128)(2,1)S(1)}, u32[]{:S(2)}, u32[]{:S(2)}) collective-permute-start(bf16[32,2048]{1,0:T(8,128)(2,1)S(1)} %attend.4.refs_4_), channel_id=1, source_target_pairs={{0,6},{2,4},{4,2},{6,0},{1,7},{3,5},{5,3},{7,1},{8,14},{10,12},{12... | collective-permute-start | bytes 393224 | tf_op jit(solution)/shard_map/ppermute | solution.py:173
  16.5 4.6 %collective-permute-start.4 = (bf16[128,256]{1,0:T(8,128)(2,1)S(1)}, bf16[128,256]{1,0:T(8,128)(2,1)S(1)}, u32[]{:S(2)}, u32[]{:S(2)}) collective-permute-start(bf16[128,256]{1,0:T(8,128)(2,1)S(1)} %collective-permute-done.3.refs_2_.refs_6_), channel_id=1, source_target_pairs={{0,8},{8,0},{16,24},{24,16},{1,9},{9,1},{17,25},{25,17},{2,10},{10... | collective-permute-start | bytes 196616 | tf_op jit(solution)/shard_map/ppermute | solution.py:110
  20.0 7.1 %collective-permute-start.11 = (bf16[32,2048]{1,0:T(8,128)(2,1)S(1)}, bf16[32,2048]{1,0:T(8,128)(2,1)S(1)}, u32[]{:S(2)}, u32[]{:S(2)}) collective-permute-start(bf16[32,2048]{1,0:T(8,128)(2,1)S(1)} %get-tuple-element.20), channel_id=1, source_target_pairs={{0,2},{2,0},{4,6},{6,4},{1,3},{3,1},{5,7},{7,5},{8,10},{10,8},{12,... | collective-permute-start | bytes 393224 | tf_op jit(solution)/shard_map/ppermute | solution.py:173
  20.6 6.9 %collective-permute-start.12 = (bf16[32,2048]{1,0:T(8,128)(2,1)S(1)}, bf16[32,2048]{1,0:T(8,128)(2,1)S(1)}, u32[]{:S(2)}, u32[]{:S(2)}) collective-permute-start(bf16[32,2048]{1,0:T(8,128)(2,1)S(1)} %get-tuple-element.15.refs_4_), channel_id=1, source_target_pairs={{0,4},{2,6},{4,0},{6,2},{1,5},{3,7},{5,1},{7,3},{8,12},{10,14},{12... | collective-permute-start | bytes 393224 | tf_op jit(solution)/shard_map/ppermute | solution.py:173
  22.5 7.0 %collective-permute-start.10 = (bf16[32,2048]{1,0:T(8,128)(2,1)S(1)}, bf16[32,2048]{1,0:T(8,128)(2,1)S(1)}, u32[]{:S(2)}, u32[]{:S(2)}) collective-permute-start(bf16[32,2048]{1,0:T(8,128)(2,1)S(1)} %get-tuple-element.19), channel_id=1, source_target_pairs={{0,6},{2,4},{4,2},{6,0},{1,7},{3,5},{5,3},{7,1},{8,14},{10,12},{12... | collective-permute-start | bytes 393224 | tf_op jit(solution)/shard_map/ppermute | solution.py:173
  24.9 6.2 %collective-permute-start.9 = (bf16[32,2048]{1,0:T(8,128)(2,1)S(1)}, bf16[32,2048]{1,0:T(8,128)(2,1)S(1)}, u32[]{:S(2)}, u32[]{:S(2)}) collective-permute-start(bf16[32,2048]{1,0:T(8,128)(2,1)S(1)} %get-tuple-element.18.refs_8_), channel_id=1, source_target_pairs={{0,4},{2,6},{4,0},{6,2},{1,5},{3,7},{5,1},{7,3},{8,12},{10,14},{12... | collective-permute-start | bytes 393224 | tf_op jit(solution)/shard_map/ppermute | solution.py:173
  25.4 5.7 %collective-permute-start.8 = (bf16[32,2048]{1,0:T(8,128)(2,1)S(1)}, bf16[32,2048]{1,0:T(8,128)(2,1)S(1)}, u32[]{:S(2)}, u32[]{:S(2)}) collective-permute-start(bf16[32,2048]{1,0:T(8,128)(2,1)S(1)} %get-tuple-element.17), channel_id=1, source_target_pairs={{0,2},{2,0},{4,6},{6,4},{1,3},{3,1},{5,7},{7,5},{8,10},{10,8},{12,... | collective-permute-start | bytes 393224 | tf_op jit(solution)/shard_map/ppermute | solution.py:173

commit v8 on v5

--- a/solution.py
+++ b/solution.py
@@ -11,7 +11,7 @@
 LOG2E = 1.4426950408889634
 VMEM = pltpu.VMEM
 VMEM_LIMIT = 48 * 1024 * 1024
-BLOCK = 8
+BLOCK = 4
 
 
 def bias_kernel(lengths, order, *refs):

time: 31.5 us -> 31.5 us (level)
  transfers between devices with their start and end apart: 13 -> 13, of which waited for: 4 -> 4; matrix products, arithmetic and copies ran while one was open for 3% -> 3% of each run, Pallas kernels for 20% -> 19%
where the time goes in v8:
time: 31.5 us; the launch traced here: 31.3 us
  starting transfers between devices  19.5 us (62%)
  Pallas kernels  6.79 us (22%)
  waiting for transfers between devices  4.05 us (13%)
  local copies, waits for them, and re-layouts  0.83 us (3%)
    ppermute x5, starting transfers between devices, handed(): return lax.ppermute(value, ('ctx', 'section'), pairs)  8.78 us
    ppermute x6, starting transfers between devices, local(): lax.ppermute(piece, 'head', [(h, h ^ d) for h in range(heads)])  8.14 us
    pallas_call x4, Pallas kernels, attend(): pl.pallas_call(functools.partial(attend_kernel, LOG2E / HD ** 0.5, slots,...  3.87 us
    ppermute x6, waiting for transfers between devices, local(): lax.ppermute(piece, 'head', [(h, h ^ d) for h in range(heads)])  2.79 us
    ppermute x2, starting transfers between devices, passed(): return lax.ppermute(value, 'ctx', [(c, c ^ step) for c in range(shards)])  2.57 us
    pallas_call x3, Pallas kernels, local(): pl.pallas_call(functools.partial(place_kernel, slots, groups), out_shape=...  2.26 us
    ppermute x5, waiting for transfers between devices, handed(): return lax.ppermute(value, ('ctx', 'section'), pairs)  0.96 us
    squeeze x1, local copies, waits for them, and re-layouts, local(): kv[0, :, g * HD:(g + 1) * HD]  0.82 us
  transfers between devices with their start and end apart: 13, of which 4 were waited for; matrix products, arithmetic and copies ran while one was open for 3% of the time, Pallas kernels for 19%

profile of v8, /device:TPU:0, one launch (start us, length us, event | category | flops | bytes accessed | tf_op | source)
XLA Modules:
  0.0 31.3 jit_solution(1887302258557810950)
XLA Ops:
  0.0 0.5 %collective-permute-start = (bf16[1,128,4096]{2,1,0:T(8,128)(2,1)}, bf16[1,128,4096]{2,1,0:T(8,128)(2,1)S(1)}, u32[]{:S(2)}, u32[]{:S(2)}) collective-permute-start(bf16[1,128,4096]{2,1,0:T(8,128)(2,1)} %param.5), channel_id=1, source_target_pairs={{0,1},{1,0},{8,9},{9,8},{16,17},{17,16},{24,25},{25,24},{2,3},{3,2... | collective-permute-start | bytes 3145736 | tf_op jit(solution)/shard_map/ppermute | solution.py:107
  0.5 0.8 %slice_bitcast_fusion.2 = (bf16[128,128]{1,0:T(8,128)(2,1)S(1)}, bf16[128,128]{1,0:T(8,128)(2,1)S(1)}, bf16[128,128]{1,0:T(8,128)(2,1)S(1)}, bf16[128,128]{1,0:T(8,128)(2,1)S(1)}) fusion(bf16[1,128,256]{2,1,0:T(8,128)(2,1)} %param.7, bf16[1,128,256]{2,1,0:T(8,128)(2,1)} %param.6), kind=kLoop, calls=%fused_computation.5 | loop fusion | bytes 262144 | tf_op jit(solution)/shard_map/squeeze | solution.py:126
  1.3 3.8 %collective-permute-start.5 = (bf16[128,256]{1,0:T(8,128)(2,1)S(1)}, bf16[128,256]{1,0:T(8,128)(2,1)S(1)}, u32[]{:S(2)}, u32[]{:S(2)}) collective-permute-start(bf16[128,256]{1,0:T(8,128)(2,1)S(1)} %get-tuple-element.27), channel_id=1, source_target_pairs={{0,17},{1,16},{8,25},{9,24},{16,1},{17,0},{24,9},{25,8},{2,19},{3,... | collective-permute-start | bytes 196616 | tf_op jit(solution)/shard_map/ppermute | solution.py:107
  5.1 0.0 copy-start
  5.1 0.0 copy-start.1
  5.1 1.2 %collective-permute-start.2 = (bf16[2,128,256]{2,1,0:T(8,128)(2,1)S(1)}, bf16[2,128,256]{2,1,0:T(8,128)(2,1)S(1)}, u32[]{:S(2)}, u32[]{:S(2)}) collective-permute-start(bf16[2,128,256]{2,1,0:T(8,128)(2,1)S(1)} %pad_maximum_fusion), channel_id=1, source_target_pairs={{0,9},{1,8},{8,1},{9,0},{16,25},{17,24},{24,17},{25,16},{2,11},{3,... | collective-permute-start | bytes 393224 | tf_op jit(solution)/shard_map/ppermute | solution.py:107
  6.4 0.0 copy-done
  6.4 0.0 copy-done.1
  6.4 0.7 %bias.1 = f32[128,512]{1,0:T(8,128)S(1)} custom-call(s32[16]{0:T(128)S(1)} %copy-done.1, s32[4,128]{1,0:T(4,128)S(1)} %bitcast.13), custom_call_target="tpu_custom_call" | custom-call | tf_op jit(solution)/shard_map/bias/pallas_call | solution.py:116
  7.0 0.6 %collective-permute-start.1 = (bf16[2,128,256]{2,1,0:T(8,128)(2,1)S(1)}, bf16[2,128,256]{2,1,0:T(8,128)(2,1)S(1)}, u32[]{:S(2)}, u32[]{:S(2)}) collective-permute-start(bf16[2,128,256]{2,1,0:T(8,128)(2,1)S(1)} %pad_maximum_fusion), channel_id=1, source_target_pairs={{0,1},{1,0},{8,9},{9,8},{16,17},{17,16},{24,25},{25,24},{2,3},{3,2... | collective-permute-start | bytes 393224 | tf_op jit(solution)/shard_map/ppermute | solution.py:107
  7.6 0.9 %collective-permute-done.5.refs_2_ = bf16[128,256]{1,0:T(8,128)(2,1)S(1)} collective-permute-done((bf16[128,256]{1,0:T(8,128)(2,1)S(1)}, bf16[128,256]{1,0:T(8,128)(2,1)S(1)}, u32[]{:S(2)}, u32[]{:S(2)}) %collective-permute-start.5) | collective-permute-done | bytes 65568 | tf_op jit(solution)/shard_map/ppermute | solution.py:107
  8.6 1.2 %collective-permute-start.6 = (bf16[128,256]{1,0:T(8,128)(2,1)S(1)}, bf16[128,256]{1,0:T(8,128)(2,1)S(1)}, u32[]{:S(2)}, u32[]{:S(2)}) collective-permute-start(bf16[128,256]{1,0:T(8,128)(2,1)S(1)} %collective-permute-done.5.refs_2_), channel_id=1, source_target_pairs={{0,8},{8,0},{16,24},{24,16},{1,9},{9,1},{17,25},{25,17},{2,10},{10... | collective-permute-start | bytes 196616 | tf_op jit(solution)/shard_map/ppermute | solution.py:110
  9.8 2.7 %collective-permute-start.3 = (bf16[128,256]{1,0:T(8,128)(2,1)S(1)}, bf16[128,256]{1,0:T(8,128)(2,1)S(1)}, u32[]{:S(2)}, u32[]{:S(2)}) collective-permute-start(bf16[128,256]{1,0:T(8,128)(2,1)S(1)} %get-tuple-element.29), channel_id=1, source_target_pairs={{0,17},{1,16},{8,25},{9,24},{16,1},{17,0},{24,9},{25,8},{2,19},{3,... | collective-permute-start | bytes 196616 | tf_op jit(solution)/shard_map/ppermute | solution.py:107
  12.5 0.0 collective-permute-done.2.refs_1_.refs_5_
  12.5 0.3 collective-permute-done.6.refs_3_
  12.8 0.0 collective-permute-done.1.refs_0_.refs_4_
  12.8 0.0 collective-permute-done.q
  12.8 0.7 %attend.4.refs_4_ = bf16[32,2048]{1,0:T(8,128)(2,1)S(1)} custom-call(bf16[1,128,4096]{2,1,0:T(8,128)(2,1)S(1)} %collective-permute-done.q, f32[128,512]{1,0:T(8,128)S(1)} %bias.1, bf16[2,128,256]{2,1,0:T(8,128)(2,1)S(1)} %collective-permute-done.1.refs_0_.refs_4_, bf16[2,128,256]{2,1,0:T(8,128)(2,1)S(1)} %collective-permute-done.2.refs_1_.refs_5_, ...), custom_call_target="tpu_custom_call" | custom-call | flops 134217728 | bytes 262144 | tf_op jit(solution)/shard_map/attend/pallas_call | solution.py:145
  13.5 2.4 %collective-permute-start.7 = (bf16[32,2048]{1,0:T(8,128)(2,1)S(1)}, bf16[32,2048]{1,0:T(8,128)(2,1)S(1)}, u32[]{:S(2)}, u32[]{:S(2)}) collective-permute-start(bf16[32,2048]{1,0:T(8,128)(2,1)S(1)} %attend.4.refs_4_), channel_id=1, source_target_pairs={{0,6},{2,4},{4,2},{6,0},{1,7},{3,5},{5,3},{7,1},{8,14},{10,12},{12... | collective-permute-start | bytes 393224 | tf_op jit(solution)/shard_map/ppermute | solution.py:170
  15.9 0.0 collective-permute-done.3.refs_2_.refs_6_
  15.9 1.3 %collective-permute-start.4 = (bf16[128,256]{1,0:T(8,128)(2,1)S(1)}, bf16[128,256]{1,0:T(8,128)(2,1)S(1)}, u32[]{:S(2)}, u32[]{:S(2)}) collective-permute-start(bf16[128,256]{1,0:T(8,128)(2,1)S(1)} %collective-permute-done.3.refs_2_.refs_6_), channel_id=1, source_target_pairs={{0,8},{8,0},{16,24},{24,16},{1,9},{9,1},{17,25},{25,17},{2,10},{10... | collective-permute-start | bytes 196616 | tf_op jit(solution)/shard_map/ppermute | solution.py:110
  17.3 1.0 %attend.5 = (bf16[32,2048]{1,0:T(8,128)(2,1)S(1)}, bf16[32,2048]{1,0:T(8,128)(2,1)S(1)}) custom-call(bf16[1,128,4096]{2,1,0:T(8,128)(2,1)S(1)} %collective-permute-done.q, f32[128,512]{1,0:T(8,128)S(1)} %bias.1, bf16[2,128,256]{2,1,0:T(8,128)(2,1)S(1)} %collective-permute-done.1.refs_0_.refs_4_, ...), custom_call_target="tpu_custom_call" | custom-call | flops 268435456 | bytes 524288 | tf_op jit(solution)/shard_map/attend/pallas_call | solution.py:145
  18.2 0.7 %collective-permute-start.11 = (bf16[32,2048]{1,0:T(8,128)(2,1)S(1)}, bf16[32,2048]{1,0:T(8,128)(2,1)S(1)}, u32[]{:S(2)}, u32[]{:S(2)}) collective-permute-start(bf16[32,2048]{1,0:T(8,128)(2,1)S(1)} %get-tuple-element.24), channel_id=1, source_target_pairs={{0,2},{2,0},{4,6},{6,4},{1,3},{3,1},{5,7},{7,5},{8,10},{10,8},{12,... | collective-permute-start | bytes 393224 | tf_op jit(solution)/shard_map/ppermute | solution.py:170
  18.9 1.5 %collective-permute-start.12 = (bf16[32,2048]{1,0:T(8,128)(2,1)S(1)}, bf16[32,2048]{1,0:T(8,128)(2,1)S(1)}, u32[]{:S(2)}, u32[]{:S(2)}) collective-permute-start(bf16[32,2048]{1,0:T(8,128)(2,1)S(1)} %get-tuple-element.19.refs_4_), channel_id=1, source_target_pairs={{0,4},{2,6},{4,0},{6,2},{1,5},{3,7},{5,1},{7,3},{8,12},{10,14},{12... | collective-permute-start | bytes 393224 | tf_op jit(solution)/shard_map/ppermute | solution.py:170
  20.4 0.0 collective-permute-done.4.refs_3_.refs_7_
  20.4 1.3 %attend.6 = (bf16[32,2048]{1,0:T(8,128)(2,1)S(1)}, bf16[32,2048]{1,0:T(8,128)(2,1)S(1)}, bf16[32,2048]{1,0:T(8,128)(2,1)S(1)}) custom-call(bf16[1,128,4096]{2,1,0:T(8,128)(2,1)S(1)} %collective-permute-done.q, f32[128,512]{1,0:T(8,128)S(1)} %bias.1, bf16[2,128,256]{2,1,0:T(8,128)(2,1)S(1)} %collective-permute-done.1.refs_0_.refs_4_, ...), custom_call_target="tpu_custom_call" | custom-call | flops 402653184 | bytes 786432 | tf_op jit(solution)/shard_map/attend/pallas_call | solution.py:145
  21.7 1.6 %collective-permute-start.10 = (bf16[32,2048]{1,0:T(8,128)(2,1)S(1)}, bf16[32,2048]{1,0:T(8,128)(2,1)S(1)}, u32[]{:S(2)}, u32[]{:S(2)}) collective-permute-start(bf16[32,2048]{1,0:T(8,128)(2,1)S(1)} %get-tuple-element.23), channel_id=1, source_target_pairs={{0,6},{2,4},{4,2},{6,0},{1,7},{3,5},{5,3},{7,1},{8,14},{10,12},{12... | collective-permute-start | bytes 393224 | tf_op jit(solution)/shard_map/ppermute | solution.py:170
  23.3 0.5 %collective-permute-start.9 = (bf16[32,2048]{1,0:T(8,128)(2,1)S(1)}, bf16[32,2048]{1,0:T(8,128)(2,1)S(1)}, u32[]{:S(2)}, u32[]{:S(2)}) collective-permute-start(bf16[32,2048]{1,0:T(8,128)(2,1)S(1)} %get-tuple-element.22.refs_8_), channel_id=1, source_target_pairs={{0,4},{2,6},{4,0},{6,2},{1,5},{3,7},{5,1},{7,3},{8,12},{10,14},{12... | collective-permute-start | bytes 393224 | tf_op jit(solution)/shard_map/ppermute | solution.py:170
  23.8 0.0 collective-permute-done.7.refs_0_
  23.8 1.5 %collective-permute-start.8 = (bf16[32,2048]{1,0:T(8,128)(2,1)S(1)}, bf16[32,2048]{1,0:T(8,128)(2,1)S(1)}, u32[]{:S(2)}, u32[]{:S(2)}) collective-permute-start(bf16[32,2048]{1,0:T(8,128)(2,1)S(1)} %get-tuple-element.21), channel_id=1, source_target_pairs={{0,2},{2,0},{4,6},{6,4},{1,3},{3,1},{5,7},{7,5},{8,10},{10,8},{12,... | collective-permute-start | bytes 393224 | tf_op jit(solution)/shard_map/ppermute | solution.py:170
  25.3 1.0 %attend.7 = (bf16[32,2048]{1,0:T(8,128)(2,1)S(1)}, bf16[32,2048]{1,0:T(8,128)(2,1)S(1)}) custom-call(bf16[1,128,4096]{2,1,0:T(8,128)(2,1)S(1)} %collective-permute-done.q, f32[128,512]{1,0:T(8,128)S(1)} %bias.1, bf16[2,128,256]{2,1,0:T(8,128)(2,1)S(1)} %collective-permute-done.1.refs_0_.refs_4_, ...), custom_call_target="tpu_custom_call" | custom-call | flops 268435456 | bytes 524288 | tf_op jit(solution)/shard_map/attend/pallas_call | solution.py:145
  26.2 0.0 collective-permute-done.11.refs_1_
  26.2 0.0 collective-permute-done.12.refs_2_
  26.3 0.9 %place.3.refs_1_ = bf16[1,32,16384]{2,1,0:T(8,128)(2,1)} custom-call(bf16[32,2048]{1,0:T(8,128)(2,1)S(1)} %collective-permute-done.7.refs_0_, bf16[32,2048]{1,0:T(8,128)(2,1)S(1)} %collective-permute-done.11.refs_1_, bf16[32,2048]{1,0:T(8,128)(2,1)S(1)} %collective-permute-done.12.refs_2_, bf16[32,2048]{1,0:T(8,128)(2,1)S(1)} %get-tuple-element.25.refs_3_, ...), custom_call_target="tpu_custom_call" | custom-call | tf_op jit(solution)/shard_map/place/pallas_call | solution.py:179
  27.1 1.1 %collective-permute-done.10.refs_0_ = bf16[32,2048]{1,0:T(8,128)(2,1)S(1)} collective-permute-done((bf16[32,2048]{1,0:T(8,128)(2,1)S(1)}, bf16[32,2048]{1,0:T(8,128)(2,1)S(1)}, u32[]{:S(2)}, u32[]{:S(2)}) %collective-permute-start.10) | collective-permute-done | bytes 131104 | tf_op jit(solution)/shard_map/ppermute | solution.py:170
  28.2 0.7 %place.4.refs_2_ = bf16[1,32,16384]{2,1,0:T(8,128)(2,1)} custom-call(bf16[32,2048]{1,0:T(8,128)(2,1)S(1)} %collective-permute-done.10.refs_0_, bf16[1,32,16384]{2,1,0:T(8,128)(2,1)} %place.3.refs_1_), custom_call_target="tpu_custom_call", output_to_operand_aliasing={{}: (1, {})} | custom-call | tf_op jit(solution)/shard_map/place/pallas_call | solution.py:179
  28.9 1.7 %collective-permute-done.9.refs_1_ = bf16[32,2048]{1,0:T(8,128)(2,1)S(1)} collective-permute-done((bf16[32,2048]{1,0:T(8,128)(2,1)S(1)}, bf16[32,2048]{1,0:T(8,128)(2,1)S(1)}, u32[]{:S(2)}, u32[]{:S(2)}) %collective-permute-start.9) | collective-permute-done | bytes 131104 | tf_op jit(solution)/shard_map/ppermute | solution.py:170
  30.6 0.0 collective-permute-done.8.refs_0_
  30.6 0.7 %place.5 = bf16[1,32,16384]{2,1,0:T(8,128)(2,1)} custom-call(bf16[32,2048]{1,0:T(8,128)(2,1)S(1)} %collective-permute-done.8.refs_0_, bf16[32,2048]{1,0:T(8,128)(2,1)S(1)} %collective-permute-done.9.refs_1_, bf16[1,32,16384]{2,1,0:T(8,128)(2,1)} %place.4.refs_2_), custom_call_target="tpu_custom_call", output_to_operand_aliasing={{}: (2, {})} | custom-call | tf_op jit(solution)/shard_map/place/pallas_call | solution.py:179
  (3 shorter events, 0.0 us)
Async XLA Ops:
  0.0 12.8 %collective-permute-start = (bf16[1,128,4096]{2,1,0:T(8,128)(2,1)}, bf16[1,128,4096]{2,1,0:T(8,128)(2,1)S(1)}, u32[]{:S(2)}, u32[]{:S(2)}) collective-permute-start(bf16[1,128,4096]{2,1,0:T(8,128)(2,1)} %param.5), channel_id=1, source_target_pairs={{0,1},{1,0},{8,9},{9,8},{16,17},{17,16},{24,25},{25,24},{2,3},{3,2... | collective-permute-start | bytes 3145736 | tf_op jit(solution)/shard_map/ppermute | solution.py:107
  1.3 7.3 %collective-permute-start.5 = (bf16[128,256]{1,0:T(8,128)(2,1)S(1)}, bf16[128,256]{1,0:T(8,128)(2,1)S(1)}, u32[]{:S(2)}, u32[]{:S(2)}) collective-permute-start(bf16[128,256]{1,0:T(8,128)(2,1)S(1)} %get-tuple-element.27), channel_id=1, source_target_pairs={{0,17},{1,16},{8,25},{9,24},{16,1},{17,0},{24,9},{25,8},{2,19},{3,... | collective-permute-start | bytes 196616 | tf_op jit(solution)/shard_map/ppermute | solution.py:107
  5.1 1.3 %copy-start = (s32[512]{0:T(512)S(1)}, s32[512]{0:T(512)}, u32[]{:S(2)}) copy-start(s32[512]{0:T(512)} %param.8) | copy-start | bytes 6148
  5.1 1.3 %copy-start.1 = (s32[16]{0:T(128)S(1)}, s32[16]{0:T(128)}, u32[]{:S(2)}) copy-start(s32[16]{0:T(128)} %lengths.1) | copy-start | bytes 196
  5.1 7.4 %collective-permute-start.2 = (bf16[2,128,256]{2,1,0:T(8,128)(2,1)S(1)}, bf16[2,128,256]{2,1,0:T(8,128)(2,1)S(1)}, u32[]{:S(2)}, u32[]{:S(2)}) collective-permute-start(bf16[2,128,256]{2,1,0:T(8,128)(2,1)S(1)} %pad_maximum_fusion), channel_id=1, source_target_pairs={{0,9},{1,8},{8,1},{9,0},{16,25},{17,24},{24,17},{25,16},{2,11},{3,... | collective-permute-start | bytes 393224 | tf_op jit(solution)/shard_map/ppermute | solution.py:107
  7.0 5.8 %collective-permute-start.1 = (bf16[2,128,256]{2,1,0:T(8,128)(2,1)S(1)}, bf16[2,128,256]{2,1,0:T(8,128)(2,1)S(1)}, u32[]{:S(2)}, u32[]{:S(2)}) collective-permute-start(bf16[2,128,256]{2,1,0:T(8,128)(2,1)S(1)} %pad_maximum_fusion), channel_id=1, source_target_pairs={{0,1},{1,0},{8,9},{9,8},{16,17},{17,16},{24,25},{25,24},{2,3},{3,2... | collective-permute-start | bytes 393224 | tf_op jit(solution)/shard_map/ppermute | solution.py:107
  8.6 4.3 %collective-permute-start.6 = (bf16[128,256]{1,0:T(8,128)(2,1)S(1)}, bf16[128,256]{1,0:T(8,128)(2,1)S(1)}, u32[]{:S(2)}, u32[]{:S(2)}) collective-permute-start(bf16[128,256]{1,0:T(8,128)(2,1)S(1)} %collective-permute-done.5.refs_2_), channel_id=1, source_target_pairs={{0,8},{8,0},{16,24},{24,16},{1,9},{9,1},{17,25},{25,17},{2,10},{10... | collective-permute-start | bytes 196616 | tf_op jit(solution)/shard_map/ppermute | solution.py:110
  9.8 6.1 %collective-permute-start.3 = (bf16[128,256]{1,0:T(8,128)(2,1)S(1)}, bf16[128,256]{1,0:T(8,128)(2,1)S(1)}, u32[]{:S(2)}, u32[]{:S(2)}) collective-permute-start(bf16[128,256]{1,0:T(8,128)(2,1)S(1)} %get-tuple-element.29), channel_id=1, source_target_pairs={{0,17},{1,16},{8,25},{9,24},{16,1},{17,0},{24,9},{25,8},{2,19},{3,... | collective-permute-start | bytes 196616 | tf_op jit(solution)/shard_map/ppermute | solution.py:107
  13.5 10.3 %collective-permute-start.7 = (bf16[32,2048]{1,0:T(8,128)(2,1)S(1)}, bf16[32,2048]{1,0:T(8,128)(2,1)S(1)}, u32[]{:S(2)}, u32[]{:S(2)}) collective-permute-start(bf16[32,2048]{1,0:T(8,128)(2,1)S(1)} %attend.4.refs_4_), channel_id=1, source_target_pairs={{0,6},{2,4},{4,2},{6,0},{1,7},{3,5},{5,3},{7,1},{8,14},{10,12},{12... | collective-permute-start | bytes 393224 | tf_op jit(solution)/shard_map/ppermute | solution.py:170
  15.9 4.5 %collective-permute-start.4 = (bf16[128,256]{1,0:T(8,128)(2,1)S(1)}, bf16[128,256]{1,0:T(8,128)(2,1)S(1)}, u32[]{:S(2)}, u32[]{:S(2)}) collective-permute-start(bf16[128,256]{1,0:T(8,128)(2,1)S(1)} %collective-permute-done.3.refs_2_.refs_6_), channel_id=1, source_target_pairs={{0,8},{8,0},{16,24},{24,16},{1,9},{9,1},{17,25},{25,17},{2,10},{10... | collective-permute-start | bytes 196616 | tf_op jit(solution)/shard_map/ppermute | solution.py:110
  18.2 8.0 %collective-permute-start.11 = (bf16[32,2048]{1,0:T(8,128)(2,1)S(1)}, bf16[32,2048]{1,0:T(8,128)(2,1)S(1)}, u32[]{:S(2)}, u32[]{:S(2)}) collective-permute-start(bf16[32,2048]{1,0:T(8,128)(2,1)S(1)} %get-tuple-element.24), channel_id=1, source_target_pairs={{0,2},{2,0},{4,6},{6,4},{1,3},{3,1},{5,7},{7,5},{8,10},{10,8},{12,... | collective-permute-start | bytes 393224 | tf_op jit(solution)/shard_map/ppermute | solution.py:170
  18.9 7.3 %collective-permute-start.12 = (bf16[32,2048]{1,0:T(8,128)(2,1)S(1)}, bf16[32,2048]{1,0:T(8,128)(2,1)S(1)}, u32[]{:S(2)}, u32[]{:S(2)}) collective-permute-start(bf16[32,2048]{1,0:T(8,128)(2,1)S(1)} %get-tuple-element.19.refs_4_), channel_id=1, source_target_pairs={{0,4},{2,6},{4,0},{6,2},{1,5},{3,7},{5,1},{7,3},{8,12},{10,14},{12... | collective-permute-start | bytes 393224 | tf_op jit(solution)/shard_map/ppermute | solution.py:170
  21.7 6.5 %collective-permute-start.10 = (bf16[32,2048]{1,0:T(8,128)(2,1)S(1)}, bf16[32,2048]{1,0:T(8,128)(2,1)S(1)}, u32[]{:S(2)}, u32[]{:S(2)}) collective-permute-start(bf16[32,2048]{1,0:T(8,128)(2,1)S(1)} %get-tuple-element.23), channel_id=1, source_target_pairs={{0,6},{2,4},{4,2},{6,0},{1,7},{3,5},{5,3},{7,1},{8,14},{10,12},{12... | collective-permute-start | bytes 393224 | tf_op jit(solution)/shard_map/ppermute | solution.py:170
  23.3 7.3 %collective-permute-start.9 = (bf16[32,2048]{1,0:T(8,128)(2,1)S(1)}, bf16[32,2048]{1,0:T(8,128)(2,1)S(1)}, u32[]{:S(2)}, u32[]{:S(2)}) collective-permute-start(bf16[32,2048]{1,0:T(8,128)(2,1)S(1)} %get-tuple-element.22.refs_8_), channel_id=1, source_target_pairs={{0,4},{2,6},{4,0},{6,2},{1,5},{3,7},{5,1},{7,3},{8,12},{10,14},{12... | collective-permute-start | bytes 393224 | tf_op jit(solution)/shard_map/ppermute | solution.py:170
  23.8 6.8 %collective-permute-start.8 = (bf16[32,2048]{1,0:T(8,128)(2,1)S(1)}, bf16[32,2048]{1,0:T(8,128)(2,1)S(1)}, u32[]{:S(2)}, u32[]{:S(2)}) collective-permute-start(bf16[32,2048]{1,0:T(8,128)(2,1)S(1)} %get-tuple-element.21), channel_id=1, source_target_pairs={{0,2},{2,0},{4,6},{6,4},{1,3},{3,1},{5,7},{7,5},{8,10},{10,8},{12,... | collective-permute-start | bytes 393224 | tf_op jit(solution)/shard_map/ppermute | solution.py:170
